TPU v7x, 32 devices: a whole 2x2x4 slice. The times are simulated.
32 devices in a mesh: row: 8 (over z, y), col: 4 (over x, core).
Axes of the slice: x: 2, y: 2, z: 4, core: 2. Of those that a mesh axis runs over, the one named last changes fastest.
Arguments:
- operator: bfloat16 [32768, 32768], P('row', 'col'), may hold values from -0.0068359375 to 0.0068359375
- rhs: float32 [32, 32768], P(None, 'row'), may hold values from -72 to 72
- bodies: int32 [32768], P('row'), may hold values from 0 to 63, as said below
- weights: float32 [32768], P('row'), may hold values from 0.5 to 1.5
Outputs:
- basis: float32 [128, 32768], P(None, ('row', 'col'))
- hess: float32 [128, 96], replicated
- start_factor: float32 [32, 32], replicated
Inputs may be any that keep to these rules, and one draw needn't show every extreme that they name: Every one of the 64 bodies has at least one node.
All inputs are finite; a program needn't handle non-finite values.
Results may differ from a plain program's by a relative error of at most 0.0025.
Values may be sent and summed in bfloat16 or wider, within the bound.
No kernel may reach another device: no remote copies, remote signals or barrier semaphores. Data moves between devices by JAX's collectives and lax.ppermute only.
A program may use at most 128 MiB of HBM per device.

v0:
```python
import jax
import jax.numpy as jnp
from jax import lax
from jax.sharding import PartitionSpec as P

N = 32768
S = 32
BODIES = 64
STEPS = 3


def product_t(left, right):
    return lax.dot_general(
        left,
        right,
        (((1,), (1,)), ((), ())),
        precision=lax.Precision.HIGHEST,
        preferred_element_type=jnp.float32,
    )


def local(operator, rhs, bodies, weights):
    col_index = lax.axis_index("col")
    col_count = lax.axis_size("col")
    row_width = rhs.shape[1]
    quarter = row_width // col_count
    own_rhs = lax.dynamic_slice_in_dim(rhs, col_index * quarter, quarter, 1)
    node_body = lax.dynamic_slice_in_dim(bodies, col_index * quarter, quarter, 0)
    node_weight = lax.dynamic_slice_in_dim(weights, col_index * quarter, quarter, 0)
    onehot = (node_body[:, None] == jnp.arange(BODIES, dtype=jnp.int32)[None, :]).astype(
        jnp.float32
    )
    onehot_part = jnp.transpose(onehot.T)
    gram_start = lax.psum(product_t(own_rhs, own_rhs), ("row", "col")) / N
    start_low = jnp.linalg.cholesky(gram_start)
    basis_list = [lax.linalg.triangular_solve(start_low, own_rhs, left_side=True, lower=True)]
    col_width = operator.shape[1]
    columns = []
    for step_index in range(STEPS):
        current = basis_list[-1]
        current_low = current.astype(jnp.bfloat16)
        gathered = lax.all_gather(current_low, ("row", "col"), axis=1, tiled=True)
        col_block = lax.dynamic_slice_in_dim(gathered, col_index * col_width, col_width, 1)
        partial_terms = lax.dot_general(
            col_block, operator, (((1,), (1,)), ((), ())), preferred_element_type=jnp.float32
        )
        coupled = lax.psum_scatter(partial_terms, "col", scatter_dimension=1, tiled=True)
        scaled = current_low.astype(jnp.float32) * node_weight[None, :]
        body_partial = jnp.dot(scaled, onehot_part, precision=lax.Precision.HIGHEST)
        body_means = lax.psum(body_partial, ("row", "col")) * (BODIES / N)
        completion = node_weight[None, :] * product_t(body_means, onehot)
        image_block = 0.5 * current + coupled + completion
        stacked = jnp.concatenate(basis_list, axis=0)
        coef_raw, gram_raw = lax.psum(
            (product_t(stacked, image_block), product_t(image_block, image_block)), ("row", "col")
        )
        first_coef = coef_raw / N
        residual_one = image_block - jnp.dot(first_coef.T, stacked, precision=lax.Precision.HIGHEST)
        gram_block = gram_raw / N - jnp.dot(
            first_coef.T, first_coef, precision=lax.Precision.HIGHEST
        )
        factor_low = jnp.linalg.cholesky(gram_block)
        basis_list.append(
            lax.linalg.triangular_solve(factor_low, residual_one, left_side=True, lower=True)
        )
        pieces = [first_coef, factor_low.T]
        below = (STEPS - 1 - step_index) * S
        if below > 0:
            pieces.append(jnp.zeros((below, S), jnp.float32))
        columns.append(jnp.concatenate(pieces, axis=0))
    basis = jnp.concatenate(basis_list, axis=0)
    return (basis, jnp.concatenate(columns, axis=1), start_low)


def solution(mesh):
    in_specs = (P("row", "col"), P(None, "row"), P("row"), P("row"))
    out_specs = (P(None, ("row", "col")), P(), P())
    return jax.shard_map(local, mesh=mesh, in_specs=in_specs, out_specs=out_specs, check_vma=False)
```

profile of v0, /device:TPU:0, one launch (start us, length us, event | category | flops | bytes accessed | tf_op | source)
XLA Modules:
  0.0 590.2 jit_solution(10057424128240899691)
XLA Ops:
  7.2 1.0 copy-done
  8.2 0.2 fusion.28
  8.5 42.1 %psum.70 = f32[32,32]{0,1:T(8,128)S(1)} all-reduce(f32[32,32]{0,1:T(8,128)S(1)} %fusion.28), channel_id=1, replica_groups=mesh['row'=8,'col'=4] {'row','col'}, use_global_device_ids=true, to_apply=%region_0.0 | all-reduce | flops 1024 | bytes 8192 | tf_op jit(solution)/shard_map/psum | solution.py:34
  50.6 0.1 copy.8
  50.7 2.9 cholesky.74
  53.6 0.6 compare_reduce_fusion.3
  54.3 1.3 select_bitcast_fusion.3
  55.5 2.4 custom-call.8
  57.9 1.0 fusion.67
  58.9 0.0 reduce-scatter.4.cloned.1.call-start
  59.0 56.0 %all-gather.4.cloned.1.call-done = bf16[32,32768]{1,0:T(8,128)(2,1)} async-done(((bf16[32,1024]{1,0:T(8,128)(2,1)}), bf16[32,32768]{1,0:T(8,128)(2,1)}) %all-gather.4.cloned.1.call-update) | async-done | bytes 2097168 | tf_op jit(solution)/shard_map/all_gather | solution.py:42
  115.0 27.6 %fusion.10 = f32[32,4096]{1,0:T(8,128)} fusion(bf16[4096,8192]{1,0:T(8,128)(2,1)} %param.7, bf16[32,32768]{1,0:T(8,128)(2,1)} %all-gather.4.cloned.1.call-done, s32[]{:T(128)S(6)} %select_n.14), kind=kOutput, calls=%fused_computation.21 | convolution fusion | flops 2147483648 | bytes 68157440 | tf_op jit(solution)/shard_map/dot_general | solution.py:44
  142.7 0.7 dynamic_slice.20
  143.4 0.7 dynamic_slice.21
  144.1 0.4 fusion.9
  144.5 39.0 %psum.71 = f32[32,64]{1,0:T(8,128)S(1)} all-reduce(f32[32,64]{1,0:T(8,128)S(1)} %fusion.9), channel_id=1, replica_groups=mesh['row'=8,'col'=4] {'row','col'}, use_global_device_ids=true, to_apply=%region_4.7 | all-reduce | flops 2048 | bytes 16384 | tf_op jit(solution)/shard_map/psum | solution.py:50
  183.5 1.4 fusion
  184.9 0.3 fusion.70
  185.1 0.2 fusion.71
  185.4 40.6 %all-reduce.2 = (f32[32,32]{0,1:T(8,128)S(1)}, f32[32,32]{0,1:T(8,128)S(1)}) all-reduce(f32[32,32]{0,1:T(8,128)S(1)} %fusion.71, f32[32,32]{0,1:T(8,128)S(1)} %fusion.70), channel_id=1, replica_groups=mesh['row'=8,'col'=4] {'row','col'}, use_global_device_ids=true, to_apply=%region_6.9 | all-reduce | flops 2048 | bytes 16384 | tf_op jit(solution)/shard_map/psum | solution.py:54
  226.0 0.3 convolution_subtract_fusion.1
  226.3 0.1 convolution_subtract_fusion.5
  226.5 0.1 copy.12
  226.5 2.9 cholesky.85
  229.5 0.6 compare_reduce_fusion.2
  230.1 0.7 fusion.48
  230.8 2.4 custom-call.9
  233.2 1.0 fusion.68
  234.2 0.0 reduce-scatter.6.cloned.1.call-start
  234.3 56.0 %all-gather.6.cloned.1.call-done = bf16[32,32768]{1,0:T(8,128)(2,1)} async-done(((bf16[32,1024]{1,0:T(8,128)(2,1)}), bf16[32,32768]{1,0:T(8,128)(2,1)}) %all-gather.6.cloned.1.call-update) | async-done | bytes 2097168 | tf_op jit(solution)/shard_map/all_gather | solution.py:42
  290.2 27.6 %fusion.5 = f32[32,4096]{1,0:T(8,128)} fusion(bf16[4096,8192]{1,0:T(8,128)(2,1)} %param.7, bf16[32,32768]{1,0:T(8,128)(2,1)} %all-gather.6.cloned.1.call-done, s32[]{:T(128)S(6)} %select_n.14), kind=kOutput, calls=%fused_computation.15 | convolution fusion | flops 2147483648 | bytes 68157440 | tf_op jit(solution)/shard_map/dot_general | solution.py:44
  317.9 0.4 fusion.8
  318.3 39.0 %psum.74 = f32[32,64]{1,0:T(8,128)S(1)} all-reduce(f32[32,64]{1,0:T(8,128)S(1)} %fusion.8), channel_id=1, replica_groups=mesh['row'=8,'col'=4] {'row','col'}, use_global_device_ids=true, to_apply=%region_8.11 | all-reduce | flops 2048 | bytes 16384 | tf_op jit(solution)/shard_map/psum | solution.py:50
  357.3 1.4 fusion.1
  358.7 0.3 fusion.19
  359.1 0.2 fusion.72
  359.3 40.8 %all-reduce.1 = (f32[64,32]{0,1:T(8,128)S(1)}, f32[32,32]{0,1:T(8,128)S(1)}) all-reduce(f32[64,32]{0,1:T(8,128)S(1)} %fusion.19, f32[32,32]{0,1:T(8,128)S(1)} %fusion.72), channel_id=1, replica_groups=mesh['row'=8,'col'=4] {'row','col'}, use_global_device_ids=true, to_apply=%region_10.13 | all-reduce | flops 3072 | bytes 24576 | tf_op jit(solution)/shard_map/psum | solution.py:54
  400.2 0.3 convolution_subtract_fusion.2
  400.4 0.1 convolution_subtract_fusion.4
  400.6 0.1 copy.15
  400.7 2.9 cholesky.96
  403.6 0.6 compare_reduce_fusion.1
  404.3 0.7 fusion.49
  404.9 2.4 custom-call.10
  407.4 1.0 fusion.69
  408.3 0.0 reduce-scatter.8.cloned.1.call-start
  408.4 56.0 %all-gather.8.cloned.1.call-done = bf16[32,32768]{1,0:T(8,128)(2,1)} async-done(((bf16[32,1024]{1,0:T(8,128)(2,1)}), bf16[32,32768]{1,0:T(8,128)(2,1)}) %all-gather.8.cloned.1.call-update) | async-done | bytes 2097168 | tf_op jit(solution)/shard_map/all_gather | solution.py:42
  464.4 27.6 %fusion.3 = f32[32,4096]{1,0:T(8,128)} fusion(bf16[4096,8192]{1,0:T(8,128)(2,1)} %param.7, bf16[32,32768]{1,0:T(8,128)(2,1)} %all-gather.8.cloned.1.call-done, s32[]{:T(128)S(6)} %select_n.14), kind=kOutput, calls=%fused_computation.13 | convolution fusion | flops 2147483648 | bytes 68157440 | tf_op jit(solution)/shard_map/dot_general | solution.py:44
  492.0 0.4 fusion.7
  492.4 39.0 %psum.77 = f32[32,64]{1,0:T(8,128)S(1)} all-reduce(f32[32,64]{1,0:T(8,128)S(1)} %fusion.7), channel_id=1, replica_groups=mesh['row'=8,'col'=4] {'row','col'}, use_global_device_ids=true, to_apply=%region_12.15 | all-reduce | flops 2048 | bytes 16384 | tf_op jit(solution)/shard_map/psum | solution.py:50
  531.4 1.4 fusion.2
  532.8 0.4 fusion.12
  533.3 0.2 fusion.73
  533.5 40.6 %all-reduce = (f32[96,32]{0,1:T(8,128)S(1)}, f32[32,32]{0,1:T(8,128)S(1)}) all-reduce(f32[96,32]{0,1:T(8,128)S(1)} %fusion.12, f32[32,32]{0,1:T(8,128)S(1)} %fusion.73), channel_id=1, replica_groups=mesh['row'=8,'col'=4] {'row','col'}, use_global_device_ids=true, to_apply=%region_14.17 | all-reduce | flops 4096 | bytes 32768 | tf_op jit(solution)/shard_map/psum | solution.py:54
  574.2 0.3 convolution_subtract_fusion
  574.5 0.1 convolution_subtract_fusion.3
  574.7 0.1 copy.18
  574.8 2.9 cholesky.107
  577.7 0.6 compare_reduce_fusion
  578.4 0.7 fusion.50
  579.0 2.4 custom-call.11
  581.5 0.3 fusion.33
  581.8 0.8 pad_maximum_fusion
  582.7 0.7 maximum_maximum_fusion
  (33 shorter events, 0.4 us)
Async XLA Ops:
  7.2 1.0 copy-start
  7.2 107.8 %all-gather.4.cloned.1.call-start = ((), (), s32[]{:S(2)}) async-start(), calls=%async_computation.3 | async-start | bytes 2162688 | tf_op jit(solution)/shard_map/all_gather | solution.py:42
  58.9 85.2 %copy-start.1 = (bf16[32,1024]{1,0:T(8,128)(2,1)S(1)}, bf16[32,1024]{1,0:T(8,128)(2,1)}, u32[]{:S(2)}) copy-start(bf16[32,1024]{1,0:T(8,128)(2,1)} %get-tuple-element.19) | copy-start | bytes 196612
  58.9 124.5 %reduce-scatter.4.cloned.1.call-start = ((), (), s32[]{:S(2)}) async-start(), calls=%async_computation.4 | async-start | bytes 655360 | tf_op jit(solution)/shard_map/reduce_scatter | solution.py:47
  142.6 147.6 %all-gather.6.cloned.1.call-start = ((), (), s32[]{:S(2)}) async-start(), calls=%async_computation.5 | async-start | bytes 2162688 | tf_op jit(solution)/shard_map/all_gather | solution.py:42
  234.2 83.7 %copy-start.3 = (bf16[32,1024]{1,0:T(8,128)(2,1)S(1)}, bf16[32,1024]{1,0:T(8,128)(2,1)}, u32[]{:S(2)}) copy-start(bf16[32,1024]{1,0:T(8,128)(2,1)} %get-tuple-element.21) | copy-start | bytes 196612
  234.2 123.1 %reduce-scatter.6.cloned.1.call-start = ((), (), s32[]{:S(2)}) async-start(), calls=%async_computation.6 | async-start | bytes 655360 | tf_op jit(solution)/shard_map/reduce_scatter | solution.py:47
  317.9 146.5 %all-gather.8.cloned.1.call-start = ((), (), s32[]{:S(2)}) async-start(), calls=%async_computation.7 | async-start | bytes 2162688 | tf_op jit(solution)/shard_map/all_gather | solution.py:42
  408.3 83.7 %copy-start.2 = (bf16[32,1024]{1,0:T(8,128)(2,1)S(1)}, bf16[32,1024]{1,0:T(8,128)(2,1)}, u32[]{:S(2)}) copy-start(bf16[32,1024]{1,0:T(8,128)(2,1)} %get-tuple-element.23) | copy-start | bytes 196612
  408.3 123.1 %reduce-scatter.8.cloned.1.call-start = ((), (), s32[]{:S(2)}) async-start(), calls=%async_computation.8 | async-start | bytes 655360 | tf_op jit(solution)/shard_map/reduce_scatter | solution.py:47
Sparse Core Ops, SparseCore 0:
  59.1 55.9 all-gather.3
  142.8 20.7 reduce-scatter.3
  234.3 55.8 all-gather.5
  318.0 20.6 reduce-scatter.5
  408.5 55.8 all-gather.7
  492.1 20.6 reduce-scatter.7
where the time goes:
time: 592 us; the launch traced here: 590 us
  blocking collectives  281 us (47%)
  waiting for transfers between devices  168 us (28%)
  matrix products  94.7 us (16%)
  other arithmetic  28.9 us (5%)
  between operations  14.4 us (2%)
    all_gather x3, waiting for transfers between devices, local(): gathered = lax.all_gather(current_low, ('row', 'col'), axis=1, tiled=True)  168 us
    psum x3, blocking collectives, local(): lax.psum((product_t(stacked, image_block), product_t(image_block, image_b...  122 us
    psum x3, blocking collectives, local(): body_means = lax.psum(body_partial, ('row', 'col')) * (BODIES / N)  117 us
    dot_general x3, matrix products, local(): lax.dot_general(col_block, operator, (((1,), (1,)), ((), ())), preferred_...  82.8 us
    psum x1, blocking collectives, local(): gram_start = lax.psum(product_t(own_rhs, own_rhs), ('row', 'col')) / N  42.1 us
  transfers between devices with their start and end apart: 6, of which 3 were waited for; matrix products, arithmetic and copies ran while one was open for 0% of the time, Pallas kernels for 0%

commit v1 on v0

v1 whole, which is shorter than its diff:
```python
import functools

import jax
import jax.numpy as jnp
from jax import lax
from jax.experimental import pallas as pl
from jax.experimental.pallas import tpu as pltpu
from jax.sharding import PartitionSpec as P

BODIES = 64
STEPS = 3
AXES = ("row", "col")
LANES = 128
EXTRA = 16
ROWS_A_COPY = 128
VMEM = pltpu.CompilerParams(vmem_limit_bytes=48 * 1024 * 1024)
f32 = jnp.float32
bf16 = jnp.bfloat16


def dot(left, right, left_dim, right_dim):
    return lax.dot_general(
        left, right, (((left_dim,), (right_dim,)), ((), ())), preferred_element_type=f32
    )


def dot_exact(left, right, left_dim, right_dim):
    return lax.dot_general(
        left,
        right,
        (((left_dim,), (right_dim,)), ((), ())),
        precision=lax.Precision.HIGHEST,
        preferred_element_type=f32,
    )


def split(value):
    high = value.astype(bf16)
    return high, (value - high.astype(f32)).astype(bf16)


def product_kernel(slots, group, q, x_ref, k_hbm, o_ref, buf, sem):
    t = buf.shape[0] // slots
    steps = k_hbm.shape[0] // t

    def copy(i, s):
        return pltpu.make_async_copy(
            k_hbm.at[pl.ds(pl.multiple_of(i * t, t), t)],
            buf.at[pl.ds(pl.multiple_of(s * t, t), t)],
            sem.at[s],
        )

    for i in range(min(slots, steps)):
        copy(i, i).start()
    x = x_ref[: o_ref.shape[1], : k_hbm.shape[1]]
    wide = t * group

    def step(i, carry):
        first = lax.rem(i * group, slots)
        for p in range(group):
            copy(i * group + p, first + p).wait()
        block = buf[pl.ds(pl.multiple_of(first * t, t), wide)]
        value = dot(block, x, 1, 1).T
        at = i * wide
        quarter = at // q
        place = (quarter // 2) * q + lax.rem(at, q)
        o_ref[lax.rem(quarter, 2), :, pl.ds(pl.multiple_of(place, LANES), wide)] = value

        @pl.when(i * group + slots < steps)
        def _():
            for p in range(group):
                copy(i * group + slots + p, first + p).start()

        return carry

    lax.fori_loop(0, steps // group, step, 0)


def product(x, s, operator, q):
    rows, width = operator.shape
    t = min(ROWS_A_COPY, q)
    group = max(1, min(4, q // t))
    slots = group * max(1, min(4, rows // (t * group)))
    return pl.pallas_call(
        functools.partial(product_kernel, slots, group, q),
        in_specs=[
            pl.BlockSpec(memory_space=pltpu.VMEM),
            pl.BlockSpec(memory_space=pl.ANY),
        ],
        out_specs=pl.BlockSpec(memory_space=pltpu.VMEM),
        out_shape=jax.ShapeDtypeStruct((2, s, rows // 2), f32),
        scratch_shapes=[
            pltpu.VMEM((slots * t, width), bf16),
            pltpu.SemaphoreType.DMA((slots,)),
        ],
        compiler_params=VMEM,
        cost_estimate=pl.CostEstimate(
            flops=2 * s * rows * width, bytes_accessed=2 * rows * width, transcendentals=0
        ),
        name="product",
    )(x, operator)


def gram_kernel(count, q, first, n_basis, *refs):
    refs = list(refs)
    off_ref = refs.pop(0)
    piece_refs = [refs.pop(0) for _ in range(count)]
    own_ref, weight_ref, body_ref = refs.pop(0), refs.pop(0), refs.pop(0)
    mean_ref = None if first else refs.pop(0)
    basis_refs = [refs.pop(0) for _ in range(n_basis)]
    w_ref, gram_ref = refs.pop(0), refs.pop(0)
    if first:
        weight_out, body_out = refs.pop(0), refs.pop(0)
    s = own_ref.shape[0]
    end = w_ref.shape[1] - q
    if not first:
        m_high, m_rest = split(mean_ref[...])
        m_rest32 = mean_ref[...] - m_high.astype(f32)
        m_low = (m_rest32 - m_rest.astype(f32)).astype(bf16)
        means = jnp.concatenate([m_high, m_rest, m_low], axis=0)
        body_row = lax.broadcasted_iota(jnp.int32, (BODIES, q), 0)

    def place(value, weight, body, at):
        if not first:
            onehot = (body_row == body).astype(f32).astype(bf16)
            picked = dot(means, onehot, 1, 0)
            value = value + weight * (picked[:s] + picked[s : 2 * s] + picked[2 * s :])
        high, low = split(value)
        w_ref[:s, pl.ds(at, q)] = high
        w_ref[s:, pl.ds(at, q)] = low

    k = 0
    for ref in piece_refs:
        for d in range(ref.shape[0]):
            at = pl.multiple_of(off_ref[k], LANES)
            k += 1
            codes = ref[d].astype(jnp.int32).astype(f32)
            scale = jnp.exp2(codes[:s, q : q + 1] * 0.125)
            value = codes[:s, :q] * scale
            if first:
                weight = (codes[s : s + 1, :q] + codes[s + 1 : s + 2, :q] * 2.0**-15) * 2.0**-14
                body = codes[s + 2 : s + 3, :q].astype(jnp.int32)
                weight_out[:, pl.ds(at, q)] = weight
                body_out[:, pl.ds(at, q)] = body
            else:
                weight = weight_ref[:, pl.ds(at, q)]
                body = body_ref[:, pl.ds(at, q)]
            place(value, weight, body, at)
    if first:
        weight_out[:, end:] = weight_ref[...]
        body_out[:, end:] = body_ref[...]
        place(own_ref[...], None, None, end)
    else:
        place(own_ref[...], weight_ref[:, end:], body_ref[:, end:], end)
    span = slice(0, end) if count else slice(0, q)
    new = w_ref[:, span]
    blocks = [ref[:, span] for ref in basis_refs] + [new]
    raw = dot(jnp.concatenate(blocks, axis=0), new, 1, 1)
    for b in range(n_basis + 1):
        part = raw[2 * s * b : 2 * s * b + s] + raw[2 * s * b + s : 2 * s * (b + 1)]
        gram_ref[s * b : s * (b + 1), :] = part[:, :s] + part[:, s:]


def gram_call(offsets, pieces, own, weight, body, means, basis, first):
    s, q = own.shape
    n_basis = len(basis)
    wide = q
    for p in pieces:
        wide += p.shape[0] * q
    outs = [
        jax.ShapeDtypeStruct((2 * s, wide), bf16),
        jax.ShapeDtypeStruct((s * (n_basis + 1), s), f32),
    ]
    if first:
        outs += [
            jax.ShapeDtypeStruct((1, wide), f32),
            jax.ShapeDtypeStruct((1, wide), jnp.int32),
        ]
    args = [offsets, *pieces, own, weight, body]
    if not first:
        args.append(means)
    args += basis
    specs = [pl.BlockSpec(memory_space=pltpu.SMEM)]
    specs += [pl.BlockSpec(memory_space=pltpu.VMEM)] * (len(args) - 1)
    return pl.pallas_call(
        functools.partial(gram_kernel, len(pieces), q, first, n_basis),
        in_specs=specs,
        out_specs=[pl.BlockSpec(memory_space=pltpu.VMEM)] * len(outs),
        out_shape=outs,
        compiler_params=VMEM,
        name="gram",
    )(*args)


def factor(gram):
    n = gram.shape[0]
    row = lax.broadcasted_iota(jnp.int32, (n, n), 0)
    lane = lax.broadcasted_iota(jnp.int32, (n, n), 1)
    left, right = gram, (row == lane).astype(f32)
    for k in range(n):
        pivot = left[k : k + 1, k : k + 1]
        root = lax.rsqrt(pivot)
        root = root * (1.5 - 0.5 * pivot * root * root)
        left_row = left[k : k + 1, :] * root
        right_row = right[k : k + 1, :] * root
        column = jnp.where(row > k, left[:, k : k + 1] * root, 0.0)
        left = jnp.where(row == k, left_row, left - column * left_row)
        right = jnp.where(row == k, right_row, right - column * right_row)
    return jnp.where(lane >= row, left, 0.0), jnp.where(lane <= row, right, 0.0)


def next_kernel(n, q, n_basis, last, *refs):
    refs = list(refs)
    gram_ref, w_ref = refs.pop(0), refs.pop(0)
    basis_refs = [refs.pop(0) for _ in range(n_basis)]
    if not last:
        weight_ref, body_ref = refs.pop(0), refs.pop(0)
    own_ref, upper_ref = refs.pop(0), refs.pop(0)
    if n_basis:
        coef_ref = refs.pop(0)
    if not last:
        v_ref, mean_ref = refs.pop(0), refs.pop(0)
    s = own_ref.shape[0]
    gram = gram_ref[n_basis * s :, :] / n
    if n_basis:
        coef = gram_ref[: n_basis * s, :] / n
        gram = gram - dot_exact(coef, coef, 0, 0)
        row = lax.broadcasted_iota(jnp.int32, (n_basis * s, s), 0)
        lane = lax.broadcasted_iota(jnp.int32, (n_basis * s, s), 1)
        coef_ref[...] = coef + jnp.where(row == lane + (n_basis - 1) * s, 0.5, 0.0)
    upper, inverse = factor(gram)
    upper_ref[...] = upper
    high, low = split(inverse)
    mix = [jnp.concatenate([high, low], axis=0)] * 2
    for b in range(n_basis):
        high, low = split(-dot_exact(inverse, coef[b * s : (b + 1) * s], 1, 1))
        mix += [jnp.concatenate([high, low], axis=0)] * 2
    mix = jnp.concatenate(mix, axis=1)
    wide = w_ref.shape[1]
    if not last:
        body_row = lax.broadcasted_iota(jnp.int32, (BODIES, q), 0)
        means = jnp.zeros((2 * s, BODIES), f32)
    for at in range(0, wide, q):
        span = slice(at, at + q)
        stack = jnp.concatenate([w_ref[:, span]] + [r[:, span] for r in basis_refs], axis=0)
        both = dot(mix, stack, 1, 0)
        value = both[:s] + both[s:]
        if at == wide - q:
            own_ref[...] = value
        if not last:
            high, low = split(value)
            v_ref[:s, span] = high
            v_ref[s:, span] = low
            if at < wide - q:
                onehot = (body_row == body_ref[:, span]).astype(f32).astype(bf16)
                u_high, u_low = split(high.astype(f32) * weight_ref[:, span])
                means = means + dot(jnp.concatenate([u_high, u_low], axis=0), onehot, 1, 1)
    if not last:
        mean_ref[...] = (means[:s] + means[s:]) * (BODIES / n)


def next_call(n, q, gram, w, basis, weight, body, last):
    s = gram.shape[1]
    n_basis = len(basis)
    outs = [jax.ShapeDtypeStruct((s, q), f32), jax.ShapeDtypeStruct((s, s), f32)]
    if n_basis:
        outs.append(jax.ShapeDtypeStruct((n_basis * s, s), f32))
    args = [gram, w, *basis]
    if not last:
        outs += [
            jax.ShapeDtypeStruct(w.shape, bf16),
            jax.ShapeDtypeStruct((s, BODIES), f32),
        ]
        args += [weight, body]
    return pl.pallas_call(
        functools.partial(next_kernel, n, q, n_basis, last),
        in_specs=[pl.BlockSpec(memory_space=pltpu.VMEM)] * len(args),
        out_specs=[pl.BlockSpec(memory_space=pltpu.VMEM)] * len(outs),
        out_shape=outs,
        compiler_params=VMEM,
        name="next_block",
    )(*args)


def encode(value):
    largest = jnp.maximum(jnp.max(jnp.abs(value), axis=1, keepdims=True), 1e-30)
    level = jnp.ceil(8.0 * jnp.log2(largest / 32000.0))
    codes = jnp.round(value / jnp.exp2(level * 0.125))
    levels = jnp.broadcast_to(level, (value.shape[0], LANES))
    return jnp.concatenate([codes, levels], axis=1).astype(jnp.int16)


def local(rows, cols, operator, rhs, bodies, weights):
    row_index, col_index = lax.axis_index("row"), lax.axis_index("col")
    s, block = rhs.shape
    n = block * rows
    q = block // cols
    span = rows // cols
    plane, inner = row_index // span, lax.rem(row_index, span)
    width = operator.shape[1]

    def index(a, g, c):
        return (a * span + g) * cols + c

    places = [(a, g, c) for a in range(cols) for g in range(span) for c in range(cols)]

    def permute(value, to):
        return lax.ppermute(value, AXES, [(index(*p), index(*to(*p))) for p in places])

    def gather(payload):
        rounds = [
            permute(payload, lambda a, g, c, d=d: ((c + d) % cols, g, a)) for d in range(cols)
        ]
        mine = jnp.stack(rounds)
        return [mine] + [
            permute(mine, lambda a, g, c, d=d: (a, (g + d) % span, c)) for d in range(1, span)
        ]

    offsets = jnp.stack(
        [
            lax.rem(inner - d + span, span) * block + lax.rem(plane - e + cols, cols) * q
            for d in range(span)
            for e in range(cols)
        ]
    ).astype(jnp.int32)

    def sum_cols(value):
        bit = 1
        while bit < cols:
            value = value + permute(value, lambda a, g, c, bit=bit: (a, g, c ^ bit))
            bit *= 2
        return value

    def sum_all(value):
        value = sum_cols(value)
        bit = 1
        while bit < span:
            value = value + permute(value, lambda a, g, c, bit=bit: (a, g ^ bit, c))
            bit *= 2
        bit = 1
        while bit < cols:
            value = value + permute(value, lambda a, g, c, bit=bit: (a ^ bit, g, c))
            bit *= 2
        return value

    def scatter_cols(partial):
        core = lax.rem(col_index, 2)
        keep = lax.dynamic_index_in_dim(partial, core, 0, False)
        send = lax.dynamic_index_in_dim(partial, 1 - core, 0, False)
        value = keep + permute(send, lambda a, g, c: (a, g, c ^ 1))
        bit = cols // 2
        while bit > 1:
            half = value.shape[1] // 2
            side = lax.rem(col_index // bit, 2)
            keep = lax.dynamic_slice_in_dim(value, side * half, half, 1)
            send = lax.dynamic_slice_in_dim(value, (1 - side) * half, half, 1)
            value = keep + permute(send, lambda a, g, c, bit=bit: (a, g, c ^ bit))
            bit //= 2
        return value

    own_rhs = lax.dynamic_slice_in_dim(rhs, col_index * q, q, 1)
    own_weight = lax.dynamic_slice_in_dim(weights, col_index * q, q, 0)[None, :]
    own_body = lax.dynamic_slice_in_dim(bodies, col_index * q, q, 0)[None, :]
    weight_scaled = own_weight * 2.0**14
    weight_high = jnp.round(weight_scaled)
    weight_low = jnp.round((weight_scaled - weight_high) * 2.0**15)
    extra = jnp.concatenate(
        [
            weight_high,
            weight_low,
            own_body.astype(f32),
            jnp.zeros((EXTRA - 3, q), f32),
        ],
        axis=0,
    ).astype(jnp.int16)
    extra = jnp.pad(extra, ((0, 0), (0, LANES)))
    payload = jnp.concatenate([encode(own_rhs), extra], axis=0)
    w, gram, weight, body = gram_call(
        offsets, gather(payload), own_rhs, own_weight, own_body, None, [], True
    )
    own, start_upper, v, means = next_call(n, q, sum_cols(gram), w, [], weight, body, False)
    basis, owns, columns = [v], [own], []
    for step in range(STEPS):
        last = step == STEPS - 1
        means = sum_cols(means)
        partial = product(basis[-1], s, operator, q)
        coupled = scatter_cols(partial)
        if last:
            own_basis = [b[:, width:] for b in basis]
            w, gram = gram_call(
                offsets, [], coupled, own_weight, own_body, means, own_basis, False
            )
            own, upper, coef = next_call(
                n, q, sum_all(gram), w, own_basis, None, None, True
            )
        else:
            w, gram = gram_call(
                offsets, gather(encode(coupled)), coupled, weight, body, means, basis, False
            )
            own, upper, coef, v, means = next_call(
                n, q, sum_cols(gram), w, basis, weight, body, False
            )
            basis.append(v)
        owns.append(own)
        pieces = [coef, upper]
        below = (STEPS - 1 - step) * s
        if below > 0:
            pieces.append(jnp.zeros((below, s), f32))
        columns.append(jnp.concatenate(pieces, axis=0))
    return (jnp.concatenate(owns, axis=0), jnp.concatenate(columns, axis=1), start_upper.T)


def solution(mesh):
    rows, cols = mesh.shape["row"], mesh.shape["col"]
    in_specs = (P("row", "col"), P(None, "row"), P("row"), P("row"))
    out_specs = (P(None, ("row", "col")), P(), P())
    return jax.shard_map(
        functools.partial(local, rows, cols),
        mesh=mesh,
        in_specs=in_specs,
        out_specs=out_specs,
        check_vma=False,
    )
```

time: 592 us -> 227 us (0.38)
  blocking collectives: 281 us -> 0 us
  waiting for transfers between devices: 168 us -> 62.3 us
  matrix products: 94.7 us -> 0 us
  Pallas kernels: 0 us -> 91.4 us
  starting transfers between devices: 0.25 us -> 65.2 us
  other arithmetic: 28.9 us -> 5.02 us
  between operations: 14.4 us -> 0.98 us
    psum x7 -> x0, blocking collectives: 281 us -> none  [the longest x3 122 us: local(): lax.psum((product_t(stacked, image_block), product_t(image_block, image_b...]
    all_gather x3 -> x0, waiting for transfers between devices: 168 us -> none  [local(): gathered = lax.all_gather(current_low, ('row', 'col'), axis=1, tiled=True)]
    dot_general x22 -> x0, matrix products: 91.5 us -> none  [the longest x3 82.8 us: local(): lax.dot_general(col_block, operator, (((1,), (1,)), ((), ())), preferred_...]
    pallas_call x0 -> x11, Pallas kernels: none -> 91.4 us  [the longest x3 68.7 us: product(): pl.pallas_call(functools.partial(product_kernel, slots, group, q), in_spe...]
    ppermute x0 -> x38, starting transfers between devices: none -> 65.2 us  [permute(): lax.ppermute(value, AXES, [(index(*p), index(*to(*p))) for p in places])]
    ppermute x0 -> x38, waiting for transfers between devices: none -> 62.3 us  [permute(): lax.ppermute(value, AXES, [(index(*p), index(*to(*p))) for p in places])]
    another operation x17 -> x9, other arithmetic: 25.4 us -> 1.82 us  [the longest x9 10.8 us: local(): factor_low = jnp.linalg.cholesky(gram_block)]
  transfers between devices with their start and end apart: 6 -> 38, of which waited for: 3 -> 29; matrix products, arithmetic and copies ran while one was open for 0% -> 0% of each run, Pallas kernels for 0% -> 0%
where the time goes in v1:
time: 227 us
  Pallas kernels  91.4 us (40%)
  starting transfers between devices  65.2 us (29%)
  waiting for transfers between devices  62.3 us (27%)
  other arithmetic  5.02 us (2%)
    pallas_call x3, Pallas kernels, product(): pl.pallas_call(functools.partial(product_kernel, slots, group, q), in_spe...  68.7 us
    ppermute x38, starting transfers between devices, permute(): lax.ppermute(value, AXES, [(index(*p), index(*to(*p))) for p in places])  65.2 us
    ppermute x38, waiting for transfers between devices, permute(): lax.ppermute(value, AXES, [(index(*p), index(*to(*p))) for p in places])  62.3 us
    pallas_call x4, Pallas kernels, next_call(): pl.pallas_call(functools.partial(next_kernel, n, q, n_basis, last), in_sp...  15.9 us
    pallas_call x4, Pallas kernels, gram_call(): pl.pallas_call(functools.partial(gram_kernel, len(pieces), q, first, n_ba...  6.77 us
  transfers between devices with their start and end apart: 38, of which 29 were waited for; matrix products, arithmetic and copies ran while one was open for 0% of the time, Pallas kernels for 0%

profile of v1, /device:TPU:0, one launch (start us, length us, event | category | flops | bytes accessed | tf_op | source)
XLA Modules:
  0.0 226.6 jit_solution(3783550698664522333)
XLA Ops:
  2.2 1.0 abs_reduce_fusion.2
  3.5 4.1 %collective-permute-start.2 = (s16[48,1152]{1,0:T(8,128)(2,1)S(1)}, s16[48,1152]{1,0:T(8,128)(2,1)S(1)}, u32[]{:S(2)}, u32[]{:S(2)}) collective-permute-start(s16[48,1152]{1,0:T(8,128)(2,1)S(1)} %pad_add_fusion.3), channel_id=1, source_target_pairs={{0,16},{1,24},{2,0},{3,8},{4,20},{5,28},{6,4},{7,12},{8,17},{9,25}... | collective-permute-start | bytes 331784 | tf_op jit(solution)/shard_map/ppermute | solution.py:308
  7.6 1.8 collective-permute-start.3
  10.1 2.2 collective-permute-start.1
  12.3 3.1 %collective-permute-done.1 = s16[48,1152]{1,0:T(8,128)(2,1)S(1)} collective-permute-done((s16[48,1152]{1,0:T(8,128)(2,1)S(1)}, s16[48,1152]{1,0:T(8,128)(2,1)S(1)}, u32[]{:S(2)}, u32[]{:S(2)}) %collective-permute-start.1) | collective-permute-done | bytes 110624 | tf_op jit(solution)/shard_map/ppermute | solution.py:308
  15.5 1.6 collective-permute-start.4
  17.2 11.2 %collective-permute-done.4.refs_2_ = s16[4,48,1152]{2,1,0:T(8,128)(2,1)S(1)} collective-permute-done((s16[4,48,1152]{2,1,0:T(8,128)(2,1)S(1)}, s16[4,48,1152]{2,1,0:T(8,128)(2,1)S(1)}, u32[]{:S(2)}, u32[]{:S(2)}) %collective-permute-start.4) | collective-permute-done | bytes 442400 | tf_op jit(solution)/shard_map/ppermute | solution.py:308
  28.3 1.4 gram.4
  29.9 1.1 collective-permute-done.5
  31.0 4.5 %collective-permute-start.6 = (f32[32,32]{1,0:T(8,128)S(1)}, f32[32,32]{1,0:T(8,128)S(1)}, u32[]{:S(2)}, u32[]{:S(2)}) collective-permute-start(f32[32,32]{1,0:T(8,128)S(1)} %add.179), channel_id=1, source_target_pairs={{0,2},{1,3},{2,0},{3,1},{4,6},{5,7},{6,4},{7,5},{8,10},{9,11},{10,... | collective-permute-start | bytes 12296 | tf_op jit(solution)/shard_map/ppermute | solution.py:308
  35.4 1.7 collective-permute-done.6
  37.1 3.7 %next_block.4 = (f32[32,1024]{1,0:T(8,128)S(1)}, f32[32,32]{1,0:T(8,128)S(1)}, bf16[64,9216]{1,0:T(8,128)(2,1)S(1)}, f32[32,64]{1,0:T(8,128)S(1)}) custom-call(f32[32,32]{1,0:T(8,128)S(1)} %add.180.refs_0_, bf16[64,9216]{1,0:T(8,128)(2,1)S(1)} %get-tuple-element.31.refs_1_, f32[1,9216]{1,0:T(1,128)S(1)} %get-tuple-element.32.refs_2_.refs_4_.refs_3_, ...), custom_call_target="tpu_custom_call" | custom-call | tf_op jit(solution)/shard_map/next_block/pallas_call | solution.py:275
  40.9 22.9 %product.3 = f32[2,32,2048]{2,1,0:T(8,128)S(1)} custom-call(bf16[64,9216]{1,0:T(8,128)(2,1)S(1)} %get-tuple-element.35.x_ref.refs_7_.refs_2_, bf16[4096,8192]{1,0:T(8,128)(2,1)} %k_hbm.5), custom_call_target="tpu_custom_call" | custom-call | flops 2147483648 | bytes 67108864 | tf_op jit(solution)/shard_map/product/pallas_call | solution.py:84
  63.9 1.5 collective-permute-done.7
  65.5 2.1 collective-permute-start.8
  67.6 3.8 %collective-permute-done.8 = f32[32,1024]{1,0:T(8,128)S(1)} collective-permute-done((f32[32,1024]{1,0:T(8,128)S(1)}, f32[32,1024]{1,0:T(8,128)S(1)}, u32[]{:S(2)}, u32[]{:S(2)}) %collective-permute-start.8) | collective-permute-done | bytes 131104 | tf_op jit(solution)/shard_map/ppermute | solution.py:308
  72.4 3.5 %collective-permute-start.10 = (s16[32,1152]{1,0:T(8,128)(2,1)S(1)}, s16[32,1152]{1,0:T(8,128)(2,1)S(1)}, u32[]{:S(2)}, u32[]{:S(2)}) collective-permute-start(s16[32,1152]{1,0:T(8,128)(2,1)S(1)} %pad_add_fusion.4), channel_id=1, source_target_pairs={{0,8},{1,16},{2,24},{3,0},{4,12},{5,20},{6,28},{7,4},{8,9},{9,17},... | collective-permute-start | bytes 221192 | tf_op jit(solution)/shard_map/ppermute | solution.py:308
  75.9 2.6 %collective-permute-start.11 = (s16[32,1152]{1,0:T(8,128)(2,1)S(1)}, s16[32,1152]{1,0:T(8,128)(2,1)S(1)}, u32[]{:S(2)}, u32[]{:S(2)}) collective-permute-start(s16[32,1152]{1,0:T(8,128)(2,1)S(1)} %pad_add_fusion.4), channel_id=1, source_target_pairs={{0,16},{1,24},{2,0},{3,8},{4,20},{5,28},{6,4},{7,12},{8,17},{9,25}... | collective-permute-start | bytes 221192 | tf_op jit(solution)/shard_map/ppermute | solution.py:308
  78.6 2.7 %collective-permute-start.12 = (s16[32,1152]{1,0:T(8,128)(2,1)S(1)}, s16[32,1152]{1,0:T(8,128)(2,1)S(1)}, u32[]{:S(2)}, u32[]{:S(2)}) collective-permute-start(s16[32,1152]{1,0:T(8,128)(2,1)S(1)} %pad_add_fusion.4), channel_id=1, source_target_pairs={{0,24},{1,0},{2,8},{3,16},{4,28},{5,4},{6,12},{7,20},{8,25},{9,1},... | collective-permute-start | bytes 221192 | tf_op jit(solution)/shard_map/ppermute | solution.py:308
  81.3 2.6 %collective-permute-done.10 = s16[32,1152]{1,0:T(8,128)(2,1)S(1)} collective-permute-done((s16[32,1152]{1,0:T(8,128)(2,1)S(1)}, s16[32,1152]{1,0:T(8,128)(2,1)S(1)}, u32[]{:S(2)}, u32[]{:S(2)}) %collective-permute-start.10) | collective-permute-done | bytes 73760 | tf_op jit(solution)/shard_map/ppermute | solution.py:308
  84.1 1.6 collective-permute-start.13
  85.7 1.7 collective-permute-start.14
  88.2 3.3 %collective-permute-start.15 = (f32[32,64]{1,0:T(8,128)S(1)}, f32[32,64]{1,0:T(8,128)S(1)}, u32[]{:S(2)}, u32[]{:S(2)}) collective-permute-start(f32[32,64]{1,0:T(8,128)S(1)} %add.187), channel_id=1, source_target_pairs={{0,2},{1,3},{2,0},{3,1},{4,6},{5,7},{6,4},{7,5},{8,10},{9,11},{10,... | collective-permute-start | bytes 24584 | tf_op jit(solution)/shard_map/ppermute | solution.py:308
  91.5 1.7 collective-permute-done.15
  93.2 2.0 gram.5
  95.9 0.9 collective-permute-done.16
  96.8 2.6 %collective-permute-start.17 = (f32[64,32]{1,0:T(8,128)S(1)}, f32[64,32]{1,0:T(8,128)S(1)}, u32[]{:S(2)}, u32[]{:S(2)}) collective-permute-start(f32[64,32]{1,0:T(8,128)S(1)} %add.189), channel_id=1, source_target_pairs={{0,2},{1,3},{2,0},{3,1},{4,6},{5,7},{6,4},{7,5},{8,10},{9,11},{10,... | collective-permute-start | bytes 24584 | tf_op jit(solution)/shard_map/ppermute | solution.py:308
  99.4 1.9 collective-permute-done.17
  101.3 4.1 %next_block.5 = (f32[32,1024]{1,0:T(8,128)S(1)}, f32[32,32]{1,0:T(8,128)S(1)}, f32[32,32]{1,0:T(8,128)S(1)}, bf16[64,9216]{1,0:T(8,128)(2,1)S(1)}, f32[32,64]{1,0:T(8,128)S(1)}) custom-call(f32[64,32]{1,0:T(8,128)S(1)} %add.190.refs_0_, bf16[64,9216]{1,0:T(8,128)(2,1)S(1)} %get-tuple-element.38.refs_1_, ...), custom_call_target="tpu_custom_call" | custom-call | tf_op jit(solution)/shard_map/next_block/pallas_call | solution.py:275
  105.4 22.9 %product.4 = f32[2,32,2048]{2,1,0:T(8,128)S(1)} custom-call(bf16[64,9216]{1,0:T(8,128)(2,1)S(1)} %get-tuple-element.40.x_ref.refs_8_.refs_3_, bf16[4096,8192]{1,0:T(8,128)(2,1)} %k_hbm.5), custom_call_target="tpu_custom_call" | custom-call | flops 2147483648 | bytes 67108864 | tf_op jit(solution)/shard_map/product/pallas_call | solution.py:84
  128.5 1.5 collective-permute-done.18
  130.1 2.1 collective-permute-start.19
  132.2 3.8 %collective-permute-done.19 = f32[32,1024]{1,0:T(8,128)S(1)} collective-permute-done((f32[32,1024]{1,0:T(8,128)S(1)}, f32[32,1024]{1,0:T(8,128)S(1)}, u32[]{:S(2)}, u32[]{:S(2)}) %collective-permute-start.19) | collective-permute-done | bytes 131104 | tf_op jit(solution)/shard_map/ppermute | solution.py:308
  137.0 3.2 %collective-permute-start.21 = (s16[32,1152]{1,0:T(8,128)(2,1)S(1)}, s16[32,1152]{1,0:T(8,128)(2,1)S(1)}, u32[]{:S(2)}, u32[]{:S(2)}) collective-permute-start(s16[32,1152]{1,0:T(8,128)(2,1)S(1)} %pad_add_fusion.5), channel_id=1, source_target_pairs={{0,8},{1,16},{2,24},{3,0},{4,12},{5,20},{6,28},{7,4},{8,9},{9,17},... | collective-permute-start | bytes 221192 | tf_op jit(solution)/shard_map/ppermute | solution.py:308
  140.1 2.6 %collective-permute-start.22 = (s16[32,1152]{1,0:T(8,128)(2,1)S(1)}, s16[32,1152]{1,0:T(8,128)(2,1)S(1)}, u32[]{:S(2)}, u32[]{:S(2)}) collective-permute-start(s16[32,1152]{1,0:T(8,128)(2,1)S(1)} %pad_add_fusion.5), channel_id=1, source_target_pairs={{0,16},{1,24},{2,0},{3,8},{4,20},{5,28},{6,4},{7,12},{8,17},{9,25}... | collective-permute-start | bytes 221192 | tf_op jit(solution)/shard_map/ppermute | solution.py:308
  142.8 2.6 %collective-permute-start.23 = (s16[32,1152]{1,0:T(8,128)(2,1)S(1)}, s16[32,1152]{1,0:T(8,128)(2,1)S(1)}, u32[]{:S(2)}, u32[]{:S(2)}) collective-permute-start(s16[32,1152]{1,0:T(8,128)(2,1)S(1)} %pad_add_fusion.5), channel_id=1, source_target_pairs={{0,24},{1,0},{2,8},{3,16},{4,28},{5,4},{6,12},{7,20},{8,25},{9,1},... | collective-permute-start | bytes 221192 | tf_op jit(solution)/shard_map/ppermute | solution.py:308
  146.1 1.2 collective-permute-done.23
  147.3 1.6 collective-permute-start.24
  148.9 1.1 collective-permute-start.25
  150.9 3.4 %collective-permute-start.26 = (f32[32,64]{1,0:T(8,128)S(1)}, f32[32,64]{1,0:T(8,128)S(1)}, u32[]{:S(2)}, u32[]{:S(2)}) collective-permute-start(f32[32,64]{1,0:T(8,128)S(1)} %add.193), channel_id=1, source_target_pairs={{0,2},{1,3},{2,0},{3,1},{4,6},{5,7},{6,4},{7,5},{8,10},{9,11},{10,... | collective-permute-start | bytes 24584 | tf_op jit(solution)/shard_map/ppermute | solution.py:308
  154.3 1.7 collective-permute-done.26
  156.0 0.9 collective-permute-done.24.refs_2_
  157.0 2.3 %gram.6 = (bf16[64,9216]{1,0:T(8,128)(2,1)S(1)}, f32[96,32]{1,0:T(8,128)S(1)}) custom-call(s32[8]{0:T(128)S(1)} %stack.80.refs_0_, s16[4,32,1152]{2,1,0:T(8,128)(2,1)S(1)} %pad_add_fusion.2.refs_1_, s16[4,32,1152]{2,1,0:T(8,128)(2,1)S(1)} %collective-permute-done.24.refs_2_, f32[32,1024]{1,0:T(8,128)S(1)} %get-tuple-element.64.refs_3_, ...), custom_call_target="tpu_custom_call" | custom-call | tf_op jit(solution)/shard_map/gram/pallas_call | solution.py:185
  159.5 1.1 collective-permute-done.27
  160.5 1.9 collective-permute-start.28
  162.4 2.3 %collective-permute-done.28 = f32[96,32]{1,0:T(8,128)S(1)} collective-permute-done((f32[96,32]{1,0:T(8,128)S(1)}, f32[96,32]{1,0:T(8,128)S(1)}, u32[]{:S(2)}, u32[]{:S(2)}) %collective-permute-start.28) | collective-permute-done | bytes 12320 | tf_op jit(solution)/shard_map/ppermute | solution.py:308
  164.7 4.5 %next_block.6 = (f32[32,1024]{1,0:T(8,128)S(1)}, f32[32,32]{1,0:T(8,128)S(1)}, f32[64,32]{1,0:T(8,128)S(1)}, bf16[64,9216]{1,0:T(8,128)(2,1)S(1)}, f32[32,64]{1,0:T(8,128)S(1)}) custom-call(f32[96,32]{1,0:T(8,128)S(1)} %add.196.refs_0_, bf16[64,9216]{1,0:T(8,128)(2,1)S(1)} %get-tuple-element.43.refs_1_, ...), custom_call_target="tpu_custom_call" | custom-call | tf_op jit(solution)/shard_map/next_block/pallas_call | solution.py:275
  169.2 22.9 %product.5 = f32[2,32,2048]{2,1,0:T(8,128)S(1)} custom-call(bf16[64,9216]{1,0:T(8,128)(2,1)S(1)} %get-tuple-element.45.x_ref, bf16[4096,8192]{1,0:T(8,128)(2,1)} %k_hbm.5), custom_call_target="tpu_custom_call" | custom-call | flops 2147483648 | bytes 67108864 | tf_op jit(solution)/shard_map/product/pallas_call | solution.py:84
  192.3 1.5 collective-permute-done.29
  193.8 1.9 collective-permute-start.30
  195.7 1.2 collective-permute-done.31
  197.2 3.5 %collective-permute-done.32 = f32[32,64]{1,0:T(8,128)S(1)} collective-permute-done((f32[32,64]{1,0:T(8,128)S(1)}, f32[32,64]{1,0:T(8,128)S(1)}, u32[]{:S(2)}, u32[]{:S(2)}) %collective-permute-start.32) | collective-permute-done | bytes 8224 | tf_op jit(solution)/shard_map/ppermute | solution.py:308
  200.7 1.1 gram.7
  201.8 1.2 collective-permute-done.33
  203.1 1.0 collective-permute-start.34
  204.1 3.3 %collective-permute-done.34 = f32[128,32]{1,0:T(8,128)S(1)} collective-permute-done((f32[128,32]{1,0:T(8,128)S(1)}, f32[128,32]{1,0:T(8,128)S(1)}, u32[]{:S(2)}, u32[]{:S(2)}) %collective-permute-start.34) | collective-permute-done | bytes 16416 | tf_op jit(solution)/shard_map/ppermute | solution.py:308
  207.4 1.6 collective-permute-start.35
  209.0 2.7 %collective-permute-done.35 = f32[128,32]{1,0:T(8,128)S(1)} collective-permute-done((f32[128,32]{1,0:T(8,128)S(1)}, f32[128,32]{1,0:T(8,128)S(1)}, u32[]{:S(2)}, u32[]{:S(2)}) %collective-permute-start.35) | collective-permute-done | bytes 16416 | tf_op jit(solution)/shard_map/ppermute | solution.py:308
  211.8 2.1 collective-permute-start.36
  213.8 2.3 %collective-permute-done.36 = f32[128,32]{1,0:T(8,128)S(1)} collective-permute-done((f32[128,32]{1,0:T(8,128)S(1)}, f32[128,32]{1,0:T(8,128)S(1)}, u32[]{:S(2)}, u32[]{:S(2)}) %collective-permute-start.36) | collective-permute-done | bytes 16416 | tf_op jit(solution)/shard_map/ppermute | solution.py:308
  216.1 2.3 %collective-permute-start.37 = (f32[128,32]{1,0:T(8,128)S(1)}, f32[128,32]{1,0:T(8,128)S(1)}, u32[]{:S(2)}, u32[]{:S(2)}) collective-permute-start(f32[128,32]{1,0:T(8,128)S(1)} %add.204), channel_id=1, source_target_pairs={{0,16},{1,17},{2,18},{3,19},{4,20},{5,21},{6,22},{7,23},{8,24},{9,... | collective-permute-start | bytes 49160 | tf_op jit(solution)/shard_map/ppermute | solution.py:308
  219.4 1.9 collective-permute-done.37
  221.4 3.5 %next_block.7 = (f32[32,1024]{1,0:T(8,128)S(1)}, f32[32,32]{1,0:T(8,128)S(1)}, f32[96,32]{1,0:T(8,128)S(1)}) custom-call(f32[128,32]{1,0:T(8,128)S(1)} %add.205.refs_0_, bf16[64,1024]{1,0:T(8,128)(2,1)S(1)} %get-tuple-element.48.refs_1_, bf16[64,1024]{1,0:T(8,128)(2,1)S(1)} %slice.9.refs_5_.refs_2_, bf16[64,1024]{1,0:T(8,128)(2,1)S(1)} %slice.10.refs_6_.refs_3_, ...), custom_call_target="tpu_custom_call" | custom-call | tf_op jit(solution)/shard_map/next_block/pallas_call | solution.py:275
  225.0 0.9 pad_maximum_fusion
  (92 shorter events, 11.0 us)
Async XLA Ops:
  3.5 8.8 %collective-permute-start.2 = (s16[48,1152]{1,0:T(8,128)(2,1)S(1)}, s16[48,1152]{1,0:T(8,128)(2,1)S(1)}, u32[]{:S(2)}, u32[]{:S(2)}) collective-permute-start(s16[48,1152]{1,0:T(8,128)(2,1)S(1)} %pad_add_fusion.3), channel_id=1, source_target_pairs={{0,16},{1,24},{2,0},{3,8},{4,20},{5,28},{6,4},{7,12},{8,17},{9,25}... | collective-permute-start | bytes 331784 | tf_op jit(solution)/shard_map/ppermute | solution.py:308
  7.6 4.7 %collective-permute-start.3 = (s16[48,1152]{1,0:T(8,128)(2,1)S(1)}, s16[48,1152]{1,0:T(8,128)(2,1)S(1)}, u32[]{:S(2)}, u32[]{:S(2)}) collective-permute-start(s16[48,1152]{1,0:T(8,128)(2,1)S(1)} %pad_add_fusion.3), channel_id=1, source_target_pairs={{0,24},{1,0},{2,8},{3,16},{4,28},{5,4},{6,12},{7,20},{8,25},{9,1},... | collective-permute-start | bytes 331784 | tf_op jit(solution)/shard_map/ppermute | solution.py:308
  9.4 2.9 %collective-permute-start = (s16[48,1152]{1,0:T(8,128)(2,1)S(1)}, s16[48,1152]{1,0:T(8,128)(2,1)S(1)}, u32[]{:S(2)}, u32[]{:S(2)}) collective-permute-start(s16[48,1152]{1,0:T(8,128)(2,1)S(1)} %pad_add_fusion.3), channel_id=1, source_target_pairs={{0,0},{1,8},{2,16},{3,24},{4,4},{5,12},{6,20},{7,28},{8,1},{9,9},{... | collective-permute-start | bytes 331784 | tf_op jit(solution)/shard_map/ppermute | solution.py:308
  10.1 5.4 %collective-permute-start.1 = (s16[48,1152]{1,0:T(8,128)(2,1)S(1)}, s16[48,1152]{1,0:T(8,128)(2,1)S(1)}, u32[]{:S(2)}, u32[]{:S(2)}) collective-permute-start(s16[48,1152]{1,0:T(8,128)(2,1)S(1)} %pad_add_fusion.3), channel_id=1, source_target_pairs={{0,8},{1,16},{2,24},{3,0},{4,12},{5,20},{6,28},{7,4},{8,9},{9,17},... | collective-permute-start | bytes 331784 | tf_op jit(solution)/shard_map/ppermute | solution.py:308
  15.5 12.8 %collective-permute-start.4 = (s16[4,48,1152]{2,1,0:T(8,128)(2,1)S(1)}, s16[4,48,1152]{2,1,0:T(8,128)(2,1)S(1)}, u32[]{:S(2)}, u32[]{:S(2)}) collective-permute-start(s16[4,48,1152]{2,1,0:T(8,128)(2,1)S(1)} %pad_add_fusion.refs_1_), channel_id=1, source_target_pairs={{0,4},{1,5},{2,6},{3,7},{4,0},{5,1},{6,2},{7,3},{8,12},{9,13},{10,... | collective-permute-start | bytes 1327112 | tf_op jit(solution)/shard_map/ppermute | solution.py:308
  29.7 1.2 collective-permute-start.5
  31.0 6.2 %collective-permute-start.6 = (f32[32,32]{1,0:T(8,128)S(1)}, f32[32,32]{1,0:T(8,128)S(1)}, u32[]{:S(2)}, u32[]{:S(2)}) collective-permute-start(f32[32,32]{1,0:T(8,128)S(1)} %add.179), channel_id=1, source_target_pairs={{0,2},{1,3},{2,0},{3,1},{4,6},{5,7},{6,4},{7,5},{8,10},{9,11},{10,... | collective-permute-start | bytes 12296 | tf_op jit(solution)/shard_map/ppermute | solution.py:308
  63.8 1.6 collective-permute-start.7
  65.5 5.9 %collective-permute-start.8 = (f32[32,1024]{1,0:T(8,128)S(1)}, f32[32,1024]{1,0:T(8,128)S(1)}, u32[]{:S(2)}, u32[]{:S(2)}) collective-permute-start(f32[32,1024]{1,0:T(8,128)S(1)} %constant_dynamic-slice_fusion.2), channel_id=1, source_target_pairs={{0,2},{1,3},{2,0},{3,1},{4,6},{5,7},{6,4},{7,5},{8,10},{9,11},{10,... | collective-permute-start | bytes 393224 | tf_op jit(solution)/shard_map/ppermute | solution.py:308
  71.7 9.6 %collective-permute-start.9 = (s16[32,1152]{1,0:T(8,128)(2,1)S(1)}, s16[32,1152]{1,0:T(8,128)(2,1)S(1)}, u32[]{:S(2)}, u32[]{:S(2)}) collective-permute-start(s16[32,1152]{1,0:T(8,128)(2,1)S(1)} %pad_add_fusion.4), channel_id=1, source_target_pairs={{0,0},{1,8},{2,16},{3,24},{4,4},{5,12},{6,20},{7,28},{8,1},{9,9},{... | collective-permute-start | bytes 221192 | tf_op jit(solution)/shard_map/ppermute | solution.py:308
  72.4 11.5 %collective-permute-start.10 = (s16[32,1152]{1,0:T(8,128)(2,1)S(1)}, s16[32,1152]{1,0:T(8,128)(2,1)S(1)}, u32[]{:S(2)}, u32[]{:S(2)}) collective-permute-start(s16[32,1152]{1,0:T(8,128)(2,1)S(1)} %pad_add_fusion.4), channel_id=1, source_target_pairs={{0,8},{1,16},{2,24},{3,0},{4,12},{5,20},{6,28},{7,4},{8,9},{9,17},... | collective-permute-start | bytes 221192 | tf_op jit(solution)/shard_map/ppermute | solution.py:308
  75.9 8.1 %collective-permute-start.11 = (s16[32,1152]{1,0:T(8,128)(2,1)S(1)}, s16[32,1152]{1,0:T(8,128)(2,1)S(1)}, u32[]{:S(2)}, u32[]{:S(2)}) collective-permute-start(s16[32,1152]{1,0:T(8,128)(2,1)S(1)} %pad_add_fusion.4), channel_id=1, source_target_pairs={{0,16},{1,24},{2,0},{3,8},{4,20},{5,28},{6,4},{7,12},{8,17},{9,25}... | collective-permute-start | bytes 221192 | tf_op jit(solution)/shard_map/ppermute | solution.py:308
  78.6 5.5 %collective-permute-start.12 = (s16[32,1152]{1,0:T(8,128)(2,1)S(1)}, s16[32,1152]{1,0:T(8,128)(2,1)S(1)}, u32[]{:S(2)}, u32[]{:S(2)}) collective-permute-start(s16[32,1152]{1,0:T(8,128)(2,1)S(1)} %pad_add_fusion.4), channel_id=1, source_target_pairs={{0,24},{1,0},{2,8},{3,16},{4,28},{5,4},{6,12},{7,20},{8,25},{9,1},... | collective-permute-start | bytes 221192 | tf_op jit(solution)/shard_map/ppermute | solution.py:308
  84.1 9.1 %collective-permute-start.13 = (s16[4,32,1152]{2,1,0:T(8,128)(2,1)S(1)}, s16[4,32,1152]{2,1,0:T(8,128)(2,1)S(1)}, u32[]{:S(2)}, u32[]{:S(2)}) collective-permute-start(s16[4,32,1152]{2,1,0:T(8,128)(2,1)S(1)} %pad_add_fusion.1.refs_1_), channel_id=1, source_target_pairs={{0,4},{1,5},{2,6},{3,7},{4,0},{5,1},{6,2},{7,3},{8,12},{9,13},{10,... | collective-permute-start | bytes 884744 | tf_op jit(solution)/shard_map/ppermute | solution.py:308
  85.7 2.6 %collective-permute-start.14 = (f32[32,64]{1,0:T(8,128)S(1)}, f32[32,64]{1,0:T(8,128)S(1)}, u32[]{:S(2)}, u32[]{:S(2)}) collective-permute-start(f32[32,64]{1,0:T(8,128)S(1)} %get-tuple-element.36), channel_id=1, source_target_pairs={{0,1},{1,0},{2,3},{3,2},{4,5},{5,4},{6,7},{7,6},{8,9},{9,8},{10,11... | collective-permute-start | bytes 24584 | tf_op jit(solution)/shard_map/ppermute | solution.py:308
  88.2 5.0 %collective-permute-start.15 = (f32[32,64]{1,0:T(8,128)S(1)}, f32[32,64]{1,0:T(8,128)S(1)}, u32[]{:S(2)}, u32[]{:S(2)}) collective-permute-start(f32[32,64]{1,0:T(8,128)S(1)} %add.187), channel_id=1, source_target_pairs={{0,2},{1,3},{2,0},{3,1},{4,6},{5,7},{6,4},{7,5},{8,10},{9,11},{10,... | collective-permute-start | bytes 24584 | tf_op jit(solution)/shard_map/ppermute | solution.py:308
  95.2 1.6 collective-permute-start.16
  96.8 4.5 %collective-permute-start.17 = (f32[64,32]{1,0:T(8,128)S(1)}, f32[64,32]{1,0:T(8,128)S(1)}, u32[]{:S(2)}, u32[]{:S(2)}) collective-permute-start(f32[64,32]{1,0:T(8,128)S(1)} %add.189), channel_id=1, source_target_pairs={{0,2},{1,3},{2,0},{3,1},{4,6},{5,7},{6,4},{7,5},{8,10},{9,11},{10,... | collective-permute-start | bytes 24584 | tf_op jit(solution)/shard_map/ppermute | solution.py:308
  128.4 1.6 collective-permute-start.18
  130.1 5.9 %collective-permute-start.19 = (f32[32,1024]{1,0:T(8,128)S(1)}, f32[32,1024]{1,0:T(8,128)S(1)}, u32[]{:S(2)}, u32[]{:S(2)}) collective-permute-start(f32[32,1024]{1,0:T(8,128)S(1)} %constant_dynamic-slice_fusion.1), channel_id=1, source_target_pairs={{0,2},{1,3},{2,0},{3,1},{4,6},{5,7},{6,4},{7,5},{8,10},{9,11},{10,... | collective-permute-start | bytes 393224 | tf_op jit(solution)/shard_map/ppermute | solution.py:308
  136.3 9.0 %collective-permute-start.20 = (s16[32,1152]{1,0:T(8,128)(2,1)S(1)}, s16[32,1152]{1,0:T(8,128)(2,1)S(1)}, u32[]{:S(2)}, u32[]{:S(2)}) collective-permute-start(s16[32,1152]{1,0:T(8,128)(2,1)S(1)} %pad_add_fusion.5), channel_id=1, source_target_pairs={{0,0},{1,8},{2,16},{3,24},{4,4},{5,12},{6,20},{7,28},{8,1},{9,9},{... | collective-permute-start | bytes 221192 | tf_op jit(solution)/shard_map/ppermute | solution.py:308
  137.0 8.4 %collective-permute-start.21 = (s16[32,1152]{1,0:T(8,128)(2,1)S(1)}, s16[32,1152]{1,0:T(8,128)(2,1)S(1)}, u32[]{:S(2)}, u32[]{:S(2)}) collective-permute-start(s16[32,1152]{1,0:T(8,128)(2,1)S(1)} %pad_add_fusion.5), channel_id=1, source_target_pairs={{0,8},{1,16},{2,24},{3,0},{4,12},{5,20},{6,28},{7,4},{8,9},{9,17},... | collective-permute-start | bytes 221192 | tf_op jit(solution)/shard_map/ppermute | solution.py:308
  140.1 6.0 %collective-permute-start.22 = (s16[32,1152]{1,0:T(8,128)(2,1)S(1)}, s16[32,1152]{1,0:T(8,128)(2,1)S(1)}, u32[]{:S(2)}, u32[]{:S(2)}) collective-permute-start(s16[32,1152]{1,0:T(8,128)(2,1)S(1)} %pad_add_fusion.5), channel_id=1, source_target_pairs={{0,16},{1,24},{2,0},{3,8},{4,20},{5,28},{6,4},{7,12},{8,17},{9,25}... | collective-permute-start | bytes 221192 | tf_op jit(solution)/shard_map/ppermute | solution.py:308
  142.8 4.5 %collective-permute-start.23 = (s16[32,1152]{1,0:T(8,128)(2,1)S(1)}, s16[32,1152]{1,0:T(8,128)(2,1)S(1)}, u32[]{:S(2)}, u32[]{:S(2)}) collective-permute-start(s16[32,1152]{1,0:T(8,128)(2,1)S(1)} %pad_add_fusion.5), channel_id=1, source_target_pairs={{0,24},{1,0},{2,8},{3,16},{4,28},{5,4},{6,12},{7,20},{8,25},{9,1},... | collective-permute-start | bytes 221192 | tf_op jit(solution)/shard_map/ppermute | solution.py:308
  147.3 9.6 %collective-permute-start.24 = (s16[4,32,1152]{2,1,0:T(8,128)(2,1)S(1)}, s16[4,32,1152]{2,1,0:T(8,128)(2,1)S(1)}, u32[]{:S(2)}, u32[]{:S(2)}) collective-permute-start(s16[4,32,1152]{2,1,0:T(8,128)(2,1)S(1)} %pad_add_fusion.2.refs_1_), channel_id=1, source_target_pairs={{0,4},{1,5},{2,6},{3,7},{4,0},{5,1},{6,2},{7,3},{8,12},{9,13},{10,... | collective-permute-start | bytes 884744 | tf_op jit(solution)/shard_map/ppermute | solution.py:308
  148.9 1.9 collective-permute-start.25
  150.9 5.1 %collective-permute-start.26 = (f32[32,64]{1,0:T(8,128)S(1)}, f32[32,64]{1,0:T(8,128)S(1)}, u32[]{:S(2)}, u32[]{:S(2)}) collective-permute-start(f32[32,64]{1,0:T(8,128)S(1)} %add.193), channel_id=1, source_target_pairs={{0,2},{1,3},{2,0},{3,1},{4,6},{5,7},{6,4},{7,5},{8,10},{9,11},{10,... | collective-permute-start | bytes 24584 | tf_op jit(solution)/shard_map/ppermute | solution.py:308
  159.2 1.3 collective-permute-start.27
  160.5 4.2 %collective-permute-start.28 = (f32[96,32]{1,0:T(8,128)S(1)}, f32[96,32]{1,0:T(8,128)S(1)}, u32[]{:S(2)}, u32[]{:S(2)}) collective-permute-start(f32[96,32]{1,0:T(8,128)S(1)} %add.195), channel_id=1, source_target_pairs={{0,2},{1,3},{2,0},{3,1},{4,6},{5,7},{6,4},{7,5},{8,10},{9,11},{10,... | collective-permute-start | bytes 36872 | tf_op jit(solution)/shard_map/ppermute | solution.py:308
  192.2 1.6 collective-permute-start.29
  193.8 6.8 %collective-permute-start.30 = (f32[32,1024]{1,0:T(8,128)S(1)}, f32[32,1024]{1,0:T(8,128)S(1)}, u32[]{:S(2)}, u32[]{:S(2)}) collective-permute-start(f32[32,1024]{1,0:T(8,128)S(1)} %constant_dynamic-slice_fusion), channel_id=1, source_target_pairs={{0,2},{1,3},{2,0},{3,1},{4,6},{5,7},{6,4},{7,5},{8,10},{9,11},{10,... | collective-permute-start | bytes 393224 | tf_op jit(solution)/shard_map/ppermute | solution.py:308
  195.7 1.2 collective-permute-start.31
  196.9 3.7 %collective-permute-start.32 = (f32[32,64]{1,0:T(8,128)S(1)}, f32[32,64]{1,0:T(8,128)S(1)}, u32[]{:S(2)}, u32[]{:S(2)}) collective-permute-start(f32[32,64]{1,0:T(8,128)S(1)} %add.199), channel_id=1, source_target_pairs={{0,2},{1,3},{2,0},{3,1},{4,6},{5,7},{6,4},{7,5},{8,10},{9,11},{10,... | collective-permute-start | bytes 24584 | tf_op jit(solution)/shard_map/ppermute | solution.py:308
  201.8 1.3 collective-permute-start.33
  203.1 4.3 %collective-permute-start.34 = (f32[128,32]{1,0:T(8,128)S(1)}, f32[128,32]{1,0:T(8,128)S(1)}, u32[]{:S(2)}, u32[]{:S(2)}) collective-permute-start(f32[128,32]{1,0:T(8,128)S(1)} %add.201), channel_id=1, source_target_pairs={{0,2},{1,3},{2,0},{3,1},{4,6},{5,7},{6,4},{7,5},{8,10},{9,11},{10,... | collective-permute-start | bytes 49160 | tf_op jit(solution)/shard_map/ppermute | solution.py:308
  207.4 4.3 %collective-permute-start.35 = (f32[128,32]{1,0:T(8,128)S(1)}, f32[128,32]{1,0:T(8,128)S(1)}, u32[]{:S(2)}, u32[]{:S(2)}) collective-permute-start(f32[128,32]{1,0:T(8,128)S(1)} %add.202), channel_id=1, source_target_pairs={{0,4},{1,5},{2,6},{3,7},{4,0},{5,1},{6,2},{7,3},{8,12},{9,13},{10,... | collective-permute-start | bytes 49160 | tf_op jit(solution)/shard_map/ppermute | solution.py:308
  211.8 4.3 %collective-permute-start.36 = (f32[128,32]{1,0:T(8,128)S(1)}, f32[128,32]{1,0:T(8,128)S(1)}, u32[]{:S(2)}, u32[]{:S(2)}) collective-permute-start(f32[128,32]{1,0:T(8,128)S(1)} %add.203), channel_id=1, source_target_pairs={{0,8},{1,9},{2,10},{3,11},{4,12},{5,13},{6,14},{7,15},{8,0},{9,1},... | collective-permute-start | bytes 49160 | tf_op jit(solution)/shard_map/ppermute | solution.py:308
  216.1 5.2 %collective-permute-start.37 = (f32[128,32]{1,0:T(8,128)S(1)}, f32[128,32]{1,0:T(8,128)S(1)}, u32[]{:S(2)}, u32[]{:S(2)}) collective-permute-start(f32[128,32]{1,0:T(8,128)S(1)} %add.204), channel_id=1, source_target_pairs={{0,16},{1,17},{2,18},{3,19},{4,20},{5,21},{6,22},{7,23},{8,24},{9,... | collective-permute-start | bytes 49160 | tf_op jit(solution)/shard_map/ppermute | solution.py:308

commit v2 on v0

v2 whole, which is shorter than its diff:
```python
import functools

import jax
import jax.numpy as jnp
from jax import lax
from jax.experimental import pallas as pl
from jax.experimental.pallas import tpu as pltpu
from jax.sharding import PartitionSpec as P

BODIES = 64
STEPS = 3
AXES = ("row", "col")
LANES = 128
EXTRA = 16
PARAMS = pltpu.CompilerParams(vmem_limit_bytes=48 * 1024 * 1024)
f32 = jnp.float32
bf16 = jnp.bfloat16
i16 = jnp.int16
i32 = jnp.int32


def dot(left, right, left_dim, right_dim):
    return lax.dot_general(
        left, right, (((left_dim,), (right_dim,)), ((), ())), preferred_element_type=f32
    )


def dot_exact(left, right, left_dim, right_dim):
    return lax.dot_general(
        left,
        right,
        (((left_dim,), (right_dim,)), ((), ())),
        precision=lax.Precision.HIGHEST,
        preferred_element_type=f32,
    )


def split(value):
    high = value.astype(bf16)
    return high, (value - high.astype(f32)).astype(bf16)


def onehot_of(body):
    row = lax.broadcasted_iota(i32, (BODIES, body.shape[1]), 0)
    return (row == body).astype(f32)


def padded(width):
    return -(-width // LANES) * LANES


def level_of(value):
    largest = jnp.maximum(jnp.max(jnp.abs(value), axis=1, keepdims=True), 1e-30)
    return jnp.ceil(8.0 * jnp.log2(largest * (1.0 / 32000.0)))


def write_payload(ref, value, sums):
    s, q = value.shape
    level = level_of(value)
    ref[:s, :q] = jnp.round(value / jnp.exp2(level * 0.125)).astype(i32).astype(i16)
    sum_level = level_of(sums)
    scaled = sums / jnp.exp2(sum_level * 0.125)
    high = jnp.round(scaled)
    low = jnp.round((scaled - high) * 2.0**15)
    k = sums.shape[1]
    rest = ref.shape[1] - q - 2 * k
    lane = lax.broadcasted_iota(i32, (s, rest), 1)
    levels = jnp.where(lane == 0, level, jnp.where(lane == 1, sum_level, 0.0))
    ref[:s, q:] = jnp.concatenate([high, low, levels], axis=1).astype(i32).astype(i16)


def read_sums(tail, k):
    scale = jnp.exp2(tail[:, 2 * k + 1 : 2 * k + 2] * 0.125)
    return (tail[:, :k] + tail[:, k : 2 * k] * 2.0**-15) * scale


def payload_width(q, k):
    return q + padded(2 * k + 2)


def start_kernel(at_ref, rhs_ref, weight_ref, body_ref, own_ref, w_ref, b_ref, payload_ref):
    s, q = own_ref.shape
    at = pl.multiple_of(at_ref[0], LANES)
    own = rhs_ref[:, pl.ds(at, q)]
    weight = weight_ref[:, pl.ds(at, q)]
    body = body_ref[:, pl.ds(at, q)]
    own_ref[...] = own
    w_ref[...] = weight
    b_ref[...] = body
    bodies = onehot_of(body) * weight
    sums = dot_exact(own, jnp.concatenate([own, bodies], axis=0), 1, 1)
    write_payload(payload_ref, own, sums)
    scaled = weight * 2.0**14
    high = jnp.round(scaled)
    low = jnp.round((scaled - high) * 2.0**15)
    row = lax.broadcasted_iota(i32, (EXTRA, q), 0)
    extra = jnp.where(row == 0, high, jnp.where(row == 1, low, 0.0))
    extra = jnp.where(row == 2, body.astype(f32), extra)
    payload_ref[s:, :q] = extra.astype(i32).astype(i16)
    payload_ref[s:, q:] = jnp.zeros((EXTRA, payload_ref.shape[1] - q), i16)


def start_call(at, rhs, weights, bodies, q):
    s = rhs.shape[0]
    k = s + BODIES
    vmem = pl.BlockSpec(memory_space=pltpu.VMEM)
    return pl.pallas_call(
        start_kernel,
        in_specs=[pl.BlockSpec(memory_space=pltpu.SMEM), vmem, vmem, vmem],
        out_specs=[vmem] * 4,
        out_shape=[
            jax.ShapeDtypeStruct((s, q), f32),
            jax.ShapeDtypeStruct((1, q), f32),
            jax.ShapeDtypeStruct((1, q), i32),
            jax.ShapeDtypeStruct((s + EXTRA, payload_width(q, k)), i16),
        ],
        compiler_params=PARAMS,
        name="start",
    )(at, rhs, weights, bodies)


def product_kernel(blocks, cols, slots, t, group, s, k, q, first, carry, *refs):
    refs = list(refs)
    place_ref = refs.pop(0)
    piece_refs = [refs.pop(0) for _ in blocks]
    if not first:
        weight_ref, body_ref, mean_ref = refs.pop(0), refs.pop(0), refs.pop(0)
    if carry:
        before_ref, sums_before_ref = refs.pop(0), refs.pop(0)
    k_hbm, o_ref, sums_ref = refs.pop(0), refs.pop(0), refs.pop(0)
    if first:
        weight_out, body_out = refs.pop(0), refs.pop(0)
    x_ref, buf, sem = refs
    block = cols * q
    wide = t * group
    steps = k_hbm.shape[0] // t

    def copies(i, slot):
        for b, d in enumerate(blocks):
            at = pl.multiple_of(place_ref[cols + d], LANES)
            yield pltpu.make_async_copy(
                k_hbm.at[pl.ds(pl.multiple_of(i * t, t), t), pl.ds(at, block)],
                buf.at[pl.ds(pl.multiple_of(slot * t, t), t), pl.ds(b * block, block)],
                sem.at[slot, b],
            )

    for i in range(min(slots, steps)):
        for copy in copies(i, i):
            copy.start()

    if not first:
        means = mean_ref[...]
        m_high, m_mid = split(means)
        m_low = (means - m_high.astype(f32) - m_mid.astype(f32)).astype(bf16)
        means = jnp.concatenate([m_high, m_mid, m_low], axis=0)
    total = jnp.zeros((s, k), f32)
    for b in range(len(blocks)):
        for e in range(cols):
            at = b * block + pl.multiple_of(place_ref[e], LANES)
            codes = piece_refs[b][e].astype(i32).astype(f32)
            tail = codes[:s, q:]
            total = total + read_sums(tail, k)
            value = codes[:s, :q] * jnp.exp2(tail[:, 2 * k : 2 * k + 1] * 0.125)
            if first:
                weight = codes[s : s + 1, :q] + codes[s + 1 : s + 2, :q] * 2.0**-15
                weight_out[:, pl.ds(at, q)] = weight * 2.0**-14
                body_out[:, pl.ds(at, q)] = codes[s + 2 : s + 3, :q].astype(i32)
            else:
                onehot = onehot_of(body_ref[:, pl.ds(at, q)]).astype(bf16)
                picked = dot(means, onehot, 1, 0)
                picked = picked[:s] + picked[s : 2 * s] + picked[2 * s :]
                value = value + weight_ref[:, pl.ds(at, q)] * picked
            high, low = split(value)
            x_ref[:s, pl.ds(at, q)] = high
            x_ref[s:, pl.ds(at, q)] = low
    if carry:
        total = total + sums_before_ref[...][:, :k]
    rest = sums_ref.shape[1] - k
    if rest:
        total = jnp.concatenate([total, jnp.zeros((s, rest), f32)], axis=1)
    sums_ref[...] = total

    def step(i, state):
        slot = lax.rem(i * group, slots)
        for p in range(group):
            for copy in copies(i * group + p, slot + p):
                copy.wait()
        rows = buf[pl.ds(pl.multiple_of(slot * t, t), wide)]
        both = dot(rows, x_ref[...], 1, 1).T
        value = both[:s] + both[s:]
        at = i * wide
        quarter = at // q
        place = pl.multiple_of((quarter // 2) * q + lax.rem(at, q), LANES)
        half = lax.rem(quarter, 2)
        if carry:
            value = value + before_ref[half, :, pl.ds(place, wide)]
        o_ref[half, :, pl.ds(place, wide)] = value

        @pl.when(i * group + slots < steps)
        def _():
            for p in range(group):
                for copy in copies(i * group + slots + p, slot + p):
                    copy.start()

        return state

    lax.fori_loop(0, steps // group, step, 0)


def product_call(blocks, places, pieces, s, k, q, cols, operator, near, before):
    rows = operator.shape[0]
    block = cols * q
    t = min(256, q)
    group = max(1, min(512, q) // t)
    slots = group * min(4, rows // (t * group))
    first = near is None
    vmem = pl.BlockSpec(memory_space=pltpu.VMEM)
    args = [places, *pieces]
    specs = [pl.BlockSpec(memory_space=pltpu.SMEM)] + [vmem] * len(pieces)
    if not first:
        args += near
        specs += [vmem] * 3
    if before is not None:
        args += before
        specs += [vmem] * 2
    args.append(operator)
    specs.append(pl.BlockSpec(memory_space=pl.ANY))
    wide = block * len(blocks)
    outs = [
        jax.ShapeDtypeStruct((2, s, rows // 2), f32),
        jax.ShapeDtypeStruct((s, padded(k)), f32),
    ]
    if first:
        outs += [jax.ShapeDtypeStruct((1, wide), f32), jax.ShapeDtypeStruct((1, wide), i32)]
    return pl.pallas_call(
        functools.partial(
            product_kernel, blocks, cols, slots, t, group, s, k, q, first, before is not None
        ),
        in_specs=specs,
        out_specs=[vmem] * len(outs),
        out_shape=outs,
        scratch_shapes=[
            pltpu.VMEM((2 * s, wide), bf16),
            pltpu.VMEM((slots * t, wide), bf16),
            pltpu.SemaphoreType.DMA((slots, len(blocks))),
        ],
        compiler_params=PARAMS,
        cost_estimate=pl.CostEstimate(
            flops=4 * s * rows * wide, bytes_accessed=2 * rows * wide, transcendentals=0
        ),
        name="product",
    )(*args)


def factor(gram):
    n = gram.shape[0]
    row = lax.broadcasted_iota(i32, (n, n), 0)
    lane = lax.broadcasted_iota(i32, (n, n), 1)
    left, right = gram, (row == lane).astype(f32)
    for k in range(n):
        pivot = left[k : k + 1, k : k + 1]
        root = lax.rsqrt(pivot)
        root = root * (1.5 - 0.5 * pivot * root * root)
        left_row = left[k : k + 1, :] * root
        right_row = right[k : k + 1, :] * root
        column = jnp.where(row > k, left[:, k : k + 1] * root, 0.0)
        left = jnp.where(row == k, left_row, left - column * left_row)
        right = jnp.where(row == k, right_row, right - column * right_row)
    return jnp.where(lane >= row, left, 0.0), jnp.where(lane <= row, right, 0.0)


def next_kernel(n, n_basis, kind, *refs):
    refs = list(refs)
    sums_ref, new_ref = refs.pop(0), refs.pop(0)
    basis_refs = [refs.pop(0) for _ in range(n_basis)]
    if kind != "last":
        image_ref, weight_ref, body_ref = refs.pop(0), refs.pop(0), refs.pop(0)
        image_refs = [refs.pop(0) for _ in range(n_basis)]
        mass_refs = [refs.pop(0) for _ in range(n_basis)]
    v_ref, upper_ref = refs.pop(0), refs.pop(0)
    if n_basis:
        coef_ref = refs.pop(0)
    s, q = v_ref.shape
    k = n_basis * s
    gram = sums_ref[:, k : k + s] / n
    if n_basis:
        coef = sums_ref[:, :k] / n
        gram = gram - dot_exact(coef, coef, 1, 1)
        row = lax.broadcasted_iota(i32, (k, s), 0)
        lane = lax.broadcasted_iota(i32, (k, s), 1)
        coef_ref[...] = coef.T + jnp.where(row == lane + (k - s), 0.5, 0.0)
    upper, inverse = factor(gram)
    upper_ref[...] = upper
    mix = inverse
    if n_basis:
        mix = jnp.concatenate([inverse, -dot_exact(inverse, coef, 1, 0)], axis=1)

    def mixed(values):
        return dot_exact(mix, jnp.concatenate(values, axis=0), 1, 0)

    v = mixed([new_ref[...]] + [r[...] for r in basis_refs])
    v_ref[...] = v
    if kind == "last":
        return
    y = mixed([image_ref[...]] + [r[...] for r in image_refs])
    mass = mixed([sums_ref[:, k + s : k + s + BODIES]] + [r[...] for r in mass_refs])
    onehot = onehot_of(body_ref[...])
    weight = weight_ref[...]
    means = mass * (BODIES / n)
    w = y + weight * dot_exact(means, onehot, 1, 0)
    stack = [r[...] for r in basis_refs] + [v, w]
    if kind == "middle":
        y_ref, w_ref, mass_ref, mean_ref, payload_ref = refs
        y_ref[...] = y
        mass_ref[...] = mass
        mean_ref[...] = means
        sums = dot_exact(w, jnp.concatenate(stack + [onehot * weight], axis=0), 1, 1)
        write_payload(payload_ref, y, sums)
    else:
        w_ref, sums_out = refs
        sums_out[...] = dot_exact(w, jnp.concatenate(stack, axis=0), 1, 1)
    w_ref[...] = w


def next_call(n, kind, sums, new, basis, image=None, weight=None, body=None, images=(), masses=()):
    s, q = new.shape
    n_basis = len(basis)
    args = [sums, new, *basis]
    if kind != "last":
        args += [image, weight, body, *images, *masses]
    outs = [jax.ShapeDtypeStruct((s, q), f32), jax.ShapeDtypeStruct((s, s), f32)]
    if n_basis:
        outs.append(jax.ShapeDtypeStruct((n_basis * s, s), f32))
    if kind == "middle":
        k = (n_basis + 2) * s + BODIES
        outs += [jax.ShapeDtypeStruct((s, q), f32)] * 2
        outs += [jax.ShapeDtypeStruct((s, BODIES), f32)] * 2
        outs.append(jax.ShapeDtypeStruct((s, payload_width(q, k)), i16))
    elif kind == "before last":
        outs.append(jax.ShapeDtypeStruct((s, q), f32))
        outs.append(jax.ShapeDtypeStruct((s, (n_basis + 2) * s), f32))
    vmem = pl.BlockSpec(memory_space=pltpu.VMEM)
    return pl.pallas_call(
        functools.partial(next_kernel, n, n_basis, kind),
        in_specs=[vmem] * len(args),
        out_specs=[vmem] * len(outs),
        out_shape=outs,
        compiler_params=PARAMS,
        name="next_block",
    )(*args)


def local(rows, cols, operator, rhs, bodies, weights):
    row_index, col_index = lax.axis_index("row"), lax.axis_index("col")
    s, block = rhs.shape
    n = block * rows
    q = block // cols
    span = rows // cols
    plane, inner = row_index // span, lax.rem(row_index, span)
    places = [(a, g, c) for a in range(cols) for g in range(span) for c in range(cols)]

    def index(a, g, c):
        return (a * span + g) * cols + c

    def permute(value, to):
        return lax.ppermute(value, AXES, [(index(*p), index(*to(*p))) for p in places])

    offsets = jnp.stack(
        [lax.rem(plane - e + cols, cols) * q for e in range(cols)]
        + [lax.rem(inner - d + span, span) * block for d in range(span)]
    ).astype(i32)

    def sum_all(value):
        for bit in [1 << b for b in range(cols.bit_length() - 1)]:
            value = value + permute(value, lambda a, g, c: (a, g, c ^ bit))
        for bit in [1 << b for b in range(span.bit_length() - 1)]:
            value = value + permute(value, lambda a, g, c: (a, g ^ bit, c))
        for bit in [1 << b for b in range(cols.bit_length() - 1)]:
            value = value + permute(value, lambda a, g, c: (a ^ bit, g, c))
        return value

    def scatter_cols(partial, sums):
        core = lax.rem(col_index, 2)
        keep = lax.dynamic_index_in_dim(partial, core, 0, False)
        send = lax.dynamic_index_in_dim(partial, 1 - core, 0, False)
        moved = permute(jnp.concatenate([send, sums], axis=1), lambda a, g, c: (a, g, c ^ 1))
        value = keep + moved[:, : keep.shape[1]]
        sums = sums + moved[:, keep.shape[1] :]
        bit = cols // 2
        while bit > 1:
            half = value.shape[1] // 2
            side = lax.rem(col_index // bit, 2)
            keep = lax.dynamic_slice_in_dim(value, side * half, half, 1)
            send = lax.dynamic_slice_in_dim(value, (1 - side) * half, half, 1)
            moved = permute(
                jnp.concatenate([send, sums], axis=1), lambda a, g, c, bit=bit: (a, g, c ^ bit)
            )
            value = keep + moved[:, :half]
            sums = sums + moved[:, half:]
            bit //= 2
        return value, sums

    def image(payload, k, near):
        rounds = [
            permute(payload, lambda a, g, c, d=d: ((c + d) % cols, g, a)) for d in range(cols)
        ]
        mine = jnp.stack(rounds)
        others = [
            permute(mine, lambda a, g, c, d=d: (a, (g + d) % span, c)) for d in range(1, span)
        ]
        first = near is None
        part = product_call(
            (0,), offsets, [mine], s, k, q, cols, operator, None if first else near[0], None
        )
        rest = product_call(
            tuple(range(1, span)),
            offsets,
            others,
            s,
            k,
            q,
            cols,
            operator,
            None if first else near[1],
            part[:2],
        )
        value, sums = scatter_cols(rest[0], rest[1])
        return value, sums, (part[2:], rest[2:])

    new, own_weight, own_body, payload = start_call(
        (col_index * q).astype(i32).reshape(1), rhs, weights[None, :], bodies[None, :], q
    )
    k = s + BODIES
    basis, images, masses, columns = [], [], [], []
    near = None
    for step in range(STEPS):
        value, sums, found = image(payload, k, near)
        if step == 0:
            around = found
        kind = "middle" if step < STEPS - 1 else "before last"
        out = next_call(
            n, kind, sums, new, basis, value, own_weight, own_body, images, masses
        )
        basis.append(out[0])
        columns.append(out[1 : 2 + min(step, 1)])
        if kind == "middle":
            y, new, mass, means, payload = out[-5:]
            images.append(y)
            masses.append(mass)
            near = [[*a, means] for a in around]
            k = (step + 2) * s + BODIES
        else:
            new, sums = out[-2:]
    out = next_call(n, "last", sum_all(sums), new, basis)
    basis.append(out[0])
    columns.append(out[1:])
    hess = []
    for step, (upper, coef) in enumerate(columns[1:]):
        below = (STEPS - 1 - step) * s
        hess.append(jnp.pad(jnp.concatenate([coef, upper], axis=0), ((0, below), (0, 0))))
    return (
        jnp.concatenate(basis, axis=0),
        jnp.concatenate(hess, axis=1),
        columns[0][0].T,
    )


def solution(mesh):
    rows, cols = mesh.shape["row"], mesh.shape["col"]
    in_specs = (P("row", "col"), P(None, "row"), P("row"), P("row"))
    out_specs = (P(None, ("row", "col")), P(), P())
    return jax.shard_map(
        functools.partial(local, rows, cols),
        mesh=mesh,
        in_specs=in_specs,
        out_specs=out_specs,
        check_vma=False,
    )
```

time: 592 us -> 191 us (0.32)
  blocking collectives: 281 us -> 0 us
  waiting for transfers between devices: 168 us -> 40.9 us
  Pallas kernels: 0 us -> 98 us
  matrix products: 94.7 us -> 0 us
  starting transfers between devices: 0.25 us -> 44.8 us
  other arithmetic: 28.9 us -> 1.54 us
  between operations: 14.4 us -> 0.97 us
    psum x7 -> x0, blocking collectives: 281 us -> none  [the longest x3 122 us: local(): lax.psum((product_t(stacked, image_block), product_t(image_block, image_b...]
    all_gather x3 -> x0, waiting for transfers between devices: 168 us -> none  [local(): gathered = lax.all_gather(current_low, ('row', 'col'), axis=1, tiled=True)]
    pallas_call x0 -> x11, Pallas kernels: none -> 98 us  [the longest x6 80.2 us: product_call(): pl.pallas_call(functools.partial(product_kernel, blocks, cols, slots, t,...]
    dot_general x22 -> x0, matrix products: 91.5 us -> none  [the longest x3 82.8 us: local(): lax.dot_general(col_block, operator, (((1,), (1,)), ((), ())), preferred_...]
    ppermute x0 -> x26, starting transfers between devices: none -> 44.8 us  [permute(): lax.ppermute(value, AXES, [(index(*p), index(*to(*p))) for p in places])]
    ppermute x0 -> x26, waiting for transfers between devices: none -> 40.9 us  [permute(): lax.ppermute(value, AXES, [(index(*p), index(*to(*p))) for p in places])]
    another operation x17 -> x3, other arithmetic: 25.4 us -> 0.12 us  [image(): mine = jnp.stack(rounds)]
  transfers between devices with their start and end apart: 6 -> 26, of which waited for: 3 -> 18; matrix products, arithmetic and copies ran while one was open for 0% -> 1% of each run, Pallas kernels for 0% -> 21%
where the time goes in v2:
time: 191 us
  Pallas kernels  98 us (51%)
  starting transfers between devices  44.8 us (23%)
  waiting for transfers between devices  40.9 us (21%)
  local copies, waits for them, and re-layouts  4.53 us (2%)
    pallas_call x6, Pallas kernels, product_call(): pl.pallas_call(functools.partial(product_kernel, blocks, cols, slots, t,...  80.2 us
    ppermute x26, starting transfers between devices, permute(): lax.ppermute(value, AXES, [(index(*p), index(*to(*p))) for p in places])  44.8 us
    ppermute x26, waiting for transfers between devices, permute(): lax.ppermute(value, AXES, [(index(*p), index(*to(*p))) for p in places])  40.9 us
    pallas_call x4, Pallas kernels, next_call(): pl.pallas_call(functools.partial(next_kernel, n, n_basis, kind), in_specs...  17.1 us
    unnamed x8, local copies, waits for them, and re-layouts  3.86 us
  transfers between devices with their start and end apart: 26, of which 18 were waited for; matrix products, arithmetic and copies ran while one was open for 1% of the time, Pallas kernels for 21%

profile of v2, /device:TPU:0, one launch (start us, length us, event | category | flops | bytes accessed | tf_op | source)
XLA Modules:
  0.0 190.8 jit_solution(943645930352335601)
XLA Ops:
  0.6 1.0 copy-done
  1.7 0.7 copy-done.1
  2.4 0.7 copy-done.2
  3.1 0.7 start.1
  3.8 5.1 %collective-permute-start.3 = (s16[48,1280]{1,0:T(8,128)(2,1)S(1)}, s16[48,1280]{1,0:T(8,128)(2,1)S(1)}, u32[]{:S(2)}, u32[]{:S(2)}) collective-permute-start(s16[48,1280]{1,0:T(8,128)(2,1)S(1)} %get-tuple-element.46), channel_id=1, source_target_pairs={{0,24},{1,0},{2,8},{3,16},{4,28},{5,4},{6,12},{7,20},{8,25},{9,1},... | collective-permute-start | bytes 368648 | tf_op jit(solution)/shard_map/ppermute | solution.py:366
  8.9 1.5 collective-permute-start.2
  10.4 0.7 collective-permute-start
  11.1 1.4 collective-permute-done.3
  12.5 3.1 %collective-permute-done.2 = s16[48,1280]{1,0:T(8,128)(2,1)S(1)} collective-permute-done((s16[48,1280]{1,0:T(8,128)(2,1)S(1)}, s16[48,1280]{1,0:T(8,128)(2,1)S(1)}, u32[]{:S(2)}, u32[]{:S(2)}) %collective-permute-start.2) | collective-permute-done | bytes 122912 | tf_op jit(solution)/shard_map/ppermute | solution.py:366
  15.5 2.2 %collective-permute-done.1 = s16[48,1280]{1,0:T(8,128)(2,1)S(1)} collective-permute-done((s16[48,1280]{1,0:T(8,128)(2,1)S(1)}, s16[48,1280]{1,0:T(8,128)(2,1)S(1)}, u32[]{:S(2)}, u32[]{:S(2)}) %collective-permute-start.1) | collective-permute-done | bytes 122912 | tf_op jit(solution)/shard_map/ppermute | solution.py:366
  17.8 1.6 collective-permute-start.4
  19.4 0.1 stack.72.refs_0_
  19.4 13.3 %product.6 = (f32[2,32,2048]{2,1,0:T(8,128)S(1)}, f32[32,128]{1,0:T(8,128)S(1)}, f32[1,4096]{1,0:T(1,128)S(1)}, s32[1,4096]{1,0:T(1,128)S(1)}) custom-call(s32[6]{0:T(128)S(1)} %stack.72.refs_0_, s16[4,48,1280]{2,1,0:T(8,128)(2,1)S(1)} %pad_add_fusion.refs_1_, bf16[4096,8192]{1,0:T(8,128)(2,1)} %refs_7_.3), custom_call_target="tpu_custom_call" | custom-call | flops 2147483648 | bytes 33554432 | tf_op jit(solution)/shard_map/product/pallas_call | solution.py:235
  32.7 13.2 %product.7 = (f32[2,32,2048]{2,1,0:T(8,128)S(1)}, f32[32,128]{1,0:T(8,128)S(1)}, f32[1,4096]{1,0:T(1,128)S(1)}, s32[1,4096]{1,0:T(1,128)S(1)}) custom-call(s32[6]{0:T(128)S(1)} %stack.72.refs_0_, s16[4,48,1280]{2,1,0:T(8,128)(2,1)S(1)} %collective-permute-done.4.refs_1_, f32[2,32,2048]{2,1,0:T(8,128)S(1)} %get-tuple-element.47.refs_2_, ...), custom_call_target="tpu_custom_call" | custom-call | flops 2147483648 | bytes 33554432 | tf_op jit(solution)/shard_map/product/pallas_call | solution.py:235
  46.0 0.1 collective-permute-start.5
  46.2 1.5 collective-permute-done.5
  47.8 5.2 %collective-permute-start.6 = (f32[32,1152]{1,0:T(8,128)S(1)}, f32[32,1152]{1,0:T(8,128)S(1)}, u32[]{:S(2)}, u32[]{:S(2)}) collective-permute-start(f32[32,1152]{1,0:T(8,128)S(1)} %pad_maximum_fusion.5), channel_id=1, source_target_pairs={{0,2},{1,3},{2,0},{3,1},{4,6},{5,7},{6,4},{7,5},{8,10},{9,11},{10,... | collective-permute-start | bytes 442376 | tf_op jit(solution)/shard_map/ppermute | solution.py:366
  52.9 4.1 %collective-permute-done.6 = f32[32,1152]{1,0:T(8,128)S(1)} collective-permute-done((f32[32,1152]{1,0:T(8,128)S(1)}, f32[32,1152]{1,0:T(8,128)S(1)}, u32[]{:S(2)}, u32[]{:S(2)}) %collective-permute-start.6) | collective-permute-done | bytes 147488 | tf_op jit(solution)/shard_map/ppermute | solution.py:366
  57.1 4.1 %next_block.4 = (f32[32,1024]{1,0:T(8,128)S(1)}, f32[32,32]{1,0:T(8,128)S(1)}, f32[32,1024]{1,0:T(8,128)S(1)}, f32[32,1024]{1,0:T(8,128)S(1)}, f32[32,64]{1,0:T(...) custom-call(f32[32,128]{1,0:T(8,128)S(1)} %slice_add_fusion.10.refs_0_, ...), custom_call_target="tpu_custom_call" | custom-call | tf_op jit(solution)/shard_map/next_block/pallas_call | solution.py:343
  61.2 2.0 %collective-permute-start.10 = (s16[32,1408]{1,0:T(8,128)(2,1)S(1)}, s16[32,1408]{1,0:T(8,128)(2,1)S(1)}, u32[]{:S(2)}, u32[]{:S(2)}) collective-permute-start(s16[32,1408]{1,0:T(8,128)(2,1)S(1)} %get-tuple-element.55), channel_id=1, source_target_pairs={{0,24},{1,0},{2,8},{3,16},{4,28},{5,4},{6,12},{7,20},{8,25},{9,1},... | collective-permute-start | bytes 270344 | tf_op jit(solution)/shard_map/ppermute | solution.py:366
  63.2 0.9 collective-permute-start.9
  64.1 1.5 collective-permute-start.8
  65.7 0.7 collective-permute-start.7
  66.3 3.0 %collective-permute-done.9 = s16[32,1408]{1,0:T(8,128)(2,1)S(1)} collective-permute-done((s16[32,1408]{1,0:T(8,128)(2,1)S(1)}, s16[32,1408]{1,0:T(8,128)(2,1)S(1)}, u32[]{:S(2)}, u32[]{:S(2)}) %collective-permute-start.9) | collective-permute-done | bytes 90144 | tf_op jit(solution)/shard_map/ppermute | solution.py:366
  69.3 0.1 collective-permute-done.8
  69.4 0.6 collective-permute-start.11
  70.0 13.4 %product.8 = (f32[2,32,2048]{2,1,0:T(8,128)S(1)}, f32[32,128]{1,0:T(8,128)S(1)}) custom-call(s32[6]{0:T(128)S(1)} %stack.72.refs_0_, s16[4,32,1408]{2,1,0:T(8,128)(2,1)S(1)} %pad_add_fusion.1.refs_1_, f32[1,4096]{1,0:T(1,128)S(1)} %get-tuple-element.59.refs_2_, s32[1,4096]{1,0:T(1,128)S(1)} %get-tuple-element.60.refs_3_, ...), custom_call_target="tpu_custom_call" | custom-call | flops 2147483648 | bytes 33554432 | tf_op jit(solution)/shard_map/product/pallas_call | solution.py:235
  83.4 13.4 %product.9 = (f32[2,32,2048]{2,1,0:T(8,128)S(1)}, f32[32,128]{1,0:T(8,128)S(1)}) custom-call(s32[6]{0:T(128)S(1)} %stack.72.refs_0_, s16[4,32,1408]{2,1,0:T(8,128)(2,1)S(1)} %collective-permute-done.11.refs_1_, f32[1,4096]{1,0:T(1,128)S(1)} %get-tuple-element.56.refs_2_, s32[1,4096]{1,0:T(1,128)S(1)} %get-tuple-element.57.refs_3_, ...), custom_call_target="tpu_custom_call" | custom-call | flops 2147483648 | bytes 33554432 | tf_op jit(solution)/shard_map/product/pallas_call | solution.py:235
  96.9 1.9 %collective-permute-start.12 = (f32[32,2176]{1,0:T(8,128)S(1)}, f32[32,2176]{1,0:T(8,128)S(1)}, u32[]{:S(2)}, u32[]{:S(2)}) collective-permute-start(f32[32,2176]{1,0:T(8,128)S(1)} %pad_maximum_fusion.3), channel_id=1, source_target_pairs={{0,1},{1,0},{2,3},{3,2},{4,5},{5,4},{6,7},{7,6},{8,9},{9,8},{10,11... | collective-permute-start | bytes 835592 | tf_op jit(solution)/shard_map/ppermute | solution.py:366
  98.9 1.2 collective-permute-done.12
  100.2 5.2 %collective-permute-start.13 = (f32[32,1152]{1,0:T(8,128)S(1)}, f32[32,1152]{1,0:T(8,128)S(1)}, u32[]{:S(2)}, u32[]{:S(2)}) collective-permute-start(f32[32,1152]{1,0:T(8,128)S(1)} %pad_maximum_fusion.6), channel_id=1, source_target_pairs={{0,2},{1,3},{2,0},{3,1},{4,6},{5,7},{6,4},{7,5},{8,10},{9,11},{10,... | collective-permute-start | bytes 442376 | tf_op jit(solution)/shard_map/ppermute | solution.py:366
  105.3 4.1 %collective-permute-done.13 = f32[32,1152]{1,0:T(8,128)S(1)} collective-permute-done((f32[32,1152]{1,0:T(8,128)S(1)}, f32[32,1152]{1,0:T(8,128)S(1)}, u32[]{:S(2)}, u32[]{:S(2)}) %collective-permute-start.13) | collective-permute-done | bytes 147488 | tf_op jit(solution)/shard_map/ppermute | solution.py:366
  109.5 4.8 %next_block.5 = (f32[32,1024]{1,0:T(8,128)S(1)}, f32[32,32]{1,0:T(8,128)S(1)}, f32[32,32]{1,0:T(8,128)S(1)}, f32[32,1024]{1,0:T(8,128)S(1)}, f32[32,1024]{1,0:T(...) custom-call(f32[32,128]{1,0:T(8,128)S(1)} %slice_add_fusion.8.refs_0_, ...), custom_call_target="tpu_custom_call" | custom-call | tf_op jit(solution)/shard_map/next_block/pallas_call | solution.py:343
  114.3 0.7 collective-permute-start.17
  115.0 1.7 collective-permute-start.16
  116.7 2.1 %collective-permute-start.15 = (s16[32,1408]{1,0:T(8,128)(2,1)S(1)}, s16[32,1408]{1,0:T(8,128)(2,1)S(1)}, u32[]{:S(2)}, u32[]{:S(2)}) collective-permute-start(s16[32,1408]{1,0:T(8,128)(2,1)S(1)} %get-tuple-element.69), channel_id=1, source_target_pairs={{0,8},{1,16},{2,24},{3,0},{4,12},{5,20},{6,28},{7,4},{8,9},{9,17},... | collective-permute-start | bytes 270344 | tf_op jit(solution)/shard_map/ppermute | solution.py:366
  118.8 0.8 collective-permute-start.14
  119.6 1.7 collective-permute-done.16
  121.3 0.5 collective-permute-done.15
  121.8 1.6 collective-permute-start.18
  123.4 13.4 %product.10 = (f32[2,32,2048]{2,1,0:T(8,128)S(1)}, f32[32,256]{1,0:T(8,128)S(1)}) custom-call(s32[6]{0:T(128)S(1)} %stack.72.refs_0_, s16[4,32,1408]{2,1,0:T(8,128)(2,1)S(1)} %pad_add_fusion.2.refs_1_, f32[1,4096]{1,0:T(1,128)S(1)} %get-tuple-element.59.refs_2_, s32[1,4096]{1,0:T(1,128)S(1)} %get-tuple-element.60.refs_3_, ...), custom_call_target="tpu_custom_call" | custom-call | flops 2147483648 | bytes 33554432 | tf_op jit(solution)/shard_map/product/pallas_call | solution.py:235
  136.8 13.4 %product.11 = (f32[2,32,2048]{2,1,0:T(8,128)S(1)}, f32[32,256]{1,0:T(8,128)S(1)}) custom-call(s32[6]{0:T(128)S(1)} %stack.72.refs_0_, s16[4,32,1408]{2,1,0:T(8,128)(2,1)S(1)} %collective-permute-done.18.refs_1_, f32[1,4096]{1,0:T(1,128)S(1)} %get-tuple-element.56.refs_2_, s32[1,4096]{1,0:T(1,128)S(1)} %get-tuple-element.57.refs_3_, ...), custom_call_target="tpu_custom_call" | custom-call | flops 2147483648 | bytes 33554432 | tf_op jit(solution)/shard_map/product/pallas_call | solution.py:235
  150.3 1.9 collective-permute-start.19
  152.2 1.2 collective-permute-done.19
  153.5 5.3 %collective-permute-start.20 = (f32[32,1280]{1,0:T(8,128)S(1)}, f32[32,1280]{1,0:T(8,128)S(1)}, u32[]{:S(2)}, u32[]{:S(2)}) collective-permute-start(f32[32,1280]{1,0:T(8,128)S(1)} %pad_maximum_fusion.4), channel_id=1, source_target_pairs={{0,2},{1,3},{2,0},{3,1},{4,6},{5,7},{6,4},{7,5},{8,10},{9,11},{10,... | collective-permute-start | bytes 491528 | tf_op jit(solution)/shard_map/ppermute | solution.py:366
  158.7 4.5 %collective-permute-done.20 = f32[32,1280]{1,0:T(8,128)S(1)} collective-permute-done((f32[32,1280]{1,0:T(8,128)S(1)}, f32[32,1280]{1,0:T(8,128)S(1)}, u32[]{:S(2)}, u32[]{:S(2)}) %collective-permute-start.20) | collective-permute-done | bytes 163872 | tf_op jit(solution)/shard_map/ppermute | solution.py:366
  163.3 4.6 %next_block.6 = (f32[32,1024]{1,0:T(8,128)S(1)}, f32[32,32]{1,0:T(8,128)S(1)}, f32[64,32]{1,0:T(8,128)S(1)}, f32[32,1024]{1,0:T(8,128)S(1)}, f32[32,128]{1,0:T(8,128)S(1)}) custom-call(f32[32,256]{1,0:T(8,128)S(1)} %slice_add_fusion.6.refs_0_, f32[32,1024]{1,0:T(8,128)S(1)} %get-tuple-element.75.refs_1_, f32[32,1024]{1,0:T(8,128)S(1)} %get-tuple-element.54.refs_2_, ...), custom_call_target="tpu_custom_call" | custom-call | tf_op jit(solution)/shard_map/next_block/pallas_call | solution.py:343
  167.9 1.2 collective-permute-done.21
  169.1 1.7 collective-permute-start.22
  170.8 2.0 %collective-permute-done.22 = f32[32,128]{1,0:T(8,128)S(1)} collective-permute-done((f32[32,128]{1,0:T(8,128)S(1)}, f32[32,128]{1,0:T(8,128)S(1)}, u32[]{:S(2)}, u32[]{:S(2)}) %collective-permute-start.22) | collective-permute-done | bytes 16416 | tf_op jit(solution)/shard_map/ppermute | solution.py:366
  172.8 0.5 collective-permute-start.23
  173.3 0.7 copy.16
  174.0 2.6 %collective-permute-done.23 = f32[32,128]{1,0:T(8,128)S(1)} collective-permute-done((f32[32,128]{1,0:T(8,128)S(1)}, f32[32,128]{1,0:T(8,128)S(1)}, u32[]{:S(2)}, u32[]{:S(2)}) %collective-permute-start.23) | collective-permute-done | bytes 16416 | tf_op jit(solution)/shard_map/ppermute | solution.py:366
  176.6 0.6 collective-permute-start.24
  177.3 3.0 %collective-permute-done.24 = f32[32,128]{1,0:T(8,128)S(1)} collective-permute-done((f32[32,128]{1,0:T(8,128)S(1)}, f32[32,128]{1,0:T(8,128)S(1)}, u32[]{:S(2)}, u32[]{:S(2)}) %collective-permute-start.24) | collective-permute-done | bytes 16416 | tf_op jit(solution)/shard_map/ppermute | solution.py:366
  180.3 1.0 collective-permute-start.25
  181.4 0.1 copy.11
  181.5 3.6 %collective-permute-done.25 = f32[32,128]{1,0:T(8,128)S(1)} collective-permute-done((f32[32,128]{1,0:T(8,128)S(1)}, f32[32,128]{1,0:T(8,128)S(1)}, u32[]{:S(2)}, u32[]{:S(2)}) %collective-permute-start.25) | collective-permute-done | bytes 16416 | tf_op jit(solution)/shard_map/ppermute | solution.py:366
  185.1 3.6 %next_block.7 = (f32[32,1024]{1,0:T(8,128)S(1)}, f32[32,32]{1,0:T(8,128)S(1)}, f32[96,32]{1,0:T(8,128)S(1)}) custom-call(f32[32,128]{1,0:T(8,128)S(1)} %add.135.refs_0_, f32[32,1024]{1,0:T(8,128)S(1)} %get-tuple-element.80.refs_1_, f32[32,1024]{1,0:T(8,128)S(1)} %get-tuple-element.54.refs_2_, f32[32,1024]{1,0:T(8,128)S(1)} %get-tuple-element.68.refs_3_, ...), custom_call_target="tpu_custom_call" | custom-call | tf_op jit(solution)/shard_map/next_block/pallas_call | solution.py:343
  188.8 0.8 pad_maximum_fusion
  189.7 0.1 pad_maximum_fusion.8
  189.8 0.1 copy.14
  189.9 0.1 fusion
  190.1 0.7 copy.15
  (51 shorter events, 1.0 us)
Async XLA Ops:
  0.6 1.0 copy-start
  1.7 0.7 copy-start.1
  2.4 0.7 copy-start.2
  3.8 8.6 %collective-permute-start.3 = (s16[48,1280]{1,0:T(8,128)(2,1)S(1)}, s16[48,1280]{1,0:T(8,128)(2,1)S(1)}, u32[]{:S(2)}, u32[]{:S(2)}) collective-permute-start(s16[48,1280]{1,0:T(8,128)(2,1)S(1)} %get-tuple-element.46), channel_id=1, source_target_pairs={{0,24},{1,0},{2,8},{3,16},{4,28},{5,4},{6,12},{7,20},{8,25},{9,1},... | collective-permute-start | bytes 368648 | tf_op jit(solution)/shard_map/ppermute | solution.py:366
  8.9 6.6 %collective-permute-start.2 = (s16[48,1280]{1,0:T(8,128)(2,1)S(1)}, s16[48,1280]{1,0:T(8,128)(2,1)S(1)}, u32[]{:S(2)}, u32[]{:S(2)}) collective-permute-start(s16[48,1280]{1,0:T(8,128)(2,1)S(1)} %get-tuple-element.46), channel_id=1, source_target_pairs={{0,16},{1,24},{2,0},{3,8},{4,20},{5,28},{6,4},{7,12},{8,17},{9,25}... | collective-permute-start | bytes 368648 | tf_op jit(solution)/shard_map/ppermute | solution.py:366
  10.4 7.3 %collective-permute-start.1 = (s16[48,1280]{1,0:T(8,128)(2,1)S(1)}, s16[48,1280]{1,0:T(8,128)(2,1)S(1)}, u32[]{:S(2)}, u32[]{:S(2)}) collective-permute-start(s16[48,1280]{1,0:T(8,128)(2,1)S(1)} %get-tuple-element.46), channel_id=1, source_target_pairs={{0,8},{1,16},{2,24},{3,0},{4,12},{5,20},{6,28},{7,4},{8,9},{9,17},... | collective-permute-start | bytes 368648 | tf_op jit(solution)/shard_map/ppermute | solution.py:366
  10.4 7.3 %collective-permute-start = (s16[48,1280]{1,0:T(8,128)(2,1)S(1)}, s16[48,1280]{1,0:T(8,128)(2,1)S(1)}, u32[]{:S(2)}, u32[]{:S(2)}) collective-permute-start(s16[48,1280]{1,0:T(8,128)(2,1)S(1)} %get-tuple-element.46), channel_id=1, source_target_pairs={{0,0},{1,8},{2,16},{3,24},{4,4},{5,12},{6,20},{7,28},{8,1},{9,9},{... | collective-permute-start | bytes 368648 | tf_op jit(solution)/shard_map/ppermute | solution.py:366
  17.8 15.0 %collective-permute-start.4 = (s16[4,48,1280]{2,1,0:T(8,128)(2,1)S(1)}, s16[4,48,1280]{2,1,0:T(8,128)(2,1)S(1)}, u32[]{:S(2)}, u32[]{:S(2)}) collective-permute-start(s16[4,48,1280]{2,1,0:T(8,128)(2,1)S(1)} %pad_add_fusion.refs_1_), channel_id=1, source_target_pairs={{0,4},{1,5},{2,6},{3,7},{4,0},{5,1},{6,2},{7,3},{8,12},{9,13},{10,... | collective-permute-start | bytes 1474568 | tf_op jit(solution)/shard_map/ppermute | solution.py:366
  46.0 1.6 collective-permute-start.5
  47.8 9.3 %collective-permute-start.6 = (f32[32,1152]{1,0:T(8,128)S(1)}, f32[32,1152]{1,0:T(8,128)S(1)}, u32[]{:S(2)}, u32[]{:S(2)}) collective-permute-start(f32[32,1152]{1,0:T(8,128)S(1)} %pad_maximum_fusion.5), channel_id=1, source_target_pairs={{0,2},{1,3},{2,0},{3,1},{4,6},{5,7},{6,4},{7,5},{8,10},{9,11},{10,... | collective-permute-start | bytes 442376 | tf_op jit(solution)/shard_map/ppermute | solution.py:366
  61.2 5.1 %collective-permute-start.10 = (s16[32,1408]{1,0:T(8,128)(2,1)S(1)}, s16[32,1408]{1,0:T(8,128)(2,1)S(1)}, u32[]{:S(2)}, u32[]{:S(2)}) collective-permute-start(s16[32,1408]{1,0:T(8,128)(2,1)S(1)} %get-tuple-element.55), channel_id=1, source_target_pairs={{0,24},{1,0},{2,8},{3,16},{4,28},{5,4},{6,12},{7,20},{8,25},{9,1},... | collective-permute-start | bytes 270344 | tf_op jit(solution)/shard_map/ppermute | solution.py:366
  63.2 6.1 %collective-permute-start.9 = (s16[32,1408]{1,0:T(8,128)(2,1)S(1)}, s16[32,1408]{1,0:T(8,128)(2,1)S(1)}, u32[]{:S(2)}, u32[]{:S(2)}) collective-permute-start(s16[32,1408]{1,0:T(8,128)(2,1)S(1)} %get-tuple-element.55), channel_id=1, source_target_pairs={{0,16},{1,24},{2,0},{3,8},{4,20},{5,28},{6,4},{7,12},{8,17},{9,25}... | collective-permute-start | bytes 270344 | tf_op jit(solution)/shard_map/ppermute | solution.py:366
  64.1 5.2 %collective-permute-start.8 = (s16[32,1408]{1,0:T(8,128)(2,1)S(1)}, s16[32,1408]{1,0:T(8,128)(2,1)S(1)}, u32[]{:S(2)}, u32[]{:S(2)}) collective-permute-start(s16[32,1408]{1,0:T(8,128)(2,1)S(1)} %get-tuple-element.55), channel_id=1, source_target_pairs={{0,8},{1,16},{2,24},{3,0},{4,12},{5,20},{6,28},{7,4},{8,9},{9,17},... | collective-permute-start | bytes 270344 | tf_op jit(solution)/shard_map/ppermute | solution.py:366
  65.7 3.7 %collective-permute-start.7 = (s16[32,1408]{1,0:T(8,128)(2,1)S(1)}, s16[32,1408]{1,0:T(8,128)(2,1)S(1)}, u32[]{:S(2)}, u32[]{:S(2)}) collective-permute-start(s16[32,1408]{1,0:T(8,128)(2,1)S(1)} %get-tuple-element.55), channel_id=1, source_target_pairs={{0,0},{1,8},{2,16},{3,24},{4,4},{5,12},{6,20},{7,28},{8,1},{9,9},{... | collective-permute-start | bytes 270344 | tf_op jit(solution)/shard_map/ppermute | solution.py:366
  69.4 14.0 %collective-permute-start.11 = (s16[4,32,1408]{2,1,0:T(8,128)(2,1)S(1)}, s16[4,32,1408]{2,1,0:T(8,128)(2,1)S(1)}, u32[]{:S(2)}, u32[]{:S(2)}) collective-permute-start(s16[4,32,1408]{2,1,0:T(8,128)(2,1)S(1)} %pad_add_fusion.1.refs_1_), channel_id=1, source_target_pairs={{0,4},{1,5},{2,6},{3,7},{4,0},{5,1},{6,2},{7,3},{8,12},{9,13},{10,... | collective-permute-start | bytes 1081352 | tf_op jit(solution)/shard_map/ppermute | solution.py:366
  96.9 3.1 %collective-permute-start.12 = (f32[32,2176]{1,0:T(8,128)S(1)}, f32[32,2176]{1,0:T(8,128)S(1)}, u32[]{:S(2)}, u32[]{:S(2)}) collective-permute-start(f32[32,2176]{1,0:T(8,128)S(1)} %pad_maximum_fusion.3), channel_id=1, source_target_pairs={{0,1},{1,0},{2,3},{3,2},{4,5},{5,4},{6,7},{7,6},{8,9},{9,8},{10,11... | collective-permute-start | bytes 835592 | tf_op jit(solution)/shard_map/ppermute | solution.py:366
  100.2 9.3 %collective-permute-start.13 = (f32[32,1152]{1,0:T(8,128)S(1)}, f32[32,1152]{1,0:T(8,128)S(1)}, u32[]{:S(2)}, u32[]{:S(2)}) collective-permute-start(f32[32,1152]{1,0:T(8,128)S(1)} %pad_maximum_fusion.6), channel_id=1, source_target_pairs={{0,2},{1,3},{2,0},{3,1},{4,6},{5,7},{6,4},{7,5},{8,10},{9,11},{10,... | collective-permute-start | bytes 442376 | tf_op jit(solution)/shard_map/ppermute | solution.py:366
  114.3 5.3 %collective-permute-start.17 = (s16[32,1408]{1,0:T(8,128)(2,1)S(1)}, s16[32,1408]{1,0:T(8,128)(2,1)S(1)}, u32[]{:S(2)}, u32[]{:S(2)}) collective-permute-start(s16[32,1408]{1,0:T(8,128)(2,1)S(1)} %get-tuple-element.69), channel_id=1, source_target_pairs={{0,24},{1,0},{2,8},{3,16},{4,28},{5,4},{6,12},{7,20},{8,25},{9,1},... | collective-permute-start | bytes 270344 | tf_op jit(solution)/shard_map/ppermute | solution.py:366
  115.0 6.3 %collective-permute-start.16 = (s16[32,1408]{1,0:T(8,128)(2,1)S(1)}, s16[32,1408]{1,0:T(8,128)(2,1)S(1)}, u32[]{:S(2)}, u32[]{:S(2)}) collective-permute-start(s16[32,1408]{1,0:T(8,128)(2,1)S(1)} %get-tuple-element.69), channel_id=1, source_target_pairs={{0,16},{1,24},{2,0},{3,8},{4,20},{5,28},{6,4},{7,12},{8,17},{9,25}... | collective-permute-start | bytes 270344 | tf_op jit(solution)/shard_map/ppermute | solution.py:366
  116.7 5.1 %collective-permute-start.15 = (s16[32,1408]{1,0:T(8,128)(2,1)S(1)}, s16[32,1408]{1,0:T(8,128)(2,1)S(1)}, u32[]{:S(2)}, u32[]{:S(2)}) collective-permute-start(s16[32,1408]{1,0:T(8,128)(2,1)S(1)} %get-tuple-element.69), channel_id=1, source_target_pairs={{0,8},{1,16},{2,24},{3,0},{4,12},{5,20},{6,28},{7,4},{8,9},{9,17},... | collective-permute-start | bytes 270344 | tf_op jit(solution)/shard_map/ppermute | solution.py:366
  118.8 3.0 %collective-permute-start.14 = (s16[32,1408]{1,0:T(8,128)(2,1)S(1)}, s16[32,1408]{1,0:T(8,128)(2,1)S(1)}, u32[]{:S(2)}, u32[]{:S(2)}) collective-permute-start(s16[32,1408]{1,0:T(8,128)(2,1)S(1)} %get-tuple-element.69), channel_id=1, source_target_pairs={{0,0},{1,8},{2,16},{3,24},{4,4},{5,12},{6,20},{7,28},{8,1},{9,9},{... | collective-permute-start | bytes 270344 | tf_op jit(solution)/shard_map/ppermute | solution.py:366
  121.8 15.0 %collective-permute-start.18 = (s16[4,32,1408]{2,1,0:T(8,128)(2,1)S(1)}, s16[4,32,1408]{2,1,0:T(8,128)(2,1)S(1)}, u32[]{:S(2)}, u32[]{:S(2)}) collective-permute-start(s16[4,32,1408]{2,1,0:T(8,128)(2,1)S(1)} %pad_add_fusion.2.refs_1_), channel_id=1, source_target_pairs={{0,4},{1,5},{2,6},{3,7},{4,0},{5,1},{6,2},{7,3},{8,12},{9,13},{10,... | collective-permute-start | bytes 1081352 | tf_op jit(solution)/shard_map/ppermute | solution.py:366
  150.3 3.1 %collective-permute-start.19 = (f32[32,2304]{1,0:T(8,128)S(1)}, f32[32,2304]{1,0:T(8,128)S(1)}, u32[]{:S(2)}, u32[]{:S(2)}) collective-permute-start(f32[32,2304]{1,0:T(8,128)S(1)} %pad_maximum_fusion.1), channel_id=1, source_target_pairs={{0,1},{1,0},{2,3},{3,2},{4,5},{5,4},{6,7},{7,6},{8,9},{9,8},{10,11... | collective-permute-start | bytes 884744 | tf_op jit(solution)/shard_map/ppermute | solution.py:366
  153.5 9.8 %collective-permute-start.20 = (f32[32,1280]{1,0:T(8,128)S(1)}, f32[32,1280]{1,0:T(8,128)S(1)}, u32[]{:S(2)}, u32[]{:S(2)}) collective-permute-start(f32[32,1280]{1,0:T(8,128)S(1)} %pad_maximum_fusion.4), channel_id=1, source_target_pairs={{0,2},{1,3},{2,0},{3,1},{4,6},{5,7},{6,4},{7,5},{8,10},{9,11},{10,... | collective-permute-start | bytes 491528 | tf_op jit(solution)/shard_map/ppermute | solution.py:366
  167.9 1.2 collective-permute-start.21
  169.1 3.7 %collective-permute-start.22 = (f32[32,128]{1,0:T(8,128)S(1)}, f32[32,128]{1,0:T(8,128)S(1)}, u32[]{:S(2)}, u32[]{:S(2)}) collective-permute-start(f32[32,128]{1,0:T(8,128)S(1)} %add.131), channel_id=1, source_target_pairs={{0,2},{1,3},{2,0},{3,1},{4,6},{5,7},{6,4},{7,5},{8,10},{9,11},{10,... | collective-permute-start | bytes 49160 | tf_op jit(solution)/shard_map/ppermute | solution.py:366
  172.8 3.7 %collective-permute-start.23 = (f32[32,128]{1,0:T(8,128)S(1)}, f32[32,128]{1,0:T(8,128)S(1)}, u32[]{:S(2)}, u32[]{:S(2)}) collective-permute-start(f32[32,128]{1,0:T(8,128)S(1)} %add.132), channel_id=1, source_target_pairs={{0,4},{1,5},{2,6},{3,7},{4,0},{5,1},{6,2},{7,3},{8,12},{9,13},{10,... | collective-permute-start | bytes 49160 | tf_op jit(solution)/shard_map/ppermute | solution.py:366
  176.6 3.7 %collective-permute-start.24 = (f32[32,128]{1,0:T(8,128)S(1)}, f32[32,128]{1,0:T(8,128)S(1)}, u32[]{:S(2)}, u32[]{:S(2)}) collective-permute-start(f32[32,128]{1,0:T(8,128)S(1)} %add.133), channel_id=1, source_target_pairs={{0,8},{1,9},{2,10},{3,11},{4,12},{5,13},{6,14},{7,15},{8,0},{9,1},... | collective-permute-start | bytes 49160 | tf_op jit(solution)/shard_map/ppermute | solution.py:366
  180.3 4.8 %collective-permute-start.25 = (f32[32,128]{1,0:T(8,128)S(1)}, f32[32,128]{1,0:T(8,128)S(1)}, u32[]{:S(2)}, u32[]{:S(2)}) collective-permute-start(f32[32,128]{1,0:T(8,128)S(1)} %add.134), channel_id=1, source_target_pairs={{0,16},{1,17},{2,18},{3,19},{4,20},{5,21},{6,22},{7,23},{8,24},{9,... | collective-permute-start | bytes 49160 | tf_op jit(solution)/shard_map/ppermute | solution.py:366

commit v3 on v2

--- a/solution.py
+++ b/solution.py
@@ -11,7 +11,7 @@
 STEPS = 3
 AXES = ("row", "col")
 LANES = 128
-EXTRA = 16
+EXTRA = 8
 PARAMS = pltpu.CompilerParams(vmem_limit_bytes=48 * 1024 * 1024)
 f32 = jnp.float32
 bf16 = jnp.bfloat16
@@ -54,50 +54,68 @@
     return jnp.ceil(8.0 * jnp.log2(largest * (1.0 / 32000.0)))
 
 
-def write_payload(ref, value, sums):
+def write_payload(ref, value, sums, extra=None):
     s, q = value.shape
+    k = sums.shape[1] - BODIES
     level = level_of(value)
-    ref[:s, :q] = jnp.round(value / jnp.exp2(level * 0.125)).astype(i32).astype(i16)
-    sum_level = level_of(sums)
-    scaled = sums / jnp.exp2(sum_level * 0.125)
+    codes = jnp.round(value / jnp.exp2(level * 0.125))
+    inner = sums[:, :k]
+    inner_level = level_of(inner)
+    scaled = inner / jnp.exp2(inner_level * 0.125)
     high = jnp.round(scaled)
-    low = jnp.round((scaled - high) * 2.0**15)
-    k = sums.shape[1]
-    rest = ref.shape[1] - q - 2 * k
+    low = jnp.round((scaled[:, k - s :] - high[:, k - s :]) * 2.0**15)
+    mass = sums[:, k:]
+    mass_level = level_of(mass)
+    mass_codes = jnp.round(mass / jnp.exp2(mass_level * 0.125))
+    rest = ref.shape[1] - q - k - s - BODIES
     lane = lax.broadcasted_iota(i32, (s, rest), 1)
-    levels = jnp.where(lane == 0, level, jnp.where(lane == 1, sum_level, 0.0))
-    ref[:s, q:] = jnp.concatenate([high, low, levels], axis=1).astype(i32).astype(i16)
+    levels = jnp.where(lane == 1, inner_level, jnp.where(lane == 2, mass_level, 0.0))
+    levels = jnp.where(lane == 0, level, levels)
+    tail = jnp.concatenate([high, low, mass_codes, levels], axis=1)
+    if extra is not None:
+        codes = jnp.concatenate([codes, extra], axis=0)
+        below = jnp.zeros((extra.shape[0], tail.shape[1]), f32)
+        tail = jnp.concatenate([tail, below], axis=0)
+    ref[:, :q] = codes.astype(i32).astype(i16)
+    ref[:, q:] = tail.astype(i32).astype(i16)
 
 
 def read_sums(tail, k):
-    scale = jnp.exp2(tail[:, 2 * k + 1 : 2 * k + 2] * 0.125)
-    return (tail[:, :k] + tail[:, k : 2 * k] * 2.0**-15) * scale
-
-
-def payload_width(q, k):
-    return q + padded(2 * k + 2)
-
-
-def start_kernel(at_ref, rhs_ref, weight_ref, body_ref, own_ref, w_ref, b_ref, payload_ref):
+    s = tail.shape[0]
+    k = k - BODIES
+    at = k + s + BODIES
+    low = jnp.concatenate([jnp.zeros((s, k - s), f32), tail[:, k : k + s]], axis=1) if k > s else tail[:, k : k + s]
+    inner = (tail[:, :k] + low * 2.0**-15) * jnp.exp2(tail[:, at + 1 : at + 2] * 0.125)
+    mass = tail[:, k + s : at] * jnp.exp2(tail[:, at + 2 : at + 3] * 0.125)
+    return jnp.concatenate([inner, mass], axis=1)
+
+
+def payload_width(q, k, s):
+    return q + padded(k + s + 3)
+
+
+def start_kernel(at_ref, rhs_hbm, weight_hbm, body_hbm, own_ref, w_ref, b_ref, payload_ref, sem):
     s, q = own_ref.shape
     at = pl.multiple_of(at_ref[0], LANES)
-    own = rhs_ref[:, pl.ds(at, q)]
-    weight = weight_ref[:, pl.ds(at, q)]
-    body = body_ref[:, pl.ds(at, q)]
-    own_ref[...] = own
-    w_ref[...] = weight
-    b_ref[...] = body
+    pairs = ((rhs_hbm, own_ref), (weight_hbm, w_ref), (body_hbm, b_ref))
+    copies = [
+        pltpu.make_async_copy(src.at[:, pl.ds(at, q)], dst, sem.at[i])
+        for i, (src, dst) in enumerate(pairs)
+    ]
+    for copy in copies:
+        copy.start()
+    for copy in copies:
+        copy.wait()
+    own, weight, body = own_ref[...], w_ref[...], b_ref[...]
     bodies = onehot_of(body) * weight
     sums = dot_exact(own, jnp.concatenate([own, bodies], axis=0), 1, 1)
-    write_payload(payload_ref, own, sums)
     scaled = weight * 2.0**14
     high = jnp.round(scaled)
     low = jnp.round((scaled - high) * 2.0**15)
     row = lax.broadcasted_iota(i32, (EXTRA, q), 0)
     extra = jnp.where(row == 0, high, jnp.where(row == 1, low, 0.0))
     extra = jnp.where(row == 2, body.astype(f32), extra)
-    payload_ref[s:, :q] = extra.astype(i32).astype(i16)
-    payload_ref[s:, q:] = jnp.zeros((EXTRA, payload_ref.shape[1] - q), i16)
+    write_payload(payload_ref, own, sums, extra)
 
 
 def start_call(at, rhs, weights, bodies, q):
@@ -106,15 +124,16 @@
     vmem = pl.BlockSpec(memory_space=pltpu.VMEM)
     return pl.pallas_call(
         start_kernel,
-        in_specs=[pl.BlockSpec(memory_space=pltpu.SMEM), vmem, vmem, vmem],
+        in_specs=[pl.BlockSpec(memory_space=pltpu.SMEM)] + [pl.BlockSpec(memory_space=pl.ANY)] * 3,
         out_specs=[vmem] * 4,
+        scratch_shapes=[pltpu.SemaphoreType.DMA((3,))],
         out_shape=[
             jax.ShapeDtypeStruct((s, q), f32),
             jax.ShapeDtypeStruct((1, q), f32),
             jax.ShapeDtypeStruct((1, q), i32),
-            jax.ShapeDtypeStruct((s + EXTRA, payload_width(q, k)), i16),
+            jax.ShapeDtypeStruct((s + EXTRA, payload_width(q, k, s)), i16),
         ],
-        compiler_params=PARAMS,
+        compiler_params=pltpu.CompilerParams(vmem_limit_bytes=63 * 1024 * 1024),
         name="start",
     )(at, rhs, weights, bodies)
 
@@ -160,7 +179,7 @@
             codes = piece_refs[b][e].astype(i32).astype(f32)
             tail = codes[:s, q:]
             total = total + read_sums(tail, k)
-            value = codes[:s, :q] * jnp.exp2(tail[:, 2 * k : 2 * k + 1] * 0.125)
+            value = codes[:s, :q] * jnp.exp2(tail[:, k + s : k + s + 1] * 0.125)
             if first:
                 weight = codes[s : s + 1, :q] + codes[s + 1 : s + 2, :q] * 2.0**-15
                 weight_out[:, pl.ds(at, q)] = weight * 2.0**-14
@@ -254,33 +273,47 @@
 
 def factor(gram):
     n = gram.shape[0]
-    row = lax.broadcasted_iota(i32, (n, n), 0)
-    lane = lax.broadcasted_iota(i32, (n, n), 1)
-    left, right = gram, (row == lane).astype(f32)
-    for k in range(n):
-        pivot = left[k : k + 1, k : k + 1]
-        root = lax.rsqrt(pivot)
-        root = root * (1.5 - 0.5 * pivot * root * root)
-        left_row = left[k : k + 1, :] * root
-        right_row = right[k : k + 1, :] * root
-        column = jnp.where(row > k, left[:, k : k + 1] * root, 0.0)
-        left = jnp.where(row == k, left_row, left - column * left_row)
-        right = jnp.where(row == k, right_row, right - column * right_row)
-    return jnp.where(lane >= row, left, 0.0), jnp.where(lane <= row, right, 0.0)
+    panel = 8
+    row = lax.broadcasted_iota(i32, (n, 2 * n), 0)
+    lane = lax.broadcasted_iota(i32, (n, 2 * n), 1)
+    left = jnp.concatenate([gram, jnp.zeros_like(gram)], axis=1) + (lane == row + n).astype(f32)
+    found, pivots = [], []
+    for at in range(0, n, panel):
+        height = n - at
+        pivot = jnp.ones((panel, 2 * n), f32)
+        for k in range(panel):
+            column = jnp.broadcast_to(left[:, at + k : at + k + 1], (height, 2 * n))
+            top = column[k : k + 1, :]
+            pivot = jnp.where(row[:panel] == k, top, pivot)
+            below = jnp.where(row[:height] > k, column, 0.0)
+            left = left - below * (left[k : k + 1, :] * (1.0 / top))
+        found.append(left[:panel])
+        pivots.append(pivot)
+        left = left[panel:]
+    left, pivot = jnp.concatenate(found, axis=0), jnp.concatenate(pivots, axis=0)
+    root = lax.rsqrt(pivot)
+    left = left * (root * (1.5 - 0.5 * pivot * root * root))
+    row, lane = row[:, :n], lane[:, :n]
+    return jnp.where(lane >= row, left[:, :n], 0.0), jnp.where(lane <= row, left[:, n:], 0.0)
 
 
 def next_kernel(n, n_basis, kind, *refs):
     refs = list(refs)
     sums_ref, new_ref = refs.pop(0), refs.pop(0)
     basis_refs = [refs.pop(0) for _ in range(n_basis)]
-    if kind != "last":
+    if kind == "last":
+        upper_refs = [refs.pop(0) for _ in range(n_basis)]
+        coef_refs = [refs.pop(0) for _ in range(n_basis - 1)]
+        out_ref, hess_ref, start_ref = refs
+        s, q = new_ref.shape
+    else:
         image_ref, weight_ref, body_ref = refs.pop(0), refs.pop(0), refs.pop(0)
         image_refs = [refs.pop(0) for _ in range(n_basis)]
         mass_refs = [refs.pop(0) for _ in range(n_basis)]
-    v_ref, upper_ref = refs.pop(0), refs.pop(0)
-    if n_basis:
-        coef_ref = refs.pop(0)
-    s, q = v_ref.shape
+        v_ref, upper_ref = refs.pop(0), refs.pop(0)
+        s, q = v_ref.shape
+        if n_basis:
+            coef_ref = refs.pop(0)
     k = n_basis * s
     gram = sums_ref[:, k : k + s] / n
     if n_basis:
@@ -288,9 +321,12 @@
         gram = gram - dot_exact(coef, coef, 1, 1)
         row = lax.broadcasted_iota(i32, (k, s), 0)
         lane = lax.broadcasted_iota(i32, (k, s), 1)
-        coef_ref[...] = coef.T + jnp.where(row == lane + (k - s), 0.5, 0.0)
+        shifted = coef.T + jnp.where(row == lane + (k - s), 0.5, 0.0)
+        if kind != "last":
+            coef_ref[...] = shifted
     upper, inverse = factor(gram)
-    upper_ref[...] = upper
+    if kind != "last":
+        upper_ref[...] = upper
     mix = inverse
     if n_basis:
         mix = jnp.concatenate([inverse, -dot_exact(inverse, coef, 1, 0)], axis=1)
@@ -299,9 +335,21 @@
         return dot_exact(mix, jnp.concatenate(values, axis=0), 1, 0)
 
     v = mixed([new_ref[...]] + [r[...] for r in basis_refs])
+    if kind == "last":
+        for b, ref in enumerate(basis_refs):
+            out_ref[b * s : (b + 1) * s, :] = ref[...]
+        out_ref[n_basis * s :, :] = v
+        hess = []
+        for b in range(n_basis):
+            blocks = [coef_refs[b][...] if b < n_basis - 1 else shifted]
+            blocks.append(upper_refs[b + 1][...] if b < n_basis - 1 else upper)
+            if b < n_basis - 1:
+                blocks.append(jnp.zeros(((n_basis - 1 - b) * s, s), f32))
+            hess.append(jnp.concatenate(blocks, axis=0))
+        hess_ref[...] = jnp.concatenate(hess, axis=1)
+        start_ref[...] = upper_refs[0][...].T
+        return
     v_ref[...] = v
-    if kind == "last":
-        return
     y = mixed([image_ref[...]] + [r[...] for r in image_refs])
     mass = mixed([sums_ref[:, k + s : k + s + BODIES]] + [r[...] for r in mass_refs])
     onehot = onehot_of(body_ref[...])
@@ -322,20 +370,25 @@
     w_ref[...] = w
 
 
-def next_call(n, kind, sums, new, basis, image=None, weight=None, body=None, images=(), masses=()):
+def next_call(n, kind, sums, new, basis, *more):
     s, q = new.shape
     n_basis = len(basis)
-    args = [sums, new, *basis]
-    if kind != "last":
-        args += [image, weight, body, *images, *masses]
-    outs = [jax.ShapeDtypeStruct((s, q), f32), jax.ShapeDtypeStruct((s, s), f32)]
-    if n_basis:
-        outs.append(jax.ShapeDtypeStruct((n_basis * s, s), f32))
+    args = [sums, new, *basis, *more]
+    if kind == "last":
+        outs = [
+            jax.ShapeDtypeStruct(((n_basis + 1) * s, q), f32),
+            jax.ShapeDtypeStruct(((n_basis + 1) * s, n_basis * s), f32),
+            jax.ShapeDtypeStruct((s, s), f32),
+        ]
+    else:
+        outs = [jax.ShapeDtypeStruct((s, q), f32), jax.ShapeDtypeStruct((s, s), f32)]
+        if n_basis:
+            outs.append(jax.ShapeDtypeStruct((n_basis * s, s), f32))
     if kind == "middle":
         k = (n_basis + 2) * s + BODIES
         outs += [jax.ShapeDtypeStruct((s, q), f32)] * 2
         outs += [jax.ShapeDtypeStruct((s, BODIES), f32)] * 2
-        outs.append(jax.ShapeDtypeStruct((s, payload_width(q, k)), i16))
+        outs.append(jax.ShapeDtypeStruct((s, payload_width(q, k, s)), i16))
     elif kind == "before last":
         outs.append(jax.ShapeDtypeStruct((s, q), f32))
         outs.append(jax.ShapeDtypeStruct((s, (n_basis + 2) * s), f32))
@@ -392,11 +445,16 @@
             side = lax.rem(col_index // bit, 2)
             keep = lax.dynamic_slice_in_dim(value, side * half, half, 1)
             send = lax.dynamic_slice_in_dim(value, (1 - side) * half, half, 1)
-            moved = permute(
-                jnp.concatenate([send, sums], axis=1), lambda a, g, c, bit=bit: (a, g, c ^ bit)
-            )
-            value = keep + moved[:, :half]
-            sums = sums + moved[:, half:]
+            level = level_of(send)
+            codes = jnp.round(send / jnp.exp2(level * 0.125))
+            levels = jnp.broadcast_to(level, (s, LANES))
+            codes = jnp.concatenate([codes, levels], axis=1).astype(i16)
+            moved, more = [
+                permute(v, lambda a, g, c, bit=bit: (a, g, c ^ bit)) for v in (codes, sums)
+            ]
+            scale = jnp.exp2(moved[:, half : half + 1].astype(f32) * 0.125)
+            value = keep + moved[:, :half].astype(f32) * scale
+            sums = sums + more
             bit //= 2
         return value, sums
 
@@ -431,38 +489,29 @@
         (col_index * q).astype(i32).reshape(1), rhs, weights[None, :], bodies[None, :], q
     )
     k = s + BODIES
-    basis, images, masses, columns = [], [], [], []
+    basis, images, masses, uppers, coefs = [], [], [], [], []
     near = None
     for step in range(STEPS):
         value, sums, found = image(payload, k, near)
         if step == 0:
             around = found
         kind = "middle" if step < STEPS - 1 else "before last"
-        out = next_call(
-            n, kind, sums, new, basis, value, own_weight, own_body, images, masses
+        out = list(
+            next_call(n, kind, sums, new, basis, value, own_weight, own_body, *images, *masses)
         )
-        basis.append(out[0])
-        columns.append(out[1 : 2 + min(step, 1)])
+        basis.append(out.pop(0))
+        uppers.append(out.pop(0))
+        if step:
+            coefs.append(out.pop(0))
         if kind == "middle":
-            y, new, mass, means, payload = out[-5:]
+            y, new, mass, means, payload = out
             images.append(y)
             masses.append(mass)
             near = [[*a, means] for a in around]
             k = (step + 2) * s + BODIES
         else:
-            new, sums = out[-2:]
-    out = next_call(n, "last", sum_all(sums), new, basis)
-    basis.append(out[0])
-    columns.append(out[1:])
-    hess = []
-    for step, (upper, coef) in enumerate(columns[1:]):
-        below = (STEPS - 1 - step) * s
-        hess.append(jnp.pad(jnp.concatenate([coef, upper], axis=0), ((0, below), (0, 0))))
-    return (
-        jnp.concatenate(basis, axis=0),
-        jnp.concatenate(hess, axis=1),
-        columns[0][0].T,
-    )
+            new, sums = out
+    return tuple(next_call(n, "last", sum_all(sums), new, basis, *uppers, *coefs))
 
 
 def solution(mesh):

time: 191 us -> 186 us (0.974)
  local copies, waits for them, and re-layouts: 4.53 us -> 1.1 us
  starting transfers between devices: 44.8 us -> 42.1 us
  Pallas kernels: 98 us -> 100 us
    unnamed x8 -> x6, local copies, waits for them, and re-layouts: 3.86 us -> 0.01 us
    ppermute x26 -> x29, starting transfers between devices: 44.8 us -> 42.1 us  [permute(): lax.ppermute(value, AXES, [(index(*p), index(*to(*p))) for p in places])]
    ppermute x26 -> x29, waiting for transfers between devices: 40.9 us -> 40 us  [permute(): lax.ppermute(value, AXES, [(index(*p), index(*to(*p))) for p in places])]
  transfers between devices with their start and end apart: 26 -> 29, of which waited for: 18 -> 18; matrix products, arithmetic and copies ran while one was open for 1% -> 0% of each run, Pallas kernels for 21% -> 22%
where the time goes in v3:
time: 186 us
  Pallas kernels  100 us (54%)
  starting transfers between devices  42.1 us (23%)
  waiting for transfers between devices  40 us (22%)
    pallas_call x6, Pallas kernels, product_call(): pl.pallas_call(functools.partial(product_kernel, blocks, cols, slots, t,...  80.1 us
    ppermute x29, starting transfers between devices, permute(): lax.ppermute(value, AXES, [(index(*p), index(*to(*p))) for p in places])  42.1 us
    ppermute x29, waiting for transfers between devices, permute(): lax.ppermute(value, AXES, [(index(*p), index(*to(*p))) for p in places])  40 us
    pallas_call x4, Pallas kernels, next_call(): pl.pallas_call(functools.partial(next_kernel, n, n_basis, kind), in_specs...  17.6 us
  transfers between devices with their start and end apart: 29, of which 18 were waited for; matrix products, arithmetic and copies ran while one was open for 0% of the time, Pallas kernels for 22%

profile of v3, /device:TPU:0, one launch (start us, length us, event | category | flops | bytes accessed | tf_op | source)
XLA Modules:
  0.0 185.8 jit_solution(5807388086652517128)
XLA Ops:
  0.6 2.3 %start.1 = (f32[32,1024]{1,0:T(8,128)}, f32[1,1024]{1,0:T(1,128)}, s32[1,1024]{1,0:T(1,128)}, s16[40,1280]{1,0:T(8,128)(2,1)}) custom-call(s32[1]{0:T(128)} %bitcast.6.at_ref, f32[32,4096]{1,0:T(8,128)} %rhs_hbm.1, f32[1,4096]{1,0:T(1,128)} %bitcast.45, s32[1,4096]{1,0:T(1,128)} %bitcast.46), custom_call_target="tpu_custom_call" | custom-call | tf_op jit(solution)/shard_map/start/pallas_call | solution.py:125
  2.9 5.1 %collective-permute-start.3 = (s16[40,1280]{1,0:T(8,128)(2,1)}, s16[40,1280]{1,0:T(8,128)(2,1)S(1)}, u32[]{:S(2)}, u32[]{:S(2)}) collective-permute-start(s16[40,1280]{1,0:T(8,128)(2,1)} %get-tuple-element.43), channel_id=1, source_target_pairs={{0,24},{1,0},{2,8},{3,16},{4,28},{5,4},{6,12},{7,20},{8,25},{9,1},... | collective-permute-start | bytes 307208 | tf_op jit(solution)/shard_map/ppermute | solution.py:419
  8.0 1.5 collective-permute-start.2
  9.5 1.5 collective-permute-start
  11.1 0.4 collective-permute-done.3
  11.4 2.3 %collective-permute-done.2 = s16[40,1280]{1,0:T(8,128)(2,1)S(1)} collective-permute-done((s16[40,1280]{1,0:T(8,128)(2,1)}, s16[40,1280]{1,0:T(8,128)(2,1)S(1)}, u32[]{:S(2)}, u32[]{:S(2)}) %collective-permute-start.2) | collective-permute-done | bytes 102432 | tf_op jit(solution)/shard_map/ppermute | solution.py:419
  13.8 2.1 %collective-permute-done.1 = s16[40,1280]{1,0:T(8,128)(2,1)S(1)} collective-permute-done((s16[40,1280]{1,0:T(8,128)(2,1)}, s16[40,1280]{1,0:T(8,128)(2,1)S(1)}, u32[]{:S(2)}, u32[]{:S(2)}) %collective-permute-start.1) | collective-permute-done | bytes 102432 | tf_op jit(solution)/shard_map/ppermute | solution.py:419
  15.9 1.6 collective-permute-start.4
  17.6 13.3 %product.6 = (f32[2,32,2048]{2,1,0:T(8,128)S(1)}, f32[32,128]{1,0:T(8,128)S(1)}, f32[1,4096]{1,0:T(1,128)S(1)}, s32[1,4096]{1,0:T(1,128)S(1)}) custom-call(s32[6]{0:T(128)S(1)} %stack.72.refs_0_, s16[4,40,1280]{2,1,0:T(8,128)(2,1)S(1)} %pad_add_fusion.refs_1_, bf16[4096,8192]{1,0:T(8,128)(2,1)} %refs_7_.3), custom_call_target="tpu_custom_call" | custom-call | flops 2147483648 | bytes 33554432 | tf_op jit(solution)/shard_map/product/pallas_call | solution.py:254
  30.9 13.3 %product.7 = (f32[2,32,2048]{2,1,0:T(8,128)S(1)}, f32[32,128]{1,0:T(8,128)S(1)}, f32[1,4096]{1,0:T(1,128)S(1)}, s32[1,4096]{1,0:T(1,128)S(1)}) custom-call(s32[6]{0:T(128)S(1)} %stack.72.refs_0_, s16[4,40,1280]{2,1,0:T(8,128)(2,1)S(1)} %collective-permute-done.4.refs_1_, f32[2,32,2048]{2,1,0:T(8,128)S(1)} %get-tuple-element.44.refs_2_, ...), custom_call_target="tpu_custom_call" | custom-call | flops 2147483648 | bytes 33554432 | tf_op jit(solution)/shard_map/product/pallas_call | solution.py:254
  44.3 0.1 collective-permute-start.5
  44.4 1.5 collective-permute-done.5
  45.9 0.1 abs_reduce_fusion.2
  46.1 0.1 round-nearest-even_convert_fusion.2
  46.3 5.7 %collective-permute-start.7 = (s16[32,1152]{1,0:T(8,128)(2,1)S(1)}, s16[32,1152]{1,0:T(8,128)(2,1)S(1)}, u32[]{:S(2)}, u32[]{:S(2)}) collective-permute-start(s16[32,1152]{1,0:T(8,128)(2,1)S(1)} %pad_add_fusion.3), channel_id=1, source_target_pairs={{0,2},{1,3},{2,0},{3,1},{4,6},{5,7},{6,4},{7,5},{8,10},{9,11},{10,... | collective-permute-start | bytes 221192 | tf_op jit(solution)/shard_map/ppermute | solution.py:419
  52.1 3.7 %collective-permute-done.6 = f32[32,128]{1,0:T(8,128)S(1)} collective-permute-done((f32[32,128]{1,0:T(8,128)S(1)}, f32[32,128]{1,0:T(8,128)S(1)}, u32[]{:S(2)}, u32[]{:S(2)}) %collective-permute-start.6) | collective-permute-done | bytes 16416 | tf_op jit(solution)/shard_map/ppermute | solution.py:419
  55.7 0.1 exponential_reduce_fusion.2
  55.8 0.1 multiply_add_fusion.2.refs_2_
  56.0 4.1 %next_block.4 = (f32[32,1024]{1,0:T(8,128)S(1)}, f32[32,32]{1,0:T(8,128)S(1)}, f32[32,1024]{1,0:T(8,128)S(1)}, f32[32,1024]{1,0:T(8,128)S(1)}, f32[32,64]{1,0:T(...) custom-call(f32[32,128]{1,0:T(8,128)S(1)} %add.113.refs_0_, f32[32,1024]{1,0:T(8,128)S(1)} %copy-done, ...), custom_call_target="tpu_custom_call" | custom-call | tf_op jit(solution)/shard_map/next_block/pallas_call | solution.py:396
  60.0 0.4 collective-permute-start.11
  60.4 0.9 collective-permute-start.10
  61.4 2.3 %collective-permute-start.9 = (s16[32,1280]{1,0:T(8,128)(2,1)S(1)}, s16[32,1280]{1,0:T(8,128)(2,1)S(1)}, u32[]{:S(2)}, u32[]{:S(2)}) collective-permute-start(s16[32,1280]{1,0:T(8,128)(2,1)S(1)} %get-tuple-element.51), channel_id=1, source_target_pairs={{0,8},{1,16},{2,24},{3,0},{4,12},{5,20},{6,28},{7,4},{8,9},{9,17},... | collective-permute-start | bytes 245768 | tf_op jit(solution)/shard_map/ppermute | solution.py:419
  63.7 0.7 collective-permute-start.8
  64.3 2.1 %collective-permute-done.10 = s16[32,1280]{1,0:T(8,128)(2,1)S(1)} collective-permute-done((s16[32,1280]{1,0:T(8,128)(2,1)S(1)}, s16[32,1280]{1,0:T(8,128)(2,1)S(1)}, u32[]{:S(2)}, u32[]{:S(2)}) %collective-permute-start.10) | collective-permute-done | bytes 81952 | tf_op jit(solution)/shard_map/ppermute | solution.py:419
  66.5 0.2 collective-permute-done.9
  66.7 0.6 collective-permute-start.12
  67.3 13.4 %product.8 = (f32[2,32,2048]{2,1,0:T(8,128)S(1)}, f32[32,128]{1,0:T(8,128)S(1)}) custom-call(s32[6]{0:T(128)S(1)} %stack.72.refs_0_, s16[4,32,1280]{2,1,0:T(8,128)(2,1)S(1)} %pad_add_fusion.1.refs_1_, f32[1,4096]{1,0:T(1,128)S(1)} %get-tuple-element.55.refs_2_, s32[1,4096]{1,0:T(1,128)S(1)} %get-tuple-element.56.refs_3_, ...), custom_call_target="tpu_custom_call" | custom-call | flops 2147483648 | bytes 33554432 | tf_op jit(solution)/shard_map/product/pallas_call | solution.py:254
  80.7 13.4 %product.9 = (f32[2,32,2048]{2,1,0:T(8,128)S(1)}, f32[32,128]{1,0:T(8,128)S(1)}) custom-call(s32[6]{0:T(128)S(1)} %stack.72.refs_0_, s16[4,32,1280]{2,1,0:T(8,128)(2,1)S(1)} %collective-permute-done.12.refs_1_, f32[1,4096]{1,0:T(1,128)S(1)} %get-tuple-element.52.refs_2_, s32[1,4096]{1,0:T(1,128)S(1)} %get-tuple-element.53.refs_3_, ...), custom_call_target="tpu_custom_call" | custom-call | flops 2147483648 | bytes 33554432 | tf_op jit(solution)/shard_map/product/pallas_call | solution.py:254
  94.2 2.3 %collective-permute-start.13 = (f32[32,2176]{1,0:T(8,128)S(1)}, f32[32,2176]{1,0:T(8,128)S(1)}, u32[]{:S(2)}, u32[]{:S(2)}) collective-permute-start(f32[32,2176]{1,0:T(8,128)S(1)} %pad_maximum_fusion.2), channel_id=1, source_target_pairs={{0,1},{1,0},{2,3},{3,2},{4,5},{5,4},{6,7},{7,6},{8,9},{9,8},{10,11... | collective-permute-start | bytes 835592 | tf_op jit(solution)/shard_map/ppermute | solution.py:419
  96.5 1.2 collective-permute-done.13
  97.7 0.1 abs_reduce_fusion.1
  97.9 0.1 round-nearest-even_convert_fusion.1
  98.1 4.6 %collective-permute-start.15 = (s16[32,1152]{1,0:T(8,128)(2,1)S(1)}, s16[32,1152]{1,0:T(8,128)(2,1)S(1)}, u32[]{:S(2)}, u32[]{:S(2)}) collective-permute-start(s16[32,1152]{1,0:T(8,128)(2,1)S(1)} %pad_add_fusion.4), channel_id=1, source_target_pairs={{0,2},{1,3},{2,0},{3,1},{4,6},{5,7},{6,4},{7,5},{8,10},{9,11},{10,... | collective-permute-start | bytes 221192 | tf_op jit(solution)/shard_map/ppermute | solution.py:419
  102.7 3.7 %collective-permute-done.14 = f32[32,128]{1,0:T(8,128)S(1)} collective-permute-done((f32[32,128]{1,0:T(8,128)S(1)}, f32[32,128]{1,0:T(8,128)S(1)}, u32[]{:S(2)}, u32[]{:S(2)}) %collective-permute-start.14) | collective-permute-done | bytes 16416 | tf_op jit(solution)/shard_map/ppermute | solution.py:419
  106.4 0.1 exponential_reduce_fusion.1
  106.5 0.1 multiply_add_fusion.1.refs_3_
  106.6 4.7 %next_block.5 = (f32[32,1024]{1,0:T(8,128)S(1)}, f32[32,32]{1,0:T(8,128)S(1)}, f32[32,32]{1,0:T(8,128)S(1)}, f32[32,1024]{1,0:T(8,128)S(1)}, f32[32,1024]{1,0:T(...) custom-call(f32[32,128]{1,0:T(8,128)S(1)} %add.120.refs_0_, ...), custom_call_target="tpu_custom_call" | custom-call | tf_op jit(solution)/shard_map/next_block/pallas_call | solution.py:396
  111.3 0.6 collective-permute-start.19
  111.9 1.1 collective-permute-start.18
  113.0 1.9 %collective-permute-start.17 = (s16[32,1280]{1,0:T(8,128)(2,1)S(1)}, s16[32,1280]{1,0:T(8,128)(2,1)S(1)}, u32[]{:S(2)}, u32[]{:S(2)}) collective-permute-start(s16[32,1280]{1,0:T(8,128)(2,1)S(1)} %get-tuple-element.65), channel_id=1, source_target_pairs={{0,8},{1,16},{2,24},{3,0},{4,12},{5,20},{6,28},{7,4},{8,9},{9,17},... | collective-permute-start | bytes 245768 | tf_op jit(solution)/shard_map/ppermute | solution.py:419
  114.9 0.8 collective-permute-start.16
  115.8 3.0 %collective-permute-done.18 = s16[32,1280]{1,0:T(8,128)(2,1)S(1)} collective-permute-done((s16[32,1280]{1,0:T(8,128)(2,1)S(1)}, s16[32,1280]{1,0:T(8,128)(2,1)S(1)}, u32[]{:S(2)}, u32[]{:S(2)}) %collective-permute-start.18) | collective-permute-done | bytes 81952 | tf_op jit(solution)/shard_map/ppermute | solution.py:419
  118.7 0.2 collective-permute-done.17
  119.0 1.6 collective-permute-start.20
  120.5 13.4 %product.10 = (f32[2,32,2048]{2,1,0:T(8,128)S(1)}, f32[32,256]{1,0:T(8,128)S(1)}) custom-call(s32[6]{0:T(128)S(1)} %stack.72.refs_0_, s16[4,32,1280]{2,1,0:T(8,128)(2,1)S(1)} %pad_add_fusion.2.refs_1_, f32[1,4096]{1,0:T(1,128)S(1)} %get-tuple-element.55.refs_2_, s32[1,4096]{1,0:T(1,128)S(1)} %get-tuple-element.56.refs_3_, ...), custom_call_target="tpu_custom_call" | custom-call | flops 2147483648 | bytes 33554432 | tf_op jit(solution)/shard_map/product/pallas_call | solution.py:254
  134.0 13.3 %product.11 = (f32[2,32,2048]{2,1,0:T(8,128)S(1)}, f32[32,256]{1,0:T(8,128)S(1)}) custom-call(s32[6]{0:T(128)S(1)} %stack.72.refs_0_, s16[4,32,1280]{2,1,0:T(8,128)(2,1)S(1)} %collective-permute-done.20.refs_1_, f32[1,4096]{1,0:T(1,128)S(1)} %get-tuple-element.52.refs_2_, s32[1,4096]{1,0:T(1,128)S(1)} %get-tuple-element.53.refs_3_, ...), custom_call_target="tpu_custom_call" | custom-call | flops 2147483648 | bytes 33554432 | tf_op jit(solution)/shard_map/product/pallas_call | solution.py:254
  147.3 1.0 collective-permute-start.21
  148.4 1.2 collective-permute-done.21
  149.6 0.1 abs_reduce_fusion
  149.8 0.1 round-nearest-even_convert_fusion
  150.0 5.1 %collective-permute-start.23 = (s16[32,1152]{1,0:T(8,128)(2,1)S(1)}, s16[32,1152]{1,0:T(8,128)(2,1)S(1)}, u32[]{:S(2)}, u32[]{:S(2)}) collective-permute-start(s16[32,1152]{1,0:T(8,128)(2,1)S(1)} %pad_add_fusion.5), channel_id=1, source_target_pairs={{0,2},{1,3},{2,0},{3,1},{4,6},{5,7},{6,4},{7,5},{8,10},{9,11},{10,... | collective-permute-start | bytes 221192 | tf_op jit(solution)/shard_map/ppermute | solution.py:419
  155.1 3.8 %collective-permute-done.22 = f32[32,256]{1,0:T(8,128)S(1)} collective-permute-done((f32[32,256]{1,0:T(8,128)S(1)}, f32[32,256]{1,0:T(8,128)S(1)}, u32[]{:S(2)}, u32[]{:S(2)}) %collective-permute-start.22) | collective-permute-done | bytes 32800 | tf_op jit(solution)/shard_map/ppermute | solution.py:419
  158.9 0.1 exponential_reduce_fusion
  159.2 4.5 %next_block.6 = (f32[32,1024]{1,0:T(8,128)S(1)}, f32[32,32]{1,0:T(8,128)S(1)}, f32[64,32]{1,0:T(8,128)S(1)}, f32[32,1024]{1,0:T(8,128)S(1)}, f32[32,128]{1,0:T(8,128)S(1)}) custom-call(f32[32,256]{1,0:T(8,128)S(1)} %add.124.refs_0_, f32[32,1024]{1,0:T(8,128)S(1)} %get-tuple-element.71.refs_1_, f32[32,1024]{1,0:T(8,128)S(1)} %get-tuple-element.62.refs_2_, ...), custom_call_target="tpu_custom_call" | custom-call | tf_op jit(solution)/shard_map/next_block/pallas_call | solution.py:396
  163.7 1.2 collective-permute-done.24
  164.9 1.1 collective-permute-start.25
  166.0 2.6 %collective-permute-done.25 = f32[32,128]{1,0:T(8,128)S(1)} collective-permute-done((f32[32,128]{1,0:T(8,128)S(1)}, f32[32,128]{1,0:T(8,128)S(1)}, u32[]{:S(2)}, u32[]{:S(2)}) %collective-permute-start.25) | collective-permute-done | bytes 16416 | tf_op jit(solution)/shard_map/ppermute | solution.py:419
  168.6 0.5 collective-permute-start.26
  169.1 3.2 %collective-permute-done.26 = f32[32,128]{1,0:T(8,128)S(1)} collective-permute-done((f32[32,128]{1,0:T(8,128)S(1)}, f32[32,128]{1,0:T(8,128)S(1)}, u32[]{:S(2)}, u32[]{:S(2)}) %collective-permute-start.26) | collective-permute-done | bytes 16416 | tf_op jit(solution)/shard_map/ppermute | solution.py:419
  172.4 3.7 %collective-permute-done.27 = f32[32,128]{1,0:T(8,128)S(1)} collective-permute-done((f32[32,128]{1,0:T(8,128)S(1)}, f32[32,128]{1,0:T(8,128)S(1)}, u32[]{:S(2)}, u32[]{:S(2)}) %collective-permute-start.27) | collective-permute-done | bytes 16416 | tf_op jit(solution)/shard_map/ppermute | solution.py:419
  176.1 0.7 collective-permute-start.28
  176.8 3.9 %collective-permute-done.28 = f32[32,128]{1,0:T(8,128)S(1)} collective-permute-done((f32[32,128]{1,0:T(8,128)S(1)}, f32[32,128]{1,0:T(8,128)S(1)}, u32[]{:S(2)}, u32[]{:S(2)}) %collective-permute-start.28) | collective-permute-done | bytes 16416 | tf_op jit(solution)/shard_map/ppermute | solution.py:419
  180.7 4.3 %next_block.7 = (f32[128,1024]{1,0:T(8,128)}, f32[128,96]{1,0:T(8,128)S(1)}, f32[32,32]{1,0:T(8,128)}) custom-call(f32[32,128]{1,0:T(8,128)S(1)} %add.131.refs_0_, f32[32,1024]{1,0:T(8,128)S(1)} %get-tuple-element.76.refs_1_, f32[32,1024]{1,0:T(8,128)S(1)} %get-tuple-element.62.refs_2_, f32[32,1024]{1,0:T(8,128)S(1)} %get-tuple-element.72.refs_3_, ...), custom_call_target="tpu_custom_call" | custom-call | tf_op jit(solution)/shard_map/next_block/pallas_call | solution.py:396
  185.1 0.7 copy.8
  (57 shorter events, 1.2 us)
Async XLA Ops:
  2.9 8.5 %collective-permute-start.3 = (s16[40,1280]{1,0:T(8,128)(2,1)}, s16[40,1280]{1,0:T(8,128)(2,1)S(1)}, u32[]{:S(2)}, u32[]{:S(2)}) collective-permute-start(s16[40,1280]{1,0:T(8,128)(2,1)} %get-tuple-element.43), channel_id=1, source_target_pairs={{0,24},{1,0},{2,8},{3,16},{4,28},{5,4},{6,12},{7,20},{8,25},{9,1},... | collective-permute-start | bytes 307208 | tf_op jit(solution)/shard_map/ppermute | solution.py:419
  8.0 5.7 %collective-permute-start.2 = (s16[40,1280]{1,0:T(8,128)(2,1)}, s16[40,1280]{1,0:T(8,128)(2,1)S(1)}, u32[]{:S(2)}, u32[]{:S(2)}) collective-permute-start(s16[40,1280]{1,0:T(8,128)(2,1)} %get-tuple-element.43), channel_id=1, source_target_pairs={{0,16},{1,24},{2,0},{3,8},{4,20},{5,28},{6,4},{7,12},{8,17},{9,25}... | collective-permute-start | bytes 307208 | tf_op jit(solution)/shard_map/ppermute | solution.py:419
  9.5 6.3 %collective-permute-start.1 = (s16[40,1280]{1,0:T(8,128)(2,1)}, s16[40,1280]{1,0:T(8,128)(2,1)S(1)}, u32[]{:S(2)}, u32[]{:S(2)}) collective-permute-start(s16[40,1280]{1,0:T(8,128)(2,1)} %get-tuple-element.43), channel_id=1, source_target_pairs={{0,8},{1,16},{2,24},{3,0},{4,12},{5,20},{6,28},{7,4},{8,9},{9,17},... | collective-permute-start | bytes 307208 | tf_op jit(solution)/shard_map/ppermute | solution.py:419
  9.5 6.3 %collective-permute-start = (s16[40,1280]{1,0:T(8,128)(2,1)}, s16[40,1280]{1,0:T(8,128)(2,1)S(1)}, u32[]{:S(2)}, u32[]{:S(2)}) collective-permute-start(s16[40,1280]{1,0:T(8,128)(2,1)} %get-tuple-element.43), channel_id=1, source_target_pairs={{0,0},{1,8},{2,16},{3,24},{4,4},{5,12},{6,20},{7,28},{8,1},{9,9},{... | collective-permute-start | bytes 307208 | tf_op jit(solution)/shard_map/ppermute | solution.py:419
  15.9 15.0 %collective-permute-start.4 = (s16[4,40,1280]{2,1,0:T(8,128)(2,1)S(1)}, s16[4,40,1280]{2,1,0:T(8,128)(2,1)S(1)}, u32[]{:S(2)}, u32[]{:S(2)}) collective-permute-start(s16[4,40,1280]{2,1,0:T(8,128)(2,1)S(1)} %pad_add_fusion.refs_1_), channel_id=1, source_target_pairs={{0,4},{1,5},{2,6},{3,7},{4,0},{5,1},{6,2},{7,3},{8,12},{9,13},{10,... | collective-permute-start | bytes 1228808 | tf_op jit(solution)/shard_map/ppermute | solution.py:419
  17.6 38.4 %copy-start = (f32[32,1024]{1,0:T(8,128)S(1)}, f32[32,1024]{1,0:T(8,128)}, u32[]{:S(2)}) copy-start(f32[32,1024]{1,0:T(8,128)} %get-tuple-element.48.refs_1_) | copy-start | bytes 393220
  17.6 38.4 %copy-start.1 = (f32[1,1024]{1,0:T(1,128)S(1)}, f32[1,1024]{1,0:T(1,128)}, u32[]{:S(2)}) copy-start(f32[1,1024]{1,0:T(1,128)} %get-tuple-element.49.refs_3_.refs_4_.refs_5_) | copy-start | bytes 12292
  17.6 38.4 %copy-start.2 = (s32[1,1024]{1,0:T(1,128)S(1)}, s32[1,1024]{1,0:T(1,128)}, u32[]{:S(2)}) copy-start(s32[1,1024]{1,0:T(1,128)} %get-tuple-element.50.refs_4_.refs_5_.refs_6_) | copy-start | bytes 12292
  44.3 1.6 collective-permute-start.5
  46.3 9.4 %collective-permute-start.7 = (s16[32,1152]{1,0:T(8,128)(2,1)S(1)}, s16[32,1152]{1,0:T(8,128)(2,1)S(1)}, u32[]{:S(2)}, u32[]{:S(2)}) collective-permute-start(s16[32,1152]{1,0:T(8,128)(2,1)S(1)} %pad_add_fusion.3), channel_id=1, source_target_pairs={{0,2},{1,3},{2,0},{3,1},{4,6},{5,7},{6,4},{7,5},{8,10},{9,11},{10,... | collective-permute-start | bytes 221192 | tf_op jit(solution)/shard_map/ppermute | solution.py:419
  52.0 3.7 %collective-permute-start.6 = (f32[32,128]{1,0:T(8,128)S(1)}, f32[32,128]{1,0:T(8,128)S(1)}, u32[]{:S(2)}, u32[]{:S(2)}) collective-permute-start(f32[32,128]{1,0:T(8,128)S(1)} %slice_add_fusion.5), channel_id=1, source_target_pairs={{0,2},{1,3},{2,0},{3,1},{4,6},{5,7},{6,4},{7,5},{8,10},{9,11},{10,... | collective-permute-start | bytes 49160 | tf_op jit(solution)/shard_map/ppermute | solution.py:419
  60.0 4.3 %collective-permute-start.11 = (s16[32,1280]{1,0:T(8,128)(2,1)S(1)}, s16[32,1280]{1,0:T(8,128)(2,1)S(1)}, u32[]{:S(2)}, u32[]{:S(2)}) collective-permute-start(s16[32,1280]{1,0:T(8,128)(2,1)S(1)} %get-tuple-element.51), channel_id=1, source_target_pairs={{0,24},{1,0},{2,8},{3,16},{4,28},{5,4},{6,12},{7,20},{8,25},{9,1},... | collective-permute-start | bytes 245768 | tf_op jit(solution)/shard_map/ppermute | solution.py:419
  60.4 6.0 %collective-permute-start.10 = (s16[32,1280]{1,0:T(8,128)(2,1)S(1)}, s16[32,1280]{1,0:T(8,128)(2,1)S(1)}, u32[]{:S(2)}, u32[]{:S(2)}) collective-permute-start(s16[32,1280]{1,0:T(8,128)(2,1)S(1)} %get-tuple-element.51), channel_id=1, source_target_pairs={{0,16},{1,24},{2,0},{3,8},{4,20},{5,28},{6,4},{7,12},{8,17},{9,25}... | collective-permute-start | bytes 245768 | tf_op jit(solution)/shard_map/ppermute | solution.py:419
  61.4 5.3 %collective-permute-start.9 = (s16[32,1280]{1,0:T(8,128)(2,1)S(1)}, s16[32,1280]{1,0:T(8,128)(2,1)S(1)}, u32[]{:S(2)}, u32[]{:S(2)}) collective-permute-start(s16[32,1280]{1,0:T(8,128)(2,1)S(1)} %get-tuple-element.51), channel_id=1, source_target_pairs={{0,8},{1,16},{2,24},{3,0},{4,12},{5,20},{6,28},{7,4},{8,9},{9,17},... | collective-permute-start | bytes 245768 | tf_op jit(solution)/shard_map/ppermute | solution.py:419
  63.7 3.0 %collective-permute-start.8 = (s16[32,1280]{1,0:T(8,128)(2,1)S(1)}, s16[32,1280]{1,0:T(8,128)(2,1)S(1)}, u32[]{:S(2)}, u32[]{:S(2)}) collective-permute-start(s16[32,1280]{1,0:T(8,128)(2,1)S(1)} %get-tuple-element.51), channel_id=1, source_target_pairs={{0,0},{1,8},{2,16},{3,24},{4,4},{5,12},{6,20},{7,28},{8,1},{9,9},{... | collective-permute-start | bytes 245768 | tf_op jit(solution)/shard_map/ppermute | solution.py:419
  66.7 13.9 %collective-permute-start.12 = (s16[4,32,1280]{2,1,0:T(8,128)(2,1)S(1)}, s16[4,32,1280]{2,1,0:T(8,128)(2,1)S(1)}, u32[]{:S(2)}, u32[]{:S(2)}) collective-permute-start(s16[4,32,1280]{2,1,0:T(8,128)(2,1)S(1)} %pad_add_fusion.1.refs_1_), channel_id=1, source_target_pairs={{0,4},{1,5},{2,6},{3,7},{4,0},{5,1},{6,2},{7,3},{8,12},{9,13},{10,... | collective-permute-start | bytes 983048 | tf_op jit(solution)/shard_map/ppermute | solution.py:419
  94.2 3.5 %collective-permute-start.13 = (f32[32,2176]{1,0:T(8,128)S(1)}, f32[32,2176]{1,0:T(8,128)S(1)}, u32[]{:S(2)}, u32[]{:S(2)}) collective-permute-start(f32[32,2176]{1,0:T(8,128)S(1)} %pad_maximum_fusion.2), channel_id=1, source_target_pairs={{0,1},{1,0},{2,3},{3,2},{4,5},{5,4},{6,7},{7,6},{8,9},{9,8},{10,11... | collective-permute-start | bytes 835592 | tf_op jit(solution)/shard_map/ppermute | solution.py:419
  98.1 8.3 %collective-permute-start.15 = (s16[32,1152]{1,0:T(8,128)(2,1)S(1)}, s16[32,1152]{1,0:T(8,128)(2,1)S(1)}, u32[]{:S(2)}, u32[]{:S(2)}) collective-permute-start(s16[32,1152]{1,0:T(8,128)(2,1)S(1)} %pad_add_fusion.4), channel_id=1, source_target_pairs={{0,2},{1,3},{2,0},{3,1},{4,6},{5,7},{6,4},{7,5},{8,10},{9,11},{10,... | collective-permute-start | bytes 221192 | tf_op jit(solution)/shard_map/ppermute | solution.py:419
  102.6 3.7 %collective-permute-start.14 = (f32[32,128]{1,0:T(8,128)S(1)}, f32[32,128]{1,0:T(8,128)S(1)}, u32[]{:S(2)}, u32[]{:S(2)}) collective-permute-start(f32[32,128]{1,0:T(8,128)S(1)} %slice_add_fusion.4), channel_id=1, source_target_pairs={{0,2},{1,3},{2,0},{3,1},{4,6},{5,7},{6,4},{7,5},{8,10},{9,11},{10,... | collective-permute-start | bytes 49160 | tf_op jit(solution)/shard_map/ppermute | solution.py:419
  111.3 4.5 %collective-permute-start.19 = (s16[32,1280]{1,0:T(8,128)(2,1)S(1)}, s16[32,1280]{1,0:T(8,128)(2,1)S(1)}, u32[]{:S(2)}, u32[]{:S(2)}) collective-permute-start(s16[32,1280]{1,0:T(8,128)(2,1)S(1)} %get-tuple-element.65), channel_id=1, source_target_pairs={{0,24},{1,0},{2,8},{3,16},{4,28},{5,4},{6,12},{7,20},{8,25},{9,1},... | collective-permute-start | bytes 245768 | tf_op jit(solution)/shard_map/ppermute | solution.py:419
  111.9 6.9 %collective-permute-start.18 = (s16[32,1280]{1,0:T(8,128)(2,1)S(1)}, s16[32,1280]{1,0:T(8,128)(2,1)S(1)}, u32[]{:S(2)}, u32[]{:S(2)}) collective-permute-start(s16[32,1280]{1,0:T(8,128)(2,1)S(1)} %get-tuple-element.65), channel_id=1, source_target_pairs={{0,16},{1,24},{2,0},{3,8},{4,20},{5,28},{6,4},{7,12},{8,17},{9,25}... | collective-permute-start | bytes 245768 | tf_op jit(solution)/shard_map/ppermute | solution.py:419
  113.0 6.0 %collective-permute-start.17 = (s16[32,1280]{1,0:T(8,128)(2,1)S(1)}, s16[32,1280]{1,0:T(8,128)(2,1)S(1)}, u32[]{:S(2)}, u32[]{:S(2)}) collective-permute-start(s16[32,1280]{1,0:T(8,128)(2,1)S(1)} %get-tuple-element.65), channel_id=1, source_target_pairs={{0,8},{1,16},{2,24},{3,0},{4,12},{5,20},{6,28},{7,4},{8,9},{9,17},... | collective-permute-start | bytes 245768 | tf_op jit(solution)/shard_map/ppermute | solution.py:419
  114.9 4.0 %collective-permute-start.16 = (s16[32,1280]{1,0:T(8,128)(2,1)S(1)}, s16[32,1280]{1,0:T(8,128)(2,1)S(1)}, u32[]{:S(2)}, u32[]{:S(2)}) collective-permute-start(s16[32,1280]{1,0:T(8,128)(2,1)S(1)} %get-tuple-element.65), channel_id=1, source_target_pairs={{0,0},{1,8},{2,16},{3,24},{4,4},{5,12},{6,20},{7,28},{8,1},{9,9},{... | collective-permute-start | bytes 245768 | tf_op jit(solution)/shard_map/ppermute | solution.py:419
  119.0 15.0 %collective-permute-start.20 = (s16[4,32,1280]{2,1,0:T(8,128)(2,1)S(1)}, s16[4,32,1280]{2,1,0:T(8,128)(2,1)S(1)}, u32[]{:S(2)}, u32[]{:S(2)}) collective-permute-start(s16[4,32,1280]{2,1,0:T(8,128)(2,1)S(1)} %pad_add_fusion.2.refs_1_), channel_id=1, source_target_pairs={{0,4},{1,5},{2,6},{3,7},{4,0},{5,1},{6,2},{7,3},{8,12},{9,13},{10,... | collective-permute-start | bytes 983048 | tf_op jit(solution)/shard_map/ppermute | solution.py:419
  147.3 2.2 %collective-permute-start.21 = (f32[32,2304]{1,0:T(8,128)S(1)}, f32[32,2304]{1,0:T(8,128)S(1)}, u32[]{:S(2)}, u32[]{:S(2)}) collective-permute-start(f32[32,2304]{1,0:T(8,128)S(1)} %pad_maximum_fusion), channel_id=1, source_target_pairs={{0,1},{1,0},{2,3},{3,2},{4,5},{5,4},{6,7},{7,6},{8,9},{9,8},{10,11... | collective-permute-start | bytes 884744 | tf_op jit(solution)/shard_map/ppermute | solution.py:419
  150.0 9.0 %collective-permute-start.23 = (s16[32,1152]{1,0:T(8,128)(2,1)S(1)}, s16[32,1152]{1,0:T(8,128)(2,1)S(1)}, u32[]{:S(2)}, u32[]{:S(2)}) collective-permute-start(s16[32,1152]{1,0:T(8,128)(2,1)S(1)} %pad_add_fusion.5), channel_id=1, source_target_pairs={{0,2},{1,3},{2,0},{3,1},{4,6},{5,7},{6,4},{7,5},{8,10},{9,11},{10,... | collective-permute-start | bytes 221192 | tf_op jit(solution)/shard_map/ppermute | solution.py:419
  155.0 3.9 %collective-permute-start.22 = (f32[32,256]{1,0:T(8,128)S(1)}, f32[32,256]{1,0:T(8,128)S(1)}, u32[]{:S(2)}, u32[]{:S(2)}) collective-permute-start(f32[32,256]{1,0:T(8,128)S(1)} %slice_add_fusion.3), channel_id=1, source_target_pairs={{0,2},{1,3},{2,0},{3,1},{4,6},{5,7},{6,4},{7,5},{8,10},{9,11},{10,... | collective-permute-start | bytes 98312 | tf_op jit(solution)/shard_map/ppermute | solution.py:419
  163.7 1.2 collective-permute-start.24
  164.9 3.7 %collective-permute-start.25 = (f32[32,128]{1,0:T(8,128)S(1)}, f32[32,128]{1,0:T(8,128)S(1)}, u32[]{:S(2)}, u32[]{:S(2)}) collective-permute-start(f32[32,128]{1,0:T(8,128)S(1)} %add.127), channel_id=1, source_target_pairs={{0,2},{1,3},{2,0},{3,1},{4,6},{5,7},{6,4},{7,5},{8,10},{9,11},{10,... | collective-permute-start | bytes 49160 | tf_op jit(solution)/shard_map/ppermute | solution.py:419
  168.6 3.7 %collective-permute-start.26 = (f32[32,128]{1,0:T(8,128)S(1)}, f32[32,128]{1,0:T(8,128)S(1)}, u32[]{:S(2)}, u32[]{:S(2)}) collective-permute-start(f32[32,128]{1,0:T(8,128)S(1)} %add.128), channel_id=1, source_target_pairs={{0,4},{1,5},{2,6},{3,7},{4,0},{5,1},{6,2},{7,3},{8,12},{9,13},{10,... | collective-permute-start | bytes 49160 | tf_op jit(solution)/shard_map/ppermute | solution.py:419
  172.4 3.7 %collective-permute-start.27 = (f32[32,128]{1,0:T(8,128)S(1)}, f32[32,128]{1,0:T(8,128)S(1)}, u32[]{:S(2)}, u32[]{:S(2)}) collective-permute-start(f32[32,128]{1,0:T(8,128)S(1)} %add.129), channel_id=1, source_target_pairs={{0,8},{1,9},{2,10},{3,11},{4,12},{5,13},{6,14},{7,15},{8,0},{9,1},... | collective-permute-start | bytes 49160 | tf_op jit(solution)/shard_map/ppermute | solution.py:419
  176.1 4.6 %collective-permute-start.28 = (f32[32,128]{1,0:T(8,128)S(1)}, f32[32,128]{1,0:T(8,128)S(1)}, u32[]{:S(2)}, u32[]{:S(2)}) collective-permute-start(f32[32,128]{1,0:T(8,128)S(1)} %add.130), channel_id=1, source_target_pairs={{0,16},{1,17},{2,18},{3,19},{4,20},{5,21},{6,22},{7,23},{8,24},{9,... | collective-permute-start | bytes 49160 | tf_op jit(solution)/shard_map/ppermute | solution.py:419

commit v4 on v3

--- a/solution.py
+++ b/solution.py
@@ -38,6 +38,14 @@
 def split(value):
     high = value.astype(bf16)
     return high, (value - high.astype(f32)).astype(bf16)
+
+
+def dot_close(left, right, left_dim, right_dim):
+    left_high, left_low = split(left)
+    right_high, right_low = split(right)
+    rows = left.shape[0]
+    both = dot(jnp.concatenate([left_high, left_low], axis=0), right_high, left_dim, right_dim)
+    return both[:rows] + both[rows:] + dot(left_high, right_low, left_dim, right_dim)
 
 
 def onehot_of(body):
@@ -108,7 +116,7 @@
         copy.wait()
     own, weight, body = own_ref[...], w_ref[...], b_ref[...]
     bodies = onehot_of(body) * weight
-    sums = dot_exact(own, jnp.concatenate([own, bodies], axis=0), 1, 1)
+    sums = dot_close(own, jnp.concatenate([own, bodies], axis=0), 1, 1)
     scaled = weight * 2.0**14
     high = jnp.round(scaled)
     low = jnp.round((scaled - high) * 2.0**15)
@@ -332,7 +340,7 @@
         mix = jnp.concatenate([inverse, -dot_exact(inverse, coef, 1, 0)], axis=1)
 
     def mixed(values):
-        return dot_exact(mix, jnp.concatenate(values, axis=0), 1, 0)
+        return dot_close(mix, jnp.concatenate(values, axis=0), 1, 0)
 
     v = mixed([new_ref[...]] + [r[...] for r in basis_refs])
     if kind == "last":
@@ -355,18 +363,18 @@
     onehot = onehot_of(body_ref[...])
     weight = weight_ref[...]
     means = mass * (BODIES / n)
-    w = y + weight * dot_exact(means, onehot, 1, 0)
+    w = y + weight * dot_close(means, onehot, 1, 0)
     stack = [r[...] for r in basis_refs] + [v, w]
     if kind == "middle":
         y_ref, w_ref, mass_ref, mean_ref, payload_ref = refs
         y_ref[...] = y
         mass_ref[...] = mass
         mean_ref[...] = means
-        sums = dot_exact(w, jnp.concatenate(stack + [onehot * weight], axis=0), 1, 1)
+        sums = dot_close(w, jnp.concatenate(stack + [onehot * weight], axis=0), 1, 1)
         write_payload(payload_ref, y, sums)
     else:
         w_ref, sums_out = refs
-        sums_out[...] = dot_exact(w, jnp.concatenate(stack, axis=0), 1, 1)
+        sums_out[...] = dot_close(w, jnp.concatenate(stack, axis=0), 1, 1)
     w_ref[...] = w
 
 

time: 186 us -> 184 us (0.989)
  no operation moved by 1% of the time
where the time goes in v4:
time: 184 us
  Pallas kernels  98.2 us (53%)
  starting transfers between devices  42.2 us (23%)
  waiting for transfers between devices  40 us (22%)
    pallas_call x6, Pallas kernels, product_call(): pl.pallas_call(functools.partial(product_kernel, blocks, cols, slots, t,...  80.1 us
    ppermute x29, starting transfers between devices, permute(): lax.ppermute(value, AXES, [(index(*p), index(*to(*p))) for p in places])  42.2 us
    ppermute x29, waiting for transfers between devices, permute(): lax.ppermute(value, AXES, [(index(*p), index(*to(*p))) for p in places])  40 us
    pallas_call x4, Pallas kernels, next_call(): pl.pallas_call(functools.partial(next_kernel, n, n_basis, kind), in_specs...  16 us
  transfers between devices with their start and end apart: 29, of which 18 were waited for; matrix products, arithmetic and copies ran while one was open for 0% of the time, Pallas kernels for 22%

profile of v4, /device:TPU:0, one launch (start us, length us, event | category | flops | bytes accessed | tf_op | source)
XLA Modules:
  0.0 184.0 jit_solution(7887868841761573491)
XLA Ops:
  0.6 2.0 %start.1 = (f32[32,1024]{1,0:T(8,128)}, f32[1,1024]{1,0:T(1,128)}, s32[1,1024]{1,0:T(1,128)}, s16[40,1280]{1,0:T(8,128)(2,1)}) custom-call(s32[1]{0:T(128)} %bitcast.6.at_ref, f32[32,4096]{1,0:T(8,128)} %rhs_hbm.1, f32[1,4096]{1,0:T(1,128)} %bitcast.45, s32[1,4096]{1,0:T(1,128)} %bitcast.46), custom_call_target="tpu_custom_call" | custom-call | tf_op jit(solution)/shard_map/start/pallas_call | solution.py:133
  2.7 5.1 %collective-permute-start.3 = (s16[40,1280]{1,0:T(8,128)(2,1)}, s16[40,1280]{1,0:T(8,128)(2,1)S(1)}, u32[]{:S(2)}, u32[]{:S(2)}) collective-permute-start(s16[40,1280]{1,0:T(8,128)(2,1)} %get-tuple-element.43), channel_id=1, source_target_pairs={{0,24},{1,0},{2,8},{3,16},{4,28},{5,4},{6,12},{7,20},{8,25},{9,1},... | collective-permute-start | bytes 307208 | tf_op jit(solution)/shard_map/ppermute | solution.py:427
  7.8 1.5 collective-permute-start.2
  9.3 1.5 collective-permute-start
  10.8 0.4 collective-permute-done.3
  11.2 2.3 %collective-permute-done.2 = s16[40,1280]{1,0:T(8,128)(2,1)S(1)} collective-permute-done((s16[40,1280]{1,0:T(8,128)(2,1)}, s16[40,1280]{1,0:T(8,128)(2,1)S(1)}, u32[]{:S(2)}, u32[]{:S(2)}) %collective-permute-start.2) | collective-permute-done | bytes 102432 | tf_op jit(solution)/shard_map/ppermute | solution.py:427
  13.5 2.1 %collective-permute-done.1 = s16[40,1280]{1,0:T(8,128)(2,1)S(1)} collective-permute-done((s16[40,1280]{1,0:T(8,128)(2,1)}, s16[40,1280]{1,0:T(8,128)(2,1)S(1)}, u32[]{:S(2)}, u32[]{:S(2)}) %collective-permute-start.1) | collective-permute-done | bytes 102432 | tf_op jit(solution)/shard_map/ppermute | solution.py:427
  15.6 1.6 collective-permute-start.4
  17.3 13.3 %product.6 = (f32[2,32,2048]{2,1,0:T(8,128)S(1)}, f32[32,128]{1,0:T(8,128)S(1)}, f32[1,4096]{1,0:T(1,128)S(1)}, s32[1,4096]{1,0:T(1,128)S(1)}) custom-call(s32[6]{0:T(128)S(1)} %stack.72.refs_0_, s16[4,40,1280]{2,1,0:T(8,128)(2,1)S(1)} %pad_add_fusion.refs_1_, bf16[4096,8192]{1,0:T(8,128)(2,1)} %refs_7_.3), custom_call_target="tpu_custom_call" | custom-call | flops 2147483648 | bytes 33554432 | tf_op jit(solution)/shard_map/product/pallas_call | solution.py:262
  30.7 13.3 %product.7 = (f32[2,32,2048]{2,1,0:T(8,128)S(1)}, f32[32,128]{1,0:T(8,128)S(1)}, f32[1,4096]{1,0:T(1,128)S(1)}, s32[1,4096]{1,0:T(1,128)S(1)}) custom-call(s32[6]{0:T(128)S(1)} %stack.72.refs_0_, s16[4,40,1280]{2,1,0:T(8,128)(2,1)S(1)} %collective-permute-done.4.refs_1_, f32[2,32,2048]{2,1,0:T(8,128)S(1)} %get-tuple-element.44.refs_2_, ...), custom_call_target="tpu_custom_call" | custom-call | flops 2147483648 | bytes 33554432 | tf_op jit(solution)/shard_map/product/pallas_call | solution.py:262
  44.0 0.1 collective-permute-start.5
  44.2 1.5 collective-permute-done.5
  45.7 0.1 abs_reduce_fusion.2
  45.8 0.1 round-nearest-even_convert_fusion.2
  46.0 5.7 %collective-permute-start.7 = (s16[32,1152]{1,0:T(8,128)(2,1)S(1)}, s16[32,1152]{1,0:T(8,128)(2,1)S(1)}, u32[]{:S(2)}, u32[]{:S(2)}) collective-permute-start(s16[32,1152]{1,0:T(8,128)(2,1)S(1)} %pad_add_fusion.3), channel_id=1, source_target_pairs={{0,2},{1,3},{2,0},{3,1},{4,6},{5,7},{6,4},{7,5},{8,10},{9,11},{10,... | collective-permute-start | bytes 221192 | tf_op jit(solution)/shard_map/ppermute | solution.py:427
  51.8 3.7 %collective-permute-done.6 = f32[32,128]{1,0:T(8,128)S(1)} collective-permute-done((f32[32,128]{1,0:T(8,128)S(1)}, f32[32,128]{1,0:T(8,128)S(1)}, u32[]{:S(2)}, u32[]{:S(2)}) %collective-permute-start.6) | collective-permute-done | bytes 16416 | tf_op jit(solution)/shard_map/ppermute | solution.py:427
  55.5 0.1 exponential_reduce_fusion.2
  55.6 0.1 multiply_add_fusion.2.refs_2_
  55.7 3.7 %next_block.4 = (f32[32,1024]{1,0:T(8,128)S(1)}, f32[32,32]{1,0:T(8,128)S(1)}, f32[32,1024]{1,0:T(8,128)S(1)}, f32[32,1024]{1,0:T(8,128)S(1)}, f32[32,64]{1,0:T(...) custom-call(f32[32,128]{1,0:T(8,128)S(1)} %add.113.refs_0_, f32[32,1024]{1,0:T(8,128)S(1)} %copy-done, ...), custom_call_target="tpu_custom_call" | custom-call | tf_op jit(solution)/shard_map/next_block/pallas_call | solution.py:404
  59.4 0.4 collective-permute-start.11
  59.8 0.9 collective-permute-start.10
  60.7 2.3 %collective-permute-start.9 = (s16[32,1280]{1,0:T(8,128)(2,1)S(1)}, s16[32,1280]{1,0:T(8,128)(2,1)S(1)}, u32[]{:S(2)}, u32[]{:S(2)}) collective-permute-start(s16[32,1280]{1,0:T(8,128)(2,1)S(1)} %get-tuple-element.51), channel_id=1, source_target_pairs={{0,8},{1,16},{2,24},{3,0},{4,12},{5,20},{6,28},{7,4},{8,9},{9,17},... | collective-permute-start | bytes 245768 | tf_op jit(solution)/shard_map/ppermute | solution.py:427
  63.0 0.7 collective-permute-start.8
  63.7 2.1 %collective-permute-done.10 = s16[32,1280]{1,0:T(8,128)(2,1)S(1)} collective-permute-done((s16[32,1280]{1,0:T(8,128)(2,1)S(1)}, s16[32,1280]{1,0:T(8,128)(2,1)S(1)}, u32[]{:S(2)}, u32[]{:S(2)}) %collective-permute-start.10) | collective-permute-done | bytes 81952 | tf_op jit(solution)/shard_map/ppermute | solution.py:427
  65.8 0.3 collective-permute-done.9
  66.1 0.6 collective-permute-start.12
  66.7 13.4 %product.8 = (f32[2,32,2048]{2,1,0:T(8,128)S(1)}, f32[32,128]{1,0:T(8,128)S(1)}) custom-call(s32[6]{0:T(128)S(1)} %stack.72.refs_0_, s16[4,32,1280]{2,1,0:T(8,128)(2,1)S(1)} %pad_add_fusion.1.refs_1_, f32[1,4096]{1,0:T(1,128)S(1)} %get-tuple-element.55.refs_2_, s32[1,4096]{1,0:T(1,128)S(1)} %get-tuple-element.56.refs_3_, ...), custom_call_target="tpu_custom_call" | custom-call | flops 2147483648 | bytes 33554432 | tf_op jit(solution)/shard_map/product/pallas_call | solution.py:262
  80.0 13.4 %product.9 = (f32[2,32,2048]{2,1,0:T(8,128)S(1)}, f32[32,128]{1,0:T(8,128)S(1)}) custom-call(s32[6]{0:T(128)S(1)} %stack.72.refs_0_, s16[4,32,1280]{2,1,0:T(8,128)(2,1)S(1)} %collective-permute-done.12.refs_1_, f32[1,4096]{1,0:T(1,128)S(1)} %get-tuple-element.52.refs_2_, s32[1,4096]{1,0:T(1,128)S(1)} %get-tuple-element.53.refs_3_, ...), custom_call_target="tpu_custom_call" | custom-call | flops 2147483648 | bytes 33554432 | tf_op jit(solution)/shard_map/product/pallas_call | solution.py:262
  93.5 2.3 %collective-permute-start.13 = (f32[32,2176]{1,0:T(8,128)S(1)}, f32[32,2176]{1,0:T(8,128)S(1)}, u32[]{:S(2)}, u32[]{:S(2)}) collective-permute-start(f32[32,2176]{1,0:T(8,128)S(1)} %pad_maximum_fusion.2), channel_id=1, source_target_pairs={{0,1},{1,0},{2,3},{3,2},{4,5},{5,4},{6,7},{7,6},{8,9},{9,8},{10,11... | collective-permute-start | bytes 835592 | tf_op jit(solution)/shard_map/ppermute | solution.py:427
  95.9 1.2 collective-permute-done.13
  97.1 0.1 abs_reduce_fusion.1
  97.2 0.1 round-nearest-even_convert_fusion.1
  97.4 4.6 %collective-permute-start.15 = (s16[32,1152]{1,0:T(8,128)(2,1)S(1)}, s16[32,1152]{1,0:T(8,128)(2,1)S(1)}, u32[]{:S(2)}, u32[]{:S(2)}) collective-permute-start(s16[32,1152]{1,0:T(8,128)(2,1)S(1)} %pad_add_fusion.4), channel_id=1, source_target_pairs={{0,2},{1,3},{2,0},{3,1},{4,6},{5,7},{6,4},{7,5},{8,10},{9,11},{10,... | collective-permute-start | bytes 221192 | tf_op jit(solution)/shard_map/ppermute | solution.py:427
  102.1 3.7 %collective-permute-done.14 = f32[32,128]{1,0:T(8,128)S(1)} collective-permute-done((f32[32,128]{1,0:T(8,128)S(1)}, f32[32,128]{1,0:T(8,128)S(1)}, u32[]{:S(2)}, u32[]{:S(2)}) %collective-permute-start.14) | collective-permute-done | bytes 16416 | tf_op jit(solution)/shard_map/ppermute | solution.py:427
  105.7 0.1 exponential_reduce_fusion.1
  105.9 0.1 multiply_add_fusion.1.refs_3_
  106.0 4.2 %next_block.5 = (f32[32,1024]{1,0:T(8,128)S(1)}, f32[32,32]{1,0:T(8,128)S(1)}, f32[32,32]{1,0:T(8,128)S(1)}, f32[32,1024]{1,0:T(8,128)S(1)}, f32[32,1024]{1,0:T(...) custom-call(f32[32,128]{1,0:T(8,128)S(1)} %add.120.refs_0_, ...), custom_call_target="tpu_custom_call" | custom-call | tf_op jit(solution)/shard_map/next_block/pallas_call | solution.py:404
  110.1 0.6 collective-permute-start.19
  110.7 1.1 collective-permute-start.18
  111.8 2.0 %collective-permute-start.17 = (s16[32,1280]{1,0:T(8,128)(2,1)S(1)}, s16[32,1280]{1,0:T(8,128)(2,1)S(1)}, u32[]{:S(2)}, u32[]{:S(2)}) collective-permute-start(s16[32,1280]{1,0:T(8,128)(2,1)S(1)} %get-tuple-element.65), channel_id=1, source_target_pairs={{0,8},{1,16},{2,24},{3,0},{4,12},{5,20},{6,28},{7,4},{8,9},{9,17},... | collective-permute-start | bytes 245768 | tf_op jit(solution)/shard_map/ppermute | solution.py:427
  113.8 0.8 collective-permute-start.16
  114.6 2.9 %collective-permute-done.18 = s16[32,1280]{1,0:T(8,128)(2,1)S(1)} collective-permute-done((s16[32,1280]{1,0:T(8,128)(2,1)S(1)}, s16[32,1280]{1,0:T(8,128)(2,1)S(1)}, u32[]{:S(2)}, u32[]{:S(2)}) %collective-permute-start.18) | collective-permute-done | bytes 81952 | tf_op jit(solution)/shard_map/ppermute | solution.py:427
  117.5 0.2 collective-permute-done.17
  117.8 1.6 collective-permute-start.20
  119.4 13.4 %product.10 = (f32[2,32,2048]{2,1,0:T(8,128)S(1)}, f32[32,256]{1,0:T(8,128)S(1)}) custom-call(s32[6]{0:T(128)S(1)} %stack.72.refs_0_, s16[4,32,1280]{2,1,0:T(8,128)(2,1)S(1)} %pad_add_fusion.2.refs_1_, f32[1,4096]{1,0:T(1,128)S(1)} %get-tuple-element.55.refs_2_, s32[1,4096]{1,0:T(1,128)S(1)} %get-tuple-element.56.refs_3_, ...), custom_call_target="tpu_custom_call" | custom-call | flops 2147483648 | bytes 33554432 | tf_op jit(solution)/shard_map/product/pallas_call | solution.py:262
  132.8 13.3 %product.11 = (f32[2,32,2048]{2,1,0:T(8,128)S(1)}, f32[32,256]{1,0:T(8,128)S(1)}) custom-call(s32[6]{0:T(128)S(1)} %stack.72.refs_0_, s16[4,32,1280]{2,1,0:T(8,128)(2,1)S(1)} %collective-permute-done.20.refs_1_, f32[1,4096]{1,0:T(1,128)S(1)} %get-tuple-element.52.refs_2_, s32[1,4096]{1,0:T(1,128)S(1)} %get-tuple-element.53.refs_3_, ...), custom_call_target="tpu_custom_call" | custom-call | flops 2147483648 | bytes 33554432 | tf_op jit(solution)/shard_map/product/pallas_call | solution.py:262
  146.2 1.0 collective-permute-start.21
  147.2 1.2 collective-permute-done.21
  148.5 0.1 abs_reduce_fusion
  148.6 0.1 round-nearest-even_convert_fusion
  148.8 5.1 %collective-permute-start.23 = (s16[32,1152]{1,0:T(8,128)(2,1)S(1)}, s16[32,1152]{1,0:T(8,128)(2,1)S(1)}, u32[]{:S(2)}, u32[]{:S(2)}) collective-permute-start(s16[32,1152]{1,0:T(8,128)(2,1)S(1)} %pad_add_fusion.5), channel_id=1, source_target_pairs={{0,2},{1,3},{2,0},{3,1},{4,6},{5,7},{6,4},{7,5},{8,10},{9,11},{10,... | collective-permute-start | bytes 221192 | tf_op jit(solution)/shard_map/ppermute | solution.py:427
  154.0 3.8 %collective-permute-done.22 = f32[32,256]{1,0:T(8,128)S(1)} collective-permute-done((f32[32,256]{1,0:T(8,128)S(1)}, f32[32,256]{1,0:T(8,128)S(1)}, u32[]{:S(2)}, u32[]{:S(2)}) %collective-permute-start.22) | collective-permute-done | bytes 32800 | tf_op jit(solution)/shard_map/ppermute | solution.py:427
  157.8 0.1 exponential_reduce_fusion
  158.0 3.9 %next_block.6 = (f32[32,1024]{1,0:T(8,128)S(1)}, f32[32,32]{1,0:T(8,128)S(1)}, f32[64,32]{1,0:T(8,128)S(1)}, f32[32,1024]{1,0:T(8,128)S(1)}, f32[32,128]{1,0:T(8,128)S(1)}) custom-call(f32[32,256]{1,0:T(8,128)S(1)} %add.124.refs_0_, f32[32,1024]{1,0:T(8,128)S(1)} %get-tuple-element.71.refs_1_, f32[32,1024]{1,0:T(8,128)S(1)} %get-tuple-element.62.refs_2_, ...), custom_call_target="tpu_custom_call" | custom-call | tf_op jit(solution)/shard_map/next_block/pallas_call | solution.py:404
  162.0 1.2 collective-permute-done.24
  163.2 1.1 collective-permute-start.25
  164.3 2.6 %collective-permute-done.25 = f32[32,128]{1,0:T(8,128)S(1)} collective-permute-done((f32[32,128]{1,0:T(8,128)S(1)}, f32[32,128]{1,0:T(8,128)S(1)}, u32[]{:S(2)}, u32[]{:S(2)}) %collective-permute-start.25) | collective-permute-done | bytes 16416 | tf_op jit(solution)/shard_map/ppermute | solution.py:427
  167.0 0.5 collective-permute-start.26
  167.5 3.2 %collective-permute-done.26 = f32[32,128]{1,0:T(8,128)S(1)} collective-permute-done((f32[32,128]{1,0:T(8,128)S(1)}, f32[32,128]{1,0:T(8,128)S(1)}, u32[]{:S(2)}, u32[]{:S(2)}) %collective-permute-start.26) | collective-permute-done | bytes 16416 | tf_op jit(solution)/shard_map/ppermute | solution.py:427
  170.7 3.7 %collective-permute-done.27 = f32[32,128]{1,0:T(8,128)S(1)} collective-permute-done((f32[32,128]{1,0:T(8,128)S(1)}, f32[32,128]{1,0:T(8,128)S(1)}, u32[]{:S(2)}, u32[]{:S(2)}) %collective-permute-start.27) | collective-permute-done | bytes 16416 | tf_op jit(solution)/shard_map/ppermute | solution.py:427
  174.4 0.8 collective-permute-start.28
  175.2 3.9 %collective-permute-done.28 = f32[32,128]{1,0:T(8,128)S(1)} collective-permute-done((f32[32,128]{1,0:T(8,128)S(1)}, f32[32,128]{1,0:T(8,128)S(1)}, u32[]{:S(2)}, u32[]{:S(2)}) %collective-permute-start.28) | collective-permute-done | bytes 16416 | tf_op jit(solution)/shard_map/ppermute | solution.py:427
  179.1 4.2 %next_block.7 = (f32[128,1024]{1,0:T(8,128)}, f32[128,96]{1,0:T(8,128)S(1)}, f32[32,32]{1,0:T(8,128)}) custom-call(f32[32,128]{1,0:T(8,128)S(1)} %add.131.refs_0_, f32[32,1024]{1,0:T(8,128)S(1)} %get-tuple-element.76.refs_1_, f32[32,1024]{1,0:T(8,128)S(1)} %get-tuple-element.62.refs_2_, f32[32,1024]{1,0:T(8,128)S(1)} %get-tuple-element.72.refs_3_, ...), custom_call_target="tpu_custom_call" | custom-call | tf_op jit(solution)/shard_map/next_block/pallas_call | solution.py:404
  183.3 0.7 copy.8
  (57 shorter events, 1.2 us)
Async XLA Ops:
  2.7 8.5 %collective-permute-start.3 = (s16[40,1280]{1,0:T(8,128)(2,1)}, s16[40,1280]{1,0:T(8,128)(2,1)S(1)}, u32[]{:S(2)}, u32[]{:S(2)}) collective-permute-start(s16[40,1280]{1,0:T(8,128)(2,1)} %get-tuple-element.43), channel_id=1, source_target_pairs={{0,24},{1,0},{2,8},{3,16},{4,28},{5,4},{6,12},{7,20},{8,25},{9,1},... | collective-permute-start | bytes 307208 | tf_op jit(solution)/shard_map/ppermute | solution.py:427
  7.8 5.7 %collective-permute-start.2 = (s16[40,1280]{1,0:T(8,128)(2,1)}, s16[40,1280]{1,0:T(8,128)(2,1)S(1)}, u32[]{:S(2)}, u32[]{:S(2)}) collective-permute-start(s16[40,1280]{1,0:T(8,128)(2,1)} %get-tuple-element.43), channel_id=1, source_target_pairs={{0,16},{1,24},{2,0},{3,8},{4,20},{5,28},{6,4},{7,12},{8,17},{9,25}... | collective-permute-start | bytes 307208 | tf_op jit(solution)/shard_map/ppermute | solution.py:427
  9.3 6.3 %collective-permute-start.1 = (s16[40,1280]{1,0:T(8,128)(2,1)}, s16[40,1280]{1,0:T(8,128)(2,1)S(1)}, u32[]{:S(2)}, u32[]{:S(2)}) collective-permute-start(s16[40,1280]{1,0:T(8,128)(2,1)} %get-tuple-element.43), channel_id=1, source_target_pairs={{0,8},{1,16},{2,24},{3,0},{4,12},{5,20},{6,28},{7,4},{8,9},{9,17},... | collective-permute-start | bytes 307208 | tf_op jit(solution)/shard_map/ppermute | solution.py:427
  9.3 6.3 %collective-permute-start = (s16[40,1280]{1,0:T(8,128)(2,1)}, s16[40,1280]{1,0:T(8,128)(2,1)S(1)}, u32[]{:S(2)}, u32[]{:S(2)}) collective-permute-start(s16[40,1280]{1,0:T(8,128)(2,1)} %get-tuple-element.43), channel_id=1, source_target_pairs={{0,0},{1,8},{2,16},{3,24},{4,4},{5,12},{6,20},{7,28},{8,1},{9,9},{... | collective-permute-start | bytes 307208 | tf_op jit(solution)/shard_map/ppermute | solution.py:427
  15.6 15.0 %collective-permute-start.4 = (s16[4,40,1280]{2,1,0:T(8,128)(2,1)S(1)}, s16[4,40,1280]{2,1,0:T(8,128)(2,1)S(1)}, u32[]{:S(2)}, u32[]{:S(2)}) collective-permute-start(s16[4,40,1280]{2,1,0:T(8,128)(2,1)S(1)} %pad_add_fusion.refs_1_), channel_id=1, source_target_pairs={{0,4},{1,5},{2,6},{3,7},{4,0},{5,1},{6,2},{7,3},{8,12},{9,13},{10,... | collective-permute-start | bytes 1228808 | tf_op jit(solution)/shard_map/ppermute | solution.py:427
  17.3 38.4 %copy-start = (f32[32,1024]{1,0:T(8,128)S(1)}, f32[32,1024]{1,0:T(8,128)}, u32[]{:S(2)}) copy-start(f32[32,1024]{1,0:T(8,128)} %get-tuple-element.48.refs_1_) | copy-start | bytes 393220
  17.3 38.4 %copy-start.1 = (f32[1,1024]{1,0:T(1,128)S(1)}, f32[1,1024]{1,0:T(1,128)}, u32[]{:S(2)}) copy-start(f32[1,1024]{1,0:T(1,128)} %get-tuple-element.49.refs_3_.refs_4_.refs_5_) | copy-start | bytes 12292
  17.3 38.4 %copy-start.2 = (s32[1,1024]{1,0:T(1,128)S(1)}, s32[1,1024]{1,0:T(1,128)}, u32[]{:S(2)}) copy-start(s32[1,1024]{1,0:T(1,128)} %get-tuple-element.50.refs_4_.refs_5_.refs_6_) | copy-start | bytes 12292
  44.0 1.6 collective-permute-start.5
  46.0 9.4 %collective-permute-start.7 = (s16[32,1152]{1,0:T(8,128)(2,1)S(1)}, s16[32,1152]{1,0:T(8,128)(2,1)S(1)}, u32[]{:S(2)}, u32[]{:S(2)}) collective-permute-start(s16[32,1152]{1,0:T(8,128)(2,1)S(1)} %pad_add_fusion.3), channel_id=1, source_target_pairs={{0,2},{1,3},{2,0},{3,1},{4,6},{5,7},{6,4},{7,5},{8,10},{9,11},{10,... | collective-permute-start | bytes 221192 | tf_op jit(solution)/shard_map/ppermute | solution.py:427
  51.7 3.7 %collective-permute-start.6 = (f32[32,128]{1,0:T(8,128)S(1)}, f32[32,128]{1,0:T(8,128)S(1)}, u32[]{:S(2)}, u32[]{:S(2)}) collective-permute-start(f32[32,128]{1,0:T(8,128)S(1)} %slice_add_fusion.5), channel_id=1, source_target_pairs={{0,2},{1,3},{2,0},{3,1},{4,6},{5,7},{6,4},{7,5},{8,10},{9,11},{10,... | collective-permute-start | bytes 49160 | tf_op jit(solution)/shard_map/ppermute | solution.py:427
  59.4 4.3 %collective-permute-start.11 = (s16[32,1280]{1,0:T(8,128)(2,1)S(1)}, s16[32,1280]{1,0:T(8,128)(2,1)S(1)}, u32[]{:S(2)}, u32[]{:S(2)}) collective-permute-start(s16[32,1280]{1,0:T(8,128)(2,1)S(1)} %get-tuple-element.51), channel_id=1, source_target_pairs={{0,24},{1,0},{2,8},{3,16},{4,28},{5,4},{6,12},{7,20},{8,25},{9,1},... | collective-permute-start | bytes 245768 | tf_op jit(solution)/shard_map/ppermute | solution.py:427
  59.8 6.0 %collective-permute-start.10 = (s16[32,1280]{1,0:T(8,128)(2,1)S(1)}, s16[32,1280]{1,0:T(8,128)(2,1)S(1)}, u32[]{:S(2)}, u32[]{:S(2)}) collective-permute-start(s16[32,1280]{1,0:T(8,128)(2,1)S(1)} %get-tuple-element.51), channel_id=1, source_target_pairs={{0,16},{1,24},{2,0},{3,8},{4,20},{5,28},{6,4},{7,12},{8,17},{9,25}... | collective-permute-start | bytes 245768 | tf_op jit(solution)/shard_map/ppermute | solution.py:427
  60.7 5.3 %collective-permute-start.9 = (s16[32,1280]{1,0:T(8,128)(2,1)S(1)}, s16[32,1280]{1,0:T(8,128)(2,1)S(1)}, u32[]{:S(2)}, u32[]{:S(2)}) collective-permute-start(s16[32,1280]{1,0:T(8,128)(2,1)S(1)} %get-tuple-element.51), channel_id=1, source_target_pairs={{0,8},{1,16},{2,24},{3,0},{4,12},{5,20},{6,28},{7,4},{8,9},{9,17},... | collective-permute-start | bytes 245768 | tf_op jit(solution)/shard_map/ppermute | solution.py:427
  63.0 3.0 %collective-permute-start.8 = (s16[32,1280]{1,0:T(8,128)(2,1)S(1)}, s16[32,1280]{1,0:T(8,128)(2,1)S(1)}, u32[]{:S(2)}, u32[]{:S(2)}) collective-permute-start(s16[32,1280]{1,0:T(8,128)(2,1)S(1)} %get-tuple-element.51), channel_id=1, source_target_pairs={{0,0},{1,8},{2,16},{3,24},{4,4},{5,12},{6,20},{7,28},{8,1},{9,9},{... | collective-permute-start | bytes 245768 | tf_op jit(solution)/shard_map/ppermute | solution.py:427
  66.1 14.0 %collective-permute-start.12 = (s16[4,32,1280]{2,1,0:T(8,128)(2,1)S(1)}, s16[4,32,1280]{2,1,0:T(8,128)(2,1)S(1)}, u32[]{:S(2)}, u32[]{:S(2)}) collective-permute-start(s16[4,32,1280]{2,1,0:T(8,128)(2,1)S(1)} %pad_add_fusion.1.refs_1_), channel_id=1, source_target_pairs={{0,4},{1,5},{2,6},{3,7},{4,0},{5,1},{6,2},{7,3},{8,12},{9,13},{10,... | collective-permute-start | bytes 983048 | tf_op jit(solution)/shard_map/ppermute | solution.py:427
  93.5 3.5 %collective-permute-start.13 = (f32[32,2176]{1,0:T(8,128)S(1)}, f32[32,2176]{1,0:T(8,128)S(1)}, u32[]{:S(2)}, u32[]{:S(2)}) collective-permute-start(f32[32,2176]{1,0:T(8,128)S(1)} %pad_maximum_fusion.2), channel_id=1, source_target_pairs={{0,1},{1,0},{2,3},{3,2},{4,5},{5,4},{6,7},{7,6},{8,9},{9,8},{10,11... | collective-permute-start | bytes 835592 | tf_op jit(solution)/shard_map/ppermute | solution.py:427
  97.4 8.3 %collective-permute-start.15 = (s16[32,1152]{1,0:T(8,128)(2,1)S(1)}, s16[32,1152]{1,0:T(8,128)(2,1)S(1)}, u32[]{:S(2)}, u32[]{:S(2)}) collective-permute-start(s16[32,1152]{1,0:T(8,128)(2,1)S(1)} %pad_add_fusion.4), channel_id=1, source_target_pairs={{0,2},{1,3},{2,0},{3,1},{4,6},{5,7},{6,4},{7,5},{8,10},{9,11},{10,... | collective-permute-start | bytes 221192 | tf_op jit(solution)/shard_map/ppermute | solution.py:427
  102.0 3.7 %collective-permute-start.14 = (f32[32,128]{1,0:T(8,128)S(1)}, f32[32,128]{1,0:T(8,128)S(1)}, u32[]{:S(2)}, u32[]{:S(2)}) collective-permute-start(f32[32,128]{1,0:T(8,128)S(1)} %slice_add_fusion.4), channel_id=1, source_target_pairs={{0,2},{1,3},{2,0},{3,1},{4,6},{5,7},{6,4},{7,5},{8,10},{9,11},{10,... | collective-permute-start | bytes 49160 | tf_op jit(solution)/shard_map/ppermute | solution.py:427
  110.1 4.5 %collective-permute-start.19 = (s16[32,1280]{1,0:T(8,128)(2,1)S(1)}, s16[32,1280]{1,0:T(8,128)(2,1)S(1)}, u32[]{:S(2)}, u32[]{:S(2)}) collective-permute-start(s16[32,1280]{1,0:T(8,128)(2,1)S(1)} %get-tuple-element.65), channel_id=1, source_target_pairs={{0,24},{1,0},{2,8},{3,16},{4,28},{5,4},{6,12},{7,20},{8,25},{9,1},... | collective-permute-start | bytes 245768 | tf_op jit(solution)/shard_map/ppermute | solution.py:427
  110.7 6.9 %collective-permute-start.18 = (s16[32,1280]{1,0:T(8,128)(2,1)S(1)}, s16[32,1280]{1,0:T(8,128)(2,1)S(1)}, u32[]{:S(2)}, u32[]{:S(2)}) collective-permute-start(s16[32,1280]{1,0:T(8,128)(2,1)S(1)} %get-tuple-element.65), channel_id=1, source_target_pairs={{0,16},{1,24},{2,0},{3,8},{4,20},{5,28},{6,4},{7,12},{8,17},{9,25}... | collective-permute-start | bytes 245768 | tf_op jit(solution)/shard_map/ppermute | solution.py:427
  111.8 6.0 %collective-permute-start.17 = (s16[32,1280]{1,0:T(8,128)(2,1)S(1)}, s16[32,1280]{1,0:T(8,128)(2,1)S(1)}, u32[]{:S(2)}, u32[]{:S(2)}) collective-permute-start(s16[32,1280]{1,0:T(8,128)(2,1)S(1)} %get-tuple-element.65), channel_id=1, source_target_pairs={{0,8},{1,16},{2,24},{3,0},{4,12},{5,20},{6,28},{7,4},{8,9},{9,17},... | collective-permute-start | bytes 245768 | tf_op jit(solution)/shard_map/ppermute | solution.py:427
  113.8 4.0 %collective-permute-start.16 = (s16[32,1280]{1,0:T(8,128)(2,1)S(1)}, s16[32,1280]{1,0:T(8,128)(2,1)S(1)}, u32[]{:S(2)}, u32[]{:S(2)}) collective-permute-start(s16[32,1280]{1,0:T(8,128)(2,1)S(1)} %get-tuple-element.65), channel_id=1, source_target_pairs={{0,0},{1,8},{2,16},{3,24},{4,4},{5,12},{6,20},{7,28},{8,1},{9,9},{... | collective-permute-start | bytes 245768 | tf_op jit(solution)/shard_map/ppermute | solution.py:427
  117.8 15.0 %collective-permute-start.20 = (s16[4,32,1280]{2,1,0:T(8,128)(2,1)S(1)}, s16[4,32,1280]{2,1,0:T(8,128)(2,1)S(1)}, u32[]{:S(2)}, u32[]{:S(2)}) collective-permute-start(s16[4,32,1280]{2,1,0:T(8,128)(2,1)S(1)} %pad_add_fusion.2.refs_1_), channel_id=1, source_target_pairs={{0,4},{1,5},{2,6},{3,7},{4,0},{5,1},{6,2},{7,3},{8,12},{9,13},{10,... | collective-permute-start | bytes 983048 | tf_op jit(solution)/shard_map/ppermute | solution.py:427
  146.2 2.2 %collective-permute-start.21 = (f32[32,2304]{1,0:T(8,128)S(1)}, f32[32,2304]{1,0:T(8,128)S(1)}, u32[]{:S(2)}, u32[]{:S(2)}) collective-permute-start(f32[32,2304]{1,0:T(8,128)S(1)} %pad_maximum_fusion), channel_id=1, source_target_pairs={{0,1},{1,0},{2,3},{3,2},{4,5},{5,4},{6,7},{7,6},{8,9},{9,8},{10,11... | collective-permute-start | bytes 884744 | tf_op jit(solution)/shard_map/ppermute | solution.py:427
  148.8 9.0 %collective-permute-start.23 = (s16[32,1152]{1,0:T(8,128)(2,1)S(1)}, s16[32,1152]{1,0:T(8,128)(2,1)S(1)}, u32[]{:S(2)}, u32[]{:S(2)}) collective-permute-start(s16[32,1152]{1,0:T(8,128)(2,1)S(1)} %pad_add_fusion.5), channel_id=1, source_target_pairs={{0,2},{1,3},{2,0},{3,1},{4,6},{5,7},{6,4},{7,5},{8,10},{9,11},{10,... | collective-permute-start | bytes 221192 | tf_op jit(solution)/shard_map/ppermute | solution.py:427
  153.9 3.9 %collective-permute-start.22 = (f32[32,256]{1,0:T(8,128)S(1)}, f32[32,256]{1,0:T(8,128)S(1)}, u32[]{:S(2)}, u32[]{:S(2)}) collective-permute-start(f32[32,256]{1,0:T(8,128)S(1)} %slice_add_fusion.3), channel_id=1, source_target_pairs={{0,2},{1,3},{2,0},{3,1},{4,6},{5,7},{6,4},{7,5},{8,10},{9,11},{10,... | collective-permute-start | bytes 98312 | tf_op jit(solution)/shard_map/ppermute | solution.py:427
  162.0 1.2 collective-permute-start.24
  163.2 3.7 %collective-permute-start.25 = (f32[32,128]{1,0:T(8,128)S(1)}, f32[32,128]{1,0:T(8,128)S(1)}, u32[]{:S(2)}, u32[]{:S(2)}) collective-permute-start(f32[32,128]{1,0:T(8,128)S(1)} %add.127), channel_id=1, source_target_pairs={{0,2},{1,3},{2,0},{3,1},{4,6},{5,7},{6,4},{7,5},{8,10},{9,11},{10,... | collective-permute-start | bytes 49160 | tf_op jit(solution)/shard_map/ppermute | solution.py:427
  167.0 3.7 %collective-permute-start.26 = (f32[32,128]{1,0:T(8,128)S(1)}, f32[32,128]{1,0:T(8,128)S(1)}, u32[]{:S(2)}, u32[]{:S(2)}) collective-permute-start(f32[32,128]{1,0:T(8,128)S(1)} %add.128), channel_id=1, source_target_pairs={{0,4},{1,5},{2,6},{3,7},{4,0},{5,1},{6,2},{7,3},{8,12},{9,13},{10,... | collective-permute-start | bytes 49160 | tf_op jit(solution)/shard_map/ppermute | solution.py:427
  170.7 3.7 %collective-permute-start.27 = (f32[32,128]{1,0:T(8,128)S(1)}, f32[32,128]{1,0:T(8,128)S(1)}, u32[]{:S(2)}, u32[]{:S(2)}) collective-permute-start(f32[32,128]{1,0:T(8,128)S(1)} %add.129), channel_id=1, source_target_pairs={{0,8},{1,9},{2,10},{3,11},{4,12},{5,13},{6,14},{7,15},{8,0},{9,1},... | collective-permute-start | bytes 49160 | tf_op jit(solution)/shard_map/ppermute | solution.py:427
  174.4 4.6 %collective-permute-start.28 = (f32[32,128]{1,0:T(8,128)S(1)}, f32[32,128]{1,0:T(8,128)S(1)}, u32[]{:S(2)}, u32[]{:S(2)}) collective-permute-start(f32[32,128]{1,0:T(8,128)S(1)} %add.130), channel_id=1, source_target_pairs={{0,16},{1,17},{2,18},{3,19},{4,20},{5,21},{6,22},{7,23},{8,24},{9,... | collective-permute-start | bytes 49160 | tf_op jit(solution)/shard_map/ppermute | solution.py:427
